TPU v7x, 32 devices: a whole 2x2x4 slice. The times are simulated.
32 devices in a mesh: group: 4 (over y, core), img: 8 (over z, x).
Axes of the slice: x: 2, y: 2, z: 4, core: 2. Of those that a mesh axis runs over, the one named last changes fastest.
Arguments:
- pixels: bfloat16 [32, 196, 8192], P(('group', 'img')), may hold values from -6 to 6
- band_mask: int32 [32, 32], P(('group', 'img')), may hold values from 0 to 1, as said below
- wavelength: int32 [4, 32], replicated, may hold values from 400 to 2499
- owner_order: int32 [7520], replicated, may hold values from 0 to 7519, as said below
- rest_weight: float32 [60160, 128], P(('group', 'img')), may hold values from -4 to 4, as said below
- rest_moment1: float32 [60160, 128], P(('group', 'img')), may hold values from -512 to 512
- rest_moment2: float32 [60160, 128], P(('group', 'img')), may hold values from 2090 to 8362
- fc_weight: float32 [128, 196608], P('group', 'img'), may hold values from -0.005859375 to 0.005859375
- fc_moment1: float32 [128, 196608], P('group', 'img'), may hold values from -2560 to 2560
- fc_moment2: float32 [128, 196608], P('group', 'img'), may hold values from 50176 to 200704
- cotangent: bfloat16 [6272, 768], P(('group', 'img')), may hold values from -6 to 6
Outputs:
- block_out: bfloat16 [6272, 768], P(('group', 'img'))
- pixel_grad: bfloat16 [32, 196, 8192], P(('group', 'img'))
- rest_new: float32 [60160, 128], P(('group', 'img'))
- rest_first: float32 [60160, 128], P(('group', 'img'))
- rest_second: float32 [60160, 128], P(('group', 'img'))
- fc_new: float32 [128, 196608], P('group', 'img')
- fc_first: float32 [128, 196608], P('group', 'img')
- fc_second: float32 [128, 196608], P('group', 'img')
Inputs may be any that keep to these rules, and one draw needn't show every extreme that they name: `band_mask`: every image has 2 to 32 present bands, and some image has all 32. `owner_order`: A permutation of the packed blocks. `rest_weight`: in the order given by owner_order; padding entries are zero and gains lie near 1.
All inputs are finite; a program needn't handle non-finite values.
Results may differ from a plain program's by a relative error of at most 0.019.
Values may be sent and summed in bfloat16 or wider, within the bound.
A program may use at most 320 MiB of HBM per device.

v0:
```python
import functools
import math

import jax
import jax.numpy as jnp
from jax import lax
from jax.experimental import pallas as pl
from jax.experimental.pallas import tpu as pltpu
from jax.sharding import PartitionSpec as P

MESH = pl.DeviceIdType.MESH

D = 768
HEADS = 12
HD = 64
HID = 3072
E = 128
HH = 4
HFF = 2048
PATCH = 256
NB = 32
STEP = 5


beta_one = 0.5
beta_two = 0.75
decay_rate = 0.05
epsilon_add = 1e-08
rest_rate = 0.02


def layout():
    return [
        ("w_qkv", (D, 3 * D)),
        ("w_out", (D, D)),
        ("w_up", (D, HID)),
        ("w_down", (HID, D)),
        ("h_query", (E, E)),
        ("h_key", (E, E)),
        ("h_value", (E, E)),
        ("h_out", (E, E)),
        ("h_ffin", (E, HFF)),
        ("h_ffout", (HFF, E)),
        ("ln1_gain", (D,)),
        ("ln1_shift", (D,)),
        ("ln2_gain", (D,)),
        ("ln2_shift", (D,)),
        ("patch_bias", (D,)),
        ("hn1_gain", (E,)),
        ("hn1_shift", (E,)),
        ("hn2_gain", (E,)),
        ("hn2_shift", (E,)),
    ]


def matrices():
    listed, at = [], 0
    for name, extent in layout():
        if len(extent) == 2:
            listed.append((name, extent[0], extent[1], at))
        at += math.prod(extent) // 128
    return listed


def vector_places():
    listed, at = [], 0
    rows = [0, 0]
    for name, extent in layout():
        if len(extent) == 1:
            kind = 0 if extent[0] == D else 1
            for j in range(extent[0] // 128):
                listed.append((at + j, kind, rows[kind], j * 128))
            rows[kind] += 1
        at += math.prod(extent) // 128
    return listed


def spread_kernel(order_ref, low_ref, *refs):
    outs, linear = refs[:-1], refs[-1]
    step = pl.program_id(0)
    rows = low_ref.shape[0]

    def two(j, carry):
        pair = low_ref[pl.ds(pl.multiple_of(j * 16, 16), 16), :].astype(jnp.float32)
        for half in range(2):
            block = order_ref[step * (rows // 8) + j * 2 + half]
            linear[pl.ds(pl.multiple_of(block * 8, 8), 8), :] = pair[half * 8 : half * 8 + 8]
        return carry

    lax.fori_loop(0, rows // 16, two, 0, unroll=8)

    @pl.when(step == pl.num_programs(0) - 1)
    def _():
        for (name, height, width, first), out in zip(matrices(), outs):
            lanes = width // 128

            def some(j, carry, out=out, lanes=lanes, first=first):
                top = pl.multiple_of(j * 128, 128)
                for lane in range(lanes):
                    part = linear[pl.ds(first + top * lanes + lane, 128, stride=lanes), :]
                    out[pl.ds(top, 128), lane * 128 : lane * 128 + 128] = part.astype(out.dtype)
                return carry

            lax.fori_loop(0, height // 128, some, 0)
        for out in outs[-2:]:
            out[...] = jnp.zeros_like(out)
        for row, kind, top, lane in vector_places():
            outs[kind - 2][top : top + 1, lane : lane + 128] = linear[row : row + 1, :]


def spread_packed(gathered, slots, blocks):
    shards, rows = gathered.shape[0], gathered.shape[1]
    shapes = [
        jax.ShapeDtypeStruct((height, width), jnp.bfloat16 if name.startswith("w_") else jnp.float32)
        for name, height, width, first in matrices()
    ]
    shapes += [jax.ShapeDtypeStruct((8, D), jnp.float32), jax.ShapeDtypeStruct((8, E), jnp.float32)]
    return pl.pallas_call(
        spread_kernel,
        out_shape=shapes,
        grid_spec=pltpu.PrefetchScalarGridSpec(
            num_scalar_prefetch=1,
            grid=(shards,),
            in_specs=[pl.BlockSpec((None, rows, 128), lambda s, order: (s, 0, 0))],
            out_specs=[pl.BlockSpec(shape.shape, lambda s, order: (0, 0), pipeline_mode=pl.Buffered(1)) for shape in shapes],
            scratch_shapes=[pltpu.VMEM(((blocks + 1) * 8, 128), jnp.float32)],
        ),
        compiler_params=pltpu.CompilerParams(vmem_limit_bytes=60 << 20),
        name="spread_packed",
    )(slots, gathered)


def collect_kernel(order_ref, *refs):
    ins, low_ref, linear = refs[:-2], refs[-2], refs[-1]
    step = pl.program_id(0)
    rows = low_ref.shape[0]

    @pl.when(step == 0)
    def _():
        for (name, height, width, first), given in zip(matrices(), ins):
            lanes = width // 128

            def some(j, carry, given=given, lanes=lanes, first=first):
                top = pl.multiple_of(j * 128, 128)
                for lane in range(lanes):
                    part = given[pl.ds(top, 128), lane * 128 : lane * 128 + 128]
                    linear[pl.ds(first + top * lanes + lane, 128, stride=lanes), :] = part.astype(jnp.float32)
                return carry

            lax.fori_loop(0, height // 128, some, 0)
        first = vector_places()[0][0]
        linear[first:, :] = jnp.zeros((linear.shape[0] - first, 128), jnp.float32)
        for row, kind, top, lane in vector_places():
            linear[row : row + 1, :] = ins[kind - 2][top : top + 1, lane : lane + 128]

    def two(j, carry):
        parts = []
        for half in range(2):
            block = order_ref[step * (rows // 8) + j * 2 + half]
            parts.append(linear[pl.ds(pl.multiple_of(block * 8, 8), 8), :])
        low_ref[pl.ds(pl.multiple_of(j * 16, 16), 16), :] = jnp.concatenate(parts, axis=0).astype(low_ref.dtype)
        return carry

    lax.fori_loop(0, rows // 16, two, 0, unroll=8)


def collect_packed(grads, slots, blocks, shards, rows):
    return pl.pallas_call(
        collect_kernel,
        out_shape=jax.ShapeDtypeStruct((shards, rows, 128), jnp.bfloat16),
        grid_spec=pltpu.PrefetchScalarGridSpec(
            num_scalar_prefetch=1,
            grid=(shards,),
            in_specs=[pl.BlockSpec(grad.shape, lambda s, order: (0, 0), pipeline_mode=pl.Buffered(1)) for grad in grads],
            out_specs=pl.BlockSpec((None, rows, 128), lambda s, order: (s, 0, 0)),
            scratch_shapes=[pltpu.VMEM(((blocks + 1) * 8, 128), jnp.float32)],
        ),
        compiler_params=pltpu.CompilerParams(vmem_limit_bytes=60 << 20),
        name="collect_packed",
    )(slots, *grads)


def embed_waves(wavelength):
    half_width = E // 2
    frequency = jnp.exp(-math.log(10000.0) * jnp.arange(half_width, dtype=jnp.float32) / half_width)
    angles = wavelength.astype(jnp.float32)[..., None] * frequency
    return jnp.concatenate([jnp.sin(angles), jnp.cos(angles)], axis=-1)


def exact(a, b, left, right):
    return lax.dot_general(
        a, b, (((left,), (right,)), ((), ())), precision=lax.Precision.HIGHEST, preferred_element_type=jnp.float32
    )


def unit_scale(values):
    center = values - jnp.mean(values, axis=-1, keepdims=True)
    scale = lax.rsqrt(jnp.mean(center * center, axis=-1, keepdims=True) + 1e-06)
    return center * scale, scale


def unit_back(grad, unit, scale, gain):
    inner = grad * gain
    return scale * (
        inner - jnp.mean(inner, axis=-1, keepdims=True) - unit * jnp.mean(inner * unit, axis=-1, keepdims=True)
    )


def wave_kernel(embed_ref, wq_ref, wk_ref, wv_ref, wo_ref, win_ref, wout_ref, vec_ref, shaped_ref, own_ref, kept_ref, slope_ref):
    rows = embed_ref.shape[0]
    groups = rows // NB
    embedded = embed_ref[...]
    queries = exact(embedded, wq_ref[...], 1, 0)
    keys = exact(embedded, wk_ref[...], 1, 0)
    values = exact(embedded, wv_ref[...], 1, 0)
    size = E // HH
    across = lax.broadcasted_iota(jnp.int32, (rows, rows), 0) // NB == lax.broadcasted_iota(jnp.int32, (rows, rows), 1) // NB
    mixed = []
    for head in range(HH):
        lanes = slice(head * size, head * size + size)
        scores = exact(queries[:, lanes], keys[:, lanes], 1, 1) * size**-0.5
        scores = jnp.where(across, scores, -1e30)
        weight = jnp.exp(scores - jnp.max(scores, axis=-1, keepdims=True))
        weight = weight / jnp.sum(weight, axis=-1, keepdims=True)
        kept_ref[head] = weight
        mixed.append(exact(weight, values[:, lanes], 1, 0))
    mixed = jnp.concatenate(mixed, axis=1)
    unit_one, scale_one = unit_scale(embedded + exact(mixed, wo_ref[...], 1, 0))
    first = unit_one * vec_ref[0:1, :] + vec_ref[1:2, :]
    inner = exact(first, win_ref[...], 1, 0)
    half = 0.5 * (1.0 + lax.erf(inner * 0.5**0.5))
    slope_ref[0] = inner * half
    slope_ref[1] = half + inner * jnp.exp(-0.5 * inner * inner) * (2.0 * math.pi) ** -0.5
    unit_two, scale_two = unit_scale(first + exact(inner * half, wout_ref[...], 1, 0))
    shaped = (unit_two * vec_ref[2:3, :] + vec_ref[3:4, :] + embedded).astype(jnp.bfloat16)
    for j, part in enumerate((queries, keys, values, mixed, unit_one, unit_two)):
        kept_ref[HH + j] = part
    kept_ref[HH + 6] = jnp.broadcast_to(scale_one, (rows, E))
    kept_ref[HH + 7] = jnp.broadcast_to(scale_two, (rows, E))
    shaped_ref[...] = shaped
    wide = shaped.astype(jnp.float32)
    width = E // groups
    group = lax.axis_index("group")
    own = jnp.zeros((rows, width), jnp.float32)
    for j in range(groups):
        own = jnp.where(group == j, wide[:, j * width : (j + 1) * width], own)
    own_ref[...] = own.astype(jnp.bfloat16)


def wave_layer(embedded, mats, vectors):
    rows = embedded.shape[0]
    groups = rows // NB
    f32, bf16 = jnp.float32, jnp.bfloat16
    return pl.pallas_call(
        wave_kernel,
        out_shape=[
            jax.ShapeDtypeStruct((rows, E), bf16),
            jax.ShapeDtypeStruct((rows, E // groups), bf16),
            jax.ShapeDtypeStruct((HH + 8, rows, E), f32),
            jax.ShapeDtypeStruct((2, rows, HFF), f32),
        ],
        compiler_params=pltpu.CompilerParams(vmem_limit_bytes=60 << 20),
        name="wave_layer",
    )(embedded, *mats, vectors)


def wave_back_kernel(part_ref, embed_ref, kept_ref, slope_ref, wq_ref, wk_ref, wv_ref, wo_ref, win_ref, wout_ref, vec_ref,
                     gq_ref, gk_ref, gv_ref, go_ref, gin_ref, gout_ref, gvec_ref):
    rows = embed_ref.shape[0]
    groups = rows // NB
    width = E // groups
    size = E // HH
    group = lax.axis_index("group")
    spread = jnp.concatenate([part_ref[...]] * groups, axis=1)
    lane = lax.broadcasted_iota(jnp.int32, (rows, E), 1) // width
    grad = jnp.where(lane == group, spread, 0.0)
    embedded = embed_ref[...]
    queries, keys, values, mixed, unit_one, unit_two, scale_one, scale_two = (kept_ref[HH + j] for j in range(8))
    gvec_ref[...] = jnp.zeros_like(gvec_ref)
    gvec_ref[2:3, :] = jnp.sum(grad * unit_two, axis=0, keepdims=True)
    gvec_ref[3:4, :] = jnp.sum(grad, axis=0, keepdims=True)
    grad = unit_back(grad, unit_two, scale_two, vec_ref[2:3, :])
    gout_ref[...] = exact(slope_ref[0], grad, 0, 0)
    inner = exact(grad, wout_ref[...], 1, 1) * slope_ref[1]
    first = unit_one * vec_ref[0:1, :] + vec_ref[1:2, :]
    gin_ref[...] = exact(first, inner, 0, 0)
    grad = grad + exact(inner, win_ref[...], 1, 1)
    gvec_ref[0:1, :] = jnp.sum(grad * unit_one, axis=0, keepdims=True)
    gvec_ref[1:2, :] = jnp.sum(grad, axis=0, keepdims=True)
    grad = unit_back(grad, unit_one, scale_one, vec_ref[0:1, :])
    go_ref[...] = exact(mixed, grad, 0, 0)
    grad = exact(grad, wo_ref[...], 1, 1)
    parts = [[], [], []]
    for head in range(HH):
        lanes = slice(head * size, head * size + size)
        weight = kept_ref[head]
        grad_weight = exact(grad[:, lanes], values[:, lanes], 1, 1)
        parts[2].append(exact(weight, grad[:, lanes], 0, 0))
        score = weight * (grad_weight - jnp.sum(weight * grad_weight, axis=-1, keepdims=True)) * size**-0.5
        parts[0].append(exact(score, keys[:, lanes], 1, 0))
        parts[1].append(exact(score, queries[:, lanes], 0, 0))
    for out, part in zip((gq_ref, gk_ref, gv_ref), parts):
        out[...] = exact(embedded, jnp.concatenate(part, axis=1), 0, 0)


def wave_back(part, embedded, kept, slope, mats, vectors):
    f32 = jnp.float32
    return pl.pallas_call(
        wave_back_kernel,
        out_shape=[jax.ShapeDtypeStruct(mat.shape, f32) for mat in mats] + [jax.ShapeDtypeStruct((8, E), f32)],
        compiler_params=pltpu.CompilerParams(vmem_limit_bytes=60 << 20),
        name="wave_back",
    )(part, embedded, kept, slope, *mats, vectors)


def tall(count):
    return -(-count // 16) * 16


def dot_nn(a, b):
    return lax.dot_general(a, b, (((1,), (0,)), ((), ())), preferred_element_type=jnp.float32)


def dot_nt(a, b):
    return lax.dot_general(a, b, (((1,), (1,)), ((), ())), preferred_element_type=jnp.float32)


def dot_tn(a, b):
    return lax.dot_general(a, b, (((0,), (0,)), ((), ())), preferred_element_type=jnp.float32)


def block_kernel(stream_ref, up_ref, vec_ref, wqkv_hbm, wout_hbm, wup_hbm, wdown_hbm,
                 out_ref, low_ref, gvec_ref, gqkv_hbm, gout_hbm, gup_hbm, gdown_hbm,
                 wqkv, wout, wup, wdown, gqkv, gout, gup, gdown,
                 xs, ups, up_low, norm_one, qkv, att, probs, mid, norm_two, acc, hid_low, datt, dqkv, in_sem, out_sem):
    f32, bf16 = jnp.float32, jnp.bfloat16
    seq = stream_ref.shape[0]
    rows = xs.shape[0]
    loads = [
        pltpu.make_async_copy(src, dst, in_sem.at[j])
        for j, (src, dst) in enumerate(((wqkv_hbm, wqkv), (wout_hbm, wout), (wup_hbm, wup), (wdown_hbm, wdown)))
    ]
    for load in loads:
        load.start()
    stores = [
        pltpu.make_async_copy(src, dst, out_sem.at[j])
        for j, (src, dst) in enumerate(((gqkv, gqkv_hbm), (gout, gout_hbm), (gup, gup_hbm), (gdown, gdown_hbm)))
    ]
    gain_one, shift_one = vec_ref[0:1, :], vec_ref[1:2, :]
    gain_two, shift_two = vec_ref[2:3, :], vec_ref[3:4, :]
    xs[...] = jnp.zeros_like(xs)
    xs[0:seq, :] = stream_ref[...] + vec_ref[4:5, :]
    ups[...] = jnp.zeros_like(ups)
    ups[0:seq, :] = up_ref[...].astype(f32)
    up_low[...] = ups[...].astype(bf16)

    def normed(values):
        center = values - jnp.mean(values, axis=-1, keepdims=True)
        scale = lax.rsqrt(jnp.mean(center * center, axis=-1, keepdims=True) + 1e-06)
        return center * scale, scale

    def normed_back(grad, unit, scale, gain):
        inner = grad * gain
        return scale * (
            inner
            - jnp.mean(inner, axis=-1, keepdims=True)
            - unit * jnp.mean(inner * unit, axis=-1, keepdims=True)
        )

    unit, scale = normed(xs[...])
    norm_one[...] = (unit * gain_one + shift_one).astype(bf16)
    loads[0].wait()

    def tile(j, size=D):
        return pl.ds(pl.multiple_of(j * size, size), size)

    def each(count, body):
        lax.fori_loop(0, count, lambda j, carry: (body(j), carry)[1], 0)

    def qkv_part(j):
        qkv[:, tile(j)] = dot_nn(norm_one[...], wqkv[:, tile(j)]).astype(bf16)

    each(3, qkv_part)
    inside = lax.broadcasted_iota(jnp.int32, (rows, rows), 1) < seq

    def heads(p):
        pair = [qkv[:, pl.ds(pl.multiple_of(j * D + p * 128, 128), 128)] for j in range(3)]
        outs = []
        for h in range(2):
            query, key, value = (part[:, h * HD : h * HD + HD] for part in pair)
            scores = jnp.where(inside, dot_nt(query, key) * (HD**-0.5), -1e30)
            weight = jnp.exp(scores - jnp.max(scores, axis=-1, keepdims=True))
            weight = weight / jnp.sum(weight, axis=-1, keepdims=True)
            probs[p * 2 + h] = weight
            outs.append(dot_nn(weight.astype(bf16), value))
        att[:, pl.ds(pl.multiple_of(p * 128, 128), 128)] = jnp.concatenate(outs, axis=1).astype(bf16)

    each(HEADS // 2, heads)
    loads[1].wait()
    mid[...] = xs[...] + dot_nn(att[...], wout[...])
    unit, scale = normed(mid[...])
    norm_two[...] = (unit * gain_two + shift_two).astype(bf16)
    loads[2].wait()
    loads[3].wait()
    acc[...] = jnp.zeros_like(acc)

    def hidden_part(j):
        hidden = dot_nn(norm_two[...], wup[:, tile(j)])
        half = 0.5 * (1.0 + lax.erf(hidden * (0.5**0.5)))
        active = (hidden * half).astype(bf16)
        slope = half + hidden * jnp.exp(-0.5 * hidden * hidden) * (2.0 * math.pi) ** -0.5
        mid[...] += dot_nn(active, wdown[tile(j), :])
        gdown[tile(j), :] = dot_tn(active, up_low[...]).astype(bf16)
        grad_hidden = (dot_nt(up_low[...], wdown[tile(j), :]) * slope).astype(bf16)
        gup[:, tile(j)] = dot_tn(norm_two[...], grad_hidden).astype(bf16)
        acc[...] += dot_nt(grad_hidden, wup[:, tile(j)])

    kept_unit, kept_scale = unit, scale
    hid_low[...] = kept_unit
    each(HID // D, hidden_part)
    stores[2].start()
    stores[3].start()
    out_ref[...] = mid[0:seq, :].astype(bf16)
    grad = acc[...]
    unit = hid_low[...]
    gvec_ref[...] = jnp.zeros_like(gvec_ref)
    gvec_ref[2:3, :] = jnp.sum(grad * unit, axis=0, keepdims=True)
    gvec_ref[3:4, :] = jnp.sum(grad, axis=0, keepdims=True)
    ups[...] += normed_back(grad, unit, kept_scale, gain_two)
    up_low[...] = ups[...].astype(bf16)
    gout[...] = dot_tn(att[...], up_low[...]).astype(bf16)
    stores[1].start()
    datt[...] = dot_nt(up_low[...], wout[...]).astype(bf16)

    def heads_back(p):
        pair = [qkv[:, pl.ds(pl.multiple_of(j * D + p * 128, 128), 128)] for j in range(3)]
        grad_pair = datt[:, pl.ds(pl.multiple_of(p * 128, 128), 128)]
        grads = [[], [], []]
        for h in range(2):
            query, key, value = (part[:, h * HD : h * HD + HD] for part in pair)
            grad_out = grad_pair[:, h * HD : h * HD + HD]
            weight = probs[p * 2 + h]
            grad_weight = dot_nt(grad_out, value)
            grads[2].append(dot_tn(weight.astype(bf16), grad_out))
            grad_score = weight * (grad_weight - jnp.sum(weight * grad_weight, axis=-1, keepdims=True))
            grad_score = grad_score.astype(bf16)
            grads[0].append(dot_nn(grad_score, key) * (HD**-0.5))
            grads[1].append(dot_tn(grad_score, query) * (HD**-0.5))
        for j in range(3):
            dqkv[:, pl.ds(pl.multiple_of(j * D + p * 128, 128), 128)] = jnp.concatenate(grads[j], axis=1).astype(bf16)

    each(HEADS // 2, heads_back)
    acc[...] = jnp.zeros_like(acc)

    def qkv_back(j):
        gqkv[:, tile(j)] = dot_tn(norm_one[...], dqkv[:, tile(j)]).astype(bf16)
        acc[...] += dot_nt(dqkv[:, tile(j)], wqkv[:, tile(j)])

    each(3, qkv_back)
    stores[0].start()
    unit, scale = normed(xs[...])
    grad = acc[...]
    gvec_ref[0:1, :] = jnp.sum(grad * unit, axis=0, keepdims=True)
    gvec_ref[1:2, :] = jnp.sum(grad, axis=0, keepdims=True)
    total = ups[...] + normed_back(grad, unit, scale, gain_one)
    gvec_ref[4:5, :] = jnp.sum(total, axis=0, keepdims=True)
    low_ref[...] = total.astype(bf16)
    for store in stores:
        store.wait()


def block_pass(stream, upstream, vectors, wqkv, wout, wup, wdown):
    f32, bf16 = jnp.float32, jnp.bfloat16
    seq = stream.shape[0]
    rows = tall(seq)
    whole = pl.BlockSpec(memory_space=pltpu.VMEM)
    far = pl.BlockSpec(memory_space=pl.ANY)
    mats = [wqkv, wout, wup, wdown]
    kept = [pltpu.VMEM(mat.shape, bf16) for mat in mats]
    dma = pltpu.SemaphoreType.DMA
    return pl.pallas_call(
        block_kernel,
        out_shape=[
            jax.ShapeDtypeStruct((seq, D), bf16),
            jax.ShapeDtypeStruct((rows, D), bf16),
            jax.ShapeDtypeStruct((8, D), f32),
        ]
        + [jax.ShapeDtypeStruct(mat.shape, bf16) for mat in mats],
        in_specs=[whole] * 3 + [far] * 4,
        out_specs=[whole] * 3 + [far] * 4,
        scratch_shapes=kept
        + kept
        + [
            pltpu.VMEM((rows, D), f32),
            pltpu.VMEM((rows, D), f32),
            pltpu.VMEM((rows, D), bf16),
            pltpu.VMEM((rows, D), bf16),
            pltpu.VMEM((rows, 3 * D), bf16),
            pltpu.VMEM((rows, D), bf16),
            pltpu.VMEM((HEADS, rows, rows), f32),
            pltpu.VMEM((rows, D), f32),
            pltpu.VMEM((rows, D), bf16),
            pltpu.VMEM((rows, D), f32),
            pltpu.VMEM((rows, D), f32),
            pltpu.VMEM((rows, D), bf16),
            pltpu.VMEM((rows, 3 * D), bf16),
            dma((4,)),
            dma((4,)),
        ],
        compiler_params=pltpu.CompilerParams(vmem_limit_bytes=60 << 20),
        cost_estimate=pl.CostEstimate(flops=8_400_000_000, bytes_accessed=30_000_000, transcendentals=2_000_000),
        name="block_pass",
    )(stream, upstream, vectors, *mats)


def adamw_step(weight, moment_one, moment_two, grad, rate):
    first = beta_one * moment_one + (1.0 - beta_one) * grad
    second = beta_two * moment_two + (1.0 - beta_two) * grad * grad
    fix_one = 1.0 - beta_one**STEP
    fix_two = 1.0 - beta_two**STEP
    update = first / fix_one / (jnp.sqrt(second / fix_two) + epsilon_add) + decay_rate * weight
    return (weight - rate * update, first, second)


NC = 15


def dims_step(count):
    return 16 if count % 16 == 0 else count


def make_kernel(shaped_ref, master_ref, kernel_ref, turned):
    dims = kernel_ref.shape[0]
    shaped = shaped_ref[pl.ds(pl.multiple_of(lax.axis_index("group") * NB, NB), NB), :]
    for dim in range(dims):
        part = dot_nn(shaped, master_ref[:, dim * PATCH : (dim + 1) * PATCH])
        turned[pl.ds(dim, NB, stride=dims), :] = part[:, :128]
        turned[pl.ds(NB * dims + dim, NB, stride=dims), :] = part[:, 128:]
    for band in range(NB):
        for half in range(2):
            row = half * NB * dims + band * dims
            lane = band * PATCH + half * 128
            kernel_ref[:, lane : lane + 128] = turned[row : row + dims, :].astype(kernel_ref.dtype)


def make_kernels(shaped, master):
    dims = master.shape[1] // PATCH
    step = dims_step(dims)
    return pl.pallas_call(
        make_kernel,
        out_shape=jax.ShapeDtypeStruct((dims, NB * PATCH), jnp.bfloat16),
        grid=(dims // step,),
        in_specs=[
            pl.BlockSpec(shaped.shape, lambda j: (0, 0)),
            pl.BlockSpec((E, step * PATCH), lambda j: (0, j)),
        ],
        out_specs=pl.BlockSpec((step, NB * PATCH), lambda j: (j, 0)),
        scratch_shapes=[pltpu.VMEM((2 * NB * step, 128), jnp.float32)],
        compiler_params=pltpu.CompilerParams(vmem_limit_bytes=60 << 20),
        name="make_kernels",
    )(shaped, master)


def embed_kernel(pixel_ref, mask_ref, kernel_ref, stream_ref):
    masked = pixel_ref[...] * mask_ref[...].astype(jnp.bfloat16)
    part = dot_nt(masked, kernel_ref[...])

    @pl.when(pl.program_id(0) == 0)
    def _():
        stream_ref[...] = part

    @pl.when(pl.program_id(0) > 0)
    def _():
        stream_ref[...] += part


def embed_patches(pixels, mask, kernels):
    seq, width = pixels.shape[1], pixels.shape[2]
    cut = 1024
    return pl.pallas_call(
        embed_kernel,
        out_shape=jax.ShapeDtypeStruct((seq, D), jnp.float32),
        grid=(width // cut,),
        in_specs=[
            pl.BlockSpec((None, seq, cut), lambda j: (0, 0, j)),
            pl.BlockSpec((1, cut), lambda j: (0, j)),
            pl.BlockSpec((D, cut), lambda j: (0, j)),
        ],
        out_specs=pl.BlockSpec((seq, D), lambda j: (0, 0)),
        compiler_params=pltpu.CompilerParams(vmem_limit_bytes=60 << 20),
        name="embed_patches",
    )(pixels, mask, kernels)


def unembed_kernel(pixel_ref, mask_ref, kernel_ref, low_ref, back_ref, grad_ref, masked):
    seq = pixel_ref.shape[0]
    mask = mask_ref[...]
    masked[...] = jnp.zeros_like(masked)
    masked[0:seq, :] = pixel_ref[...].astype(jnp.float32) * mask
    back_ref[...] = (dot_nn(low_ref[...], kernel_ref[...])[0:seq] * mask).astype(back_ref.dtype)
    grad_ref[...] = dot_tn(low_ref[...], masked[...].astype(jnp.bfloat16)).astype(grad_ref.dtype)


def unembed_patches(pixels, mask, kernels, low):
    seq, width = pixels.shape[1], pixels.shape[2]
    cut = 1024
    return pl.pallas_call(
        unembed_kernel,
        out_shape=[
            jax.ShapeDtypeStruct(pixels.shape, jnp.bfloat16),
            jax.ShapeDtypeStruct((D, width), jnp.bfloat16),
        ],
        grid=(width // cut,),
        in_specs=[
            pl.BlockSpec((None, seq, cut), lambda j: (0, 0, j)),
            pl.BlockSpec((1, cut), lambda j: (0, j)),
            pl.BlockSpec((D, cut), lambda j: (0, j)),
            pl.BlockSpec(low.shape, lambda j: (0, 0)),
        ],
        out_specs=[
            pl.BlockSpec((None, seq, cut), lambda j: (0, 0, j)),
            pl.BlockSpec((D, cut), lambda j: (0, j)),
        ],
        scratch_shapes=[pltpu.VMEM((low.shape[0], cut), jnp.float32)],
        compiler_params=pltpu.CompilerParams(vmem_limit_bytes=60 << 20),
        name="unembed_patches",
    )(pixels, mask, kernels, low)


def master_kernel(rate, grad_ref, shaped_ref, weight_ref, one_ref, two_ref, new_ref, first_ref, second_ref, back_ref, turned):
    groups, dims = grad_ref.shape[0], grad_ref.shape[1]
    bands = groups * NB
    for group in range(groups):
        for band in range(NB):
            for half in range(2):
                row = half * bands * dims + (group * NB + band) * dims
                lane = band * PATCH + half * 128
                turned[row : row + dims, :] = grad_ref[group, :, lane : lane + 128].astype(jnp.float32)
    total = jnp.zeros(back_ref.shape, jnp.float32)
    for dim in range(dims):
        part = jnp.concatenate(
            [turned[pl.ds(half * bands * dims + dim, bands, stride=dims), :] for half in range(2)], axis=1
        ).astype(jnp.bfloat16)
        lanes = slice(dim * PATCH, (dim + 1) * PATCH)
        weight = weight_ref[:, lanes]
        total += dot_nt(part, weight.astype(jnp.bfloat16))
        grad = dot_tn(shaped_ref[...], part)
        new_ref[:, lanes], first_ref[:, lanes], second_ref[:, lanes] = adamw_step(
            weight, one_ref[:, lanes], two_ref[:, lanes], grad, rate
        )

    @pl.when(pl.program_id(0) == 0)
    def _():
        back_ref[...] = total

    @pl.when(pl.program_id(0) > 0)
    def _():
        back_ref[...] += total


def master_update(grads, shaped, weight, one, two, rate):
    groups, dims = grads.shape[0], grads.shape[1]
    step = dims_step(dims)
    columns = pl.BlockSpec((weight.shape[0], step * PATCH), lambda j: (0, j))
    like = jax.ShapeDtypeStruct(weight.shape, jnp.float32)
    return pl.pallas_call(
        functools.partial(master_kernel, rate),
        out_shape=[like, like, like, jax.ShapeDtypeStruct(shaped.shape, jnp.float32)],
        grid=(dims // step,),
        in_specs=[
            pl.BlockSpec((groups, step, NB * PATCH), lambda j: (0, j, 0)),
            pl.BlockSpec(shaped.shape, lambda j: (0, 0)),
            columns,
            columns,
            columns,
        ],
        out_specs=[columns, columns, columns, pl.BlockSpec(shaped.shape, lambda j: (0, 0))],
        scratch_shapes=[pltpu.VMEM((2 * groups * NB * step, 128), jnp.float32)],
        compiler_params=pltpu.CompilerParams(vmem_limit_bytes=60 << 20),
        name="master_update",
    )(grads, shaped, weight, one, two)


def spot():
    group = lax.axis_index("group")
    image = lax.axis_index("img")
    return group // 2, group % 2, image // 2, image % 2


def place(y, c, z, x):
    return (y * 2 + c, z * 2 + x)


def partners():
    y, c, z, x = spot()
    x2, y2 = x + (1 - c) * (1 - 2 * x), y + c * (1 - 2 * y)
    x3, y3 = x + c * (1 - 2 * x), y + (1 - c) * (1 - 2 * y)
    around = [place(y, c, (z + d) % 4, x) for d in (1, 2, 3)]
    return (x2, y2), (x3, y3), around, place(y2, c, z, x2), place(y3, c, z, x3), place(y, 1 - c, z, x)


def greet(peers):
    barrier = pltpu.get_barrier_semaphore()
    for peer in peers:
        pl.semaphore_signal(barrier, inc=1, device_id=peer, device_id_type=MESH)
    pl.semaphore_wait(barrier, len(peers))


def gather_kernel(own_ref, all_ref, local_sem, line_send, line_recv, group_send, group_recv, twin_send, twin_recv):
    y, c, z, x = spot()
    (x2, y2), (x3, y3), around, second, third, twin = partners()
    rows = own_ref.shape[0] // NC

    def cut(k):
        return pl.ds(k * rows, rows)

    def remote(src, dst, send_sem, recv_sem, target):
        return pltpu.make_async_remote_copy(
            src_ref=src, dst_ref=dst, send_sem=send_sem, recv_sem=recv_sem, device_id=target, device_id_type=MESH
        )

    def along(d, k):
        return remote(own_ref.at[cut(k)], all_ref.at[y, c, z, x, cut(k)], line_send.at[d - 1, k], line_recv.at[d - 1, k], around[d - 1])

    def along_in(d, k):
        return remote(own_ref.at[cut(k)], all_ref.at[y, c, (z + 4 - d) % 4, x, cut(k)], line_send.at[d - 1, k], line_recv.at[d - 1, k], around[d - 1])

    def square(core, j):
        yy, xx = ((y, x), (y2, x2), (y3, x3), (1 - y, 1 - x))[j]
        return all_ref.at[yy, core, :, xx]

    def hop(j, to, k, slot, landing):
        part = square(c, j).at[:, cut(k)]
        return remote(part, part, group_send.at[slot, k], group_recv.at[landing, k], to)

    def hop_in(landing, k):
        part = square(c, landing).at[:, cut(k)]
        return remote(part, part, group_send.at[0, k], group_recv.at[landing, k], twin)

    def share(j, k):
        part = square(c, j).at[:, cut(k)]
        yy, xx = ((y, x), (y2, x2), (y3, x3), (1 - y, 1 - x))[j]
        landing = (0, 2, 1, 3)[j]
        return remote(part, part, twin_send.at[j, k], twin_recv.at[landing, k], twin)

    def share_in(landing, k):
        yy, xx = ((y, x), (y2, x2), (y3, x3), (1 - y, 1 - x))[landing]
        part = all_ref.at[yy, 1 - c, :, xx, cut(k)]
        return remote(part, part, twin_send.at[0, k], twin_recv.at[landing, k], twin)

    keep = pltpu.make_async_copy(own_ref, all_ref.at[y, c, z, x], local_sem)
    keep.start()
    greet(around + [second, third, twin])
    for k in range(NC):
        for d in (1, 2, 3):
            along(d, k).start()
    keep.wait()
    for step in range(NC + 2):
        k = step
        if k < NC:
            for d in (1, 2, 3):
                along_in(d, k).wait_recv()
            hop(0, third, k, 0, 2).start()
            hop(0, second, k, 1, 1).start()
            share(0, k).start()
        k = step - 1
        if 0 <= k < NC:
            hop_in(1, k).wait_recv()
            hop(1, third, k, 2, 3).start()
            share(1, k).start()
        k = step - 2
        if 0 <= k < NC:
            hop_in(2, k).wait_recv()
            share(2, k).start()
            hop_in(3, k).wait_recv()
            share(3, k).start()
    for k in range(NC):
        for d in (1, 2, 3):
            along(d, k).wait_send()
        hop(0, third, k, 0, 2).wait_send()
        hop(0, second, k, 1, 1).wait_send()
        hop(1, third, k, 2, 3).wait_send()
        for j in range(4):
            share(j, k).wait_send()
            share_in(j, k).wait_recv()


def gather_packed(own):
    rows = own.shape[0]
    dma = pltpu.SemaphoreType.DMA
    return pl.pallas_call(
        gather_kernel,
        out_shape=jax.ShapeDtypeStruct((2, 2, 4, 2, rows, 128), own.dtype),
        in_specs=[pl.BlockSpec(memory_space=pltpu.VMEM)],
        out_specs=pl.BlockSpec(memory_space=pl.ANY),
        scratch_shapes=[dma, dma((3, NC)), dma((3, NC)), dma((3, NC)), dma((4, NC)), dma((4, NC)), dma((4, NC))],
        compiler_params=pltpu.CompilerParams(collective_id=0, has_side_effects=True, vmem_limit_bytes=60 << 20),
        name="gather_packed",
    )(own)


def reduce_kernel(part_ref, sum_ref, own, twin_in, third_in, second_in, line_in, load_sem, twin_send, twin_recv, third_send, third_recv, second_send, second_recv, line_send, line_recv):
    f32, bf16 = jnp.float32, jnp.bfloat16
    y, c, z, x = spot()
    (x2, y2), (x3, y3), around, second, third, twin = partners()
    rows = sum_ref.shape[0] // NC

    def cut(k):
        return pl.ds(k * rows, rows)

    def remote(src, dst, send_sem, recv_sem, target):
        return pltpu.make_async_remote_copy(
            src_ref=src, dst_ref=dst, send_sem=send_sem, recv_sem=recv_sem, device_id=target, device_id_type=MESH
        )

    spots = ((1 - y, 1 - x), (y3, x3), (y2, x2), (y, x))
    turned = ((1 - y, 1 - x), (y2, x2), (y3, x3), (y, x))

    def load(j, k):
        yy, xx = spots[j]
        return pltpu.make_async_copy(part_ref.at[yy, c, :, xx, cut(k)], own.at[j, :, cut(k)], load_sem.at[j, k])

    def swap(j, k):
        yy, xx = turned[j]
        return remote(part_ref.at[yy, 1 - c, :, xx, cut(k)], twin_in.at[j, :, cut(k)], twin_send.at[j, k], twin_recv.at[j, k], twin)

    def to_third(j, k):
        return remote(own.at[j, :, cut(k)], third_in.at[j, :, cut(k)], third_send.at[j, k], third_recv.at[j, k], third)

    def to_second(k):
        return remote(own.at[2, :, cut(k)], second_in.at[:, cut(k)], second_send.at[k], second_recv.at[k], second)

    def to_line(d, k):
        return remote(own.at[3, (z + d) % 4, cut(k)], line_in.at[d - 1, cut(k)], line_send.at[d - 1, k], line_recv.at[d - 1, k], around[d - 1])

    for k in range(NC):
        for j in range(4):
            load(j, k).start()
    greet(around + [second, third, twin])
    for k in range(NC):
        for j in range(4):
            swap(j, k).start()

    def pair(j, k):
        load(j, k).wait()
        swap(j, k).wait_recv()
        return own[j, :, cut(k)].astype(f32) + twin_in[j, :, cut(k)].astype(f32)

    for step in range(NC + 3):
        k = step
        if k < NC:
            for j in (0, 1):
                own[j, :, cut(k)] = pair(j, k).astype(bf16)
                to_third(j, k).start()
        k = step - 1
        if 0 <= k < NC:
            held = pair(2, k)
            to_third(0, k).wait_recv()
            own[2, :, cut(k)] = (held + third_in[0, :, cut(k)].astype(f32)).astype(bf16)
            to_second(k).start()
        k = step - 2
        if 0 <= k < NC:
            held = pair(3, k)
            to_third(1, k).wait_recv()
            to_second(k).wait_recv()
            held += third_in[1, :, cut(k)].astype(f32) + second_in[:, cut(k)].astype(f32)
            own[3, :, cut(k)] = held.astype(bf16)
            for d in (1, 2, 3):
                to_line(d, k).start()
        k = step - 3
        if 0 <= k < NC:
            total = own[3, z, cut(k)].astype(f32)
            for d in (1, 2, 3):
                to_line(d, k).wait_recv()
                total += line_in[d - 1, cut(k)].astype(f32)
            sum_ref[cut(k)] = total
    for k in range(NC):
        for j in range(4):
            swap(j, k).wait_send()
        for j in (0, 1):
            to_third(j, k).wait_send()
        to_second(k).wait_send()
        for d in (1, 2, 3):
            to_line(d, k).wait_send()


def reduce_packed(part):
    rows = part.shape[-2]
    bf16 = jnp.bfloat16
    dma = pltpu.SemaphoreType.DMA
    return pl.pallas_call(
        reduce_kernel,
        out_shape=jax.ShapeDtypeStruct((rows, 128), jnp.float32),
        in_specs=[pl.BlockSpec(memory_space=pl.ANY)],
        out_specs=pl.BlockSpec(memory_space=pltpu.VMEM),
        scratch_shapes=[
            pltpu.VMEM((4, 4, rows, 128), bf16),
            pltpu.VMEM((4, 4, rows, 128), bf16),
            pltpu.VMEM((2, 4, rows, 128), bf16),
            pltpu.VMEM((4, rows, 128), bf16),
            pltpu.VMEM((3, rows, 128), bf16),
            dma((4, NC)), dma((4, NC)), dma((4, NC)), dma((2, NC)), dma((2, NC)), dma((NC,)), dma((NC,)), dma((3, NC)), dma((3, NC)),
        ],
        compiler_params=pltpu.CompilerParams(collective_id=1, has_side_effects=True, vmem_limit_bytes=56 << 20),
        name="reduce_packed",
    )(part)


CHUNK = 16


def over_x(k):
    return k % 2 == 0


def quad_peers():
    y, c, z, x = spot()
    low = z % 2
    side = place(y, c, z, 1 - x)
    along = place(y, c, z + 1 - 2 * low, x)
    twin = place(y, 1 - c, z, x)
    partner = place(y, 1 - c, (z + 2) % 4, x)
    moved = (c + z // 2) % 2 == 1
    return y, c, z, x, low, side, along, twin, partner, moved


def swap_images(value):
    pairs = []
    for y in range(2):
        for c in range(2):
            for z in range(4):
                for x in range(2):
                    other = (1 - c, (z + 2) % 4) if c != z // 2 else (c, z)
                    pairs.append((((y * 2 + c) * 4 + z) * 2 + x, ((y * 2 + other[0]) * 4 + other[1]) * 2 + x))
    return lax.ppermute(value, ("group", "img"), pairs)


def remote(src, dst, send_sem, recv_sem, target):
    return pltpu.make_async_remote_copy(
        src_ref=src, dst_ref=dst, send_sem=send_sem, recv_sem=recv_sem, device_id=target, device_id_type=MESH
    )


def share_kernel(made_ref, all_ref, keep_sem, swap_send, swap_recv, side_send, side_recv, along_send, along_recv, far_send, far_recv, twin_send, twin_recv):
    y, c, z, x, low, side, along, twin, partner, moved = quad_peers()
    count = made_ref.shape[0] // CHUNK

    def cut(k):
        return pl.ds(k * CHUNK, CHUNK)

    def block(core, j, k):
        return all_ref.at[2 * core + (low + j // 2) % 2, (x + j % 2) % 2, cut(k)]

    def keep(k):
        return pltpu.make_async_copy(made_ref.at[cut(k)], block(c, 0, k), keep_sem.at[k])

    def swap(k):
        return remote(made_ref.at[cut(k)], block(1 - c, 0, k), swap_send.at[k], swap_recv.at[k], partner)

    def swap_in(k):
        return remote(made_ref.at[cut(k)], block(c, 0, k), swap_send.at[k], swap_recv.at[k], partner)

    def to_side(k):
        return remote(block(c, 0, k), block(c, 0, k), side_send.at[k], side_recv.at[k], side)

    def from_side(k):
        return remote(block(c, 1, k), block(c, 1, k), side_send.at[k], side_recv.at[k], side)

    def to_along(k):
        return remote(block(c, 0, k), block(c, 0, k), along_send.at[k], along_recv.at[k], along)

    def from_along(k):
        return remote(block(c, 2, k), block(c, 2, k), along_send.at[k], along_recv.at[k], along)

    def pass_on(k):
        j, to = (2, side) if over_x(k) else (1, along)
        return remote(block(c, j, k), block(c, j, k), far_send.at[k], far_recv.at[k], to)

    def from_far(k):
        return remote(block(c, 3, k), block(c, 3, k), far_send.at[k], far_recv.at[k], twin)

    def give(j, k):
        return remote(block(c, j, k), block(c, j, k), twin_send.at[j, k], twin_recv.at[j, k], twin)

    def given(j, k):
        return remote(block(1 - c, j, k), block(1 - c, j, k), twin_send.at[j, k], twin_recv.at[j, k], twin)

    @pl.when(jnp.logical_not(moved))
    def _():
        for k in range(count):
            keep(k).start()

    greet([side, along, twin, partner])

    @pl.when(moved)
    def _():
        for k in range(count):
            swap(k).start()

    for step in range(count + 2):
        k = step
        if k < count:

            @pl.when(moved)
            def _(k=k):
                swap_in(k).wait_recv()

            @pl.when(jnp.logical_not(moved))
            def _(k=k):
                keep(k).wait()

            to_side(k).start()
            to_along(k).start()
            give(0, k).start()
        k = step - 1
        if 0 <= k < count:
            if over_x(k):
                from_along(k).wait_recv()
                pass_on(k).start()
                from_side(k).wait_recv()
            else:
                from_side(k).wait_recv()
                pass_on(k).start()
                from_along(k).wait_recv()
            give(1, k).start()
            give(2, k).start()
        k = step - 2
        if 0 <= k < count:
            from_far(k).wait_recv()
            give(3, k).start()

    @pl.when(moved)
    def _():
        for k in range(count):
            swap(k).wait_send()

    for k in range(count):
        to_side(k).wait_send()
        to_along(k).wait_send()
        pass_on(k).wait_send()
        for j in range(4):
            give(j, k).wait_send()
            given(j, k).wait_recv()


def share_kernels(made):
    dims, width = made.shape
    count = dims // CHUNK
    dma = pltpu.SemaphoreType.DMA
    shared = pl.pallas_call(
        share_kernel,
        out_shape=jax.ShapeDtypeStruct((4, 2, dims, width), made.dtype),
        in_specs=[pl.BlockSpec(memory_space=pltpu.VMEM)],
        out_specs=pl.BlockSpec(memory_space=pl.ANY),
        scratch_shapes=[dma((count,))] * 9 + [dma((4, count))] * 2,
        compiler_params=pltpu.CompilerParams(collective_id=2, has_side_effects=True, vmem_limit_bytes=60 << 20),
        name="share_kernels",
    )(made)
    return shared.reshape(8 * dims, width)


def fold_kernel(part_ref, all_ref, own, twin_in, relay_in, side_in, along_in, load_sem, keep_sem, twin_send, twin_recv, relay_send, relay_recv,
                side_send, side_recv, along_send, along_recv, swap_send, swap_recv, group_send, group_recv, give_send, give_recv):
    f32, bf16 = jnp.float32, jnp.bfloat16
    y, c, z, x, low, side, along, twin, partner, moved = quad_peers()
    over = place(1 - y, c, z, x)
    count = all_ref.shape[2] // CHUNK

    def cut(k):
        return pl.ds(k * CHUNK, CHUNK)

    def part(core, j, k):
        return part_ref.at[2 * core + (low + j // 2) % 2, (x + j % 2) % 2, cut(k)]

    def load(j, k):
        return pltpu.make_async_copy(part(c, j, k), own.at[j, cut(k)], load_sem.at[j, k])

    def swap(j, k):
        return remote(part(1 - c, j, k), twin_in.at[j, cut(k)], twin_send.at[j, k], twin_recv.at[j, k], twin)

    def relay(k):
        return remote(own.at[3, cut(k)], relay_in.at[cut(k)], relay_send.at[k], relay_recv.at[k], along if over_x(k) else side)

    def to_side(k):
        return remote(own.at[1, cut(k)], side_in.at[cut(k)], side_send.at[k], side_recv.at[k], side)

    def to_along(k):
        return remote(own.at[2, cut(k)], along_in.at[cut(k)], along_send.at[k], along_recv.at[k], along)

    def keep(k):
        return pltpu.make_async_copy(own.at[0, cut(k)], all_ref.at[y, c, cut(k)], keep_sem.at[k])

    def move(k):
        return remote(own.at[0, cut(k)], all_ref.at[y, 1 - c, cut(k)], swap_send.at[k], swap_recv.at[k], partner)

    def moved_in(k):
        return remote(own.at[0, cut(k)], all_ref.at[y, c, cut(k)], swap_send.at[k], swap_recv.at[k], partner)

    def cross(k):
        return remote(all_ref.at[y, c, cut(k)], all_ref.at[y, c, cut(k)], group_send.at[k], group_recv.at[k], over)

    def crossed(k):
        return remote(all_ref.at[1 - y, c, cut(k)], all_ref.at[1 - y, c, cut(k)], group_send.at[k], group_recv.at[k], over)

    def give(j, k):
        here = all_ref.at[(y + j) % 2, c, cut(k)]
        return remote(here, here, give_send.at[j, k], give_recv.at[j, k], twin)

    def given(j, k):
        here = all_ref.at[(y + j) % 2, 1 - c, cut(k)]
        return remote(here, here, give_send.at[j, k], give_recv.at[j, k], twin)

    def pair(j, k):
        load(j, k).wait()
        swap(j, k).wait_recv()
        return own[j, cut(k)].astype(f32) + twin_in[j, cut(k)].astype(f32)

    for k in range(count):
        for j in (3, 1, 2, 0):
            load(j, k).start()
    greet([side, along, twin, partner, over])
    for k in range(count):
        for j in (3, 1, 2, 0):
            swap(j, k).start()

    for step in range(count + 4):
        k = step
        if k < count:
            own[3, cut(k)] = pair(3, k).astype(bf16)
            relay(k).start()
        k = step - 1
        if 0 <= k < count:
            first, second = (to_along, to_side) if over_x(k) else (to_side, to_along)
            plain, summed = (2, 1) if over_x(k) else (1, 2)
            own[plain, cut(k)] = pair(plain, k).astype(bf16)
            first(k).start()
            held = pair(summed, k)
            relay(k).wait_recv()
            own[summed, cut(k)] = (held + relay_in[cut(k)].astype(f32)).astype(bf16)
            second(k).start()
        k = step - 2
        if 0 <= k < count:
            held = pair(0, k)
            to_side(k).wait_recv()
            to_along(k).wait_recv()
            held += side_in[cut(k)].astype(f32) + along_in[cut(k)].astype(f32)
            own[0, cut(k)] = held.astype(bf16)

            @pl.when(moved)
            def _(k=k):
                move(k).start()

            @pl.when(jnp.logical_not(moved))
            def _(k=k):
                keep(k).start()

        k = step - 3
        if 0 <= k < count:

            @pl.when(moved)
            def _(k=k):
                moved_in(k).wait_recv()

            @pl.when(jnp.logical_not(moved))
            def _(k=k):
                keep(k).wait()

            cross(k).start()
            give(0, k).start()
        k = step - 4
        if 0 <= k < count:
            crossed(k).wait_recv()
            give(1, k).start()

    @pl.when(moved)
    def _():
        for k in range(count):
            move(k).wait_send()

    for k in range(count):
        for j in range(4):
            swap(j, k).wait_send()
        relay(k).wait_send()
        to_side(k).wait_send()
        to_along(k).wait_send()
        cross(k).wait_send()
        for j in range(2):
            give(j, k).wait_send()
            given(j, k).wait_recv()


def fold_kernels(part):
    width = part.shape[1]
    dims = part.shape[0] // 8
    count = dims // CHUNK
    bf16 = jnp.bfloat16
    dma = pltpu.SemaphoreType.DMA
    folded = pl.pallas_call(
        fold_kernel,
        out_shape=jax.ShapeDtypeStruct((2, 2, dims, width), bf16),
        in_specs=[pl.BlockSpec(memory_space=pl.ANY)],
        out_specs=pl.BlockSpec(memory_space=pl.ANY),
        scratch_shapes=[
            pltpu.VMEM((4, dims, width), bf16),
            pltpu.VMEM((4, dims, width), bf16),
            pltpu.VMEM((dims, width), bf16),
            pltpu.VMEM((dims, width), bf16),
            pltpu.VMEM((dims, width), bf16),
            dma((4, count)),
            dma((count,)),
            dma((4, count)),
            dma((4, count)),
        ]
        + [dma((count,))] * 10
        + [dma((2, count))] * 2,
        compiler_params=pltpu.CompilerParams(collective_id=3, has_side_effects=True, vmem_limit_bytes=60 << 20),
        name="fold_kernels",
    )(part.reshape(4, 2, dims, width))
    return folded.reshape(4, dims, width)


def on_device(
    pixels,
    band_mask,
    wavelength,
    owner_order,
    rest_weight,
    rest_moment1,
    rest_moment2,
    fc_weight,
    fc_moment1,
    fc_moment2,
    cotangent,
):
    f32 = jnp.float32
    bf16 = jnp.bfloat16
    kernel_rate = float(E * PATCH * NB) ** (-0.5)
    groups = lax.axis_size("group")
    own_rows = rest_weight.shape[0]
    own_blocks = own_rows // 8
    fits = lax.axis_size("group") == 4 and lax.axis_size("img") == 8
    extra = -own_rows % 128
    slot_blocks = (own_rows + extra) // 8
    mask = band_mask.astype(f32)
    low_weight = fc_weight.astype(bf16)
    rest_low = jnp.pad(rest_weight.astype(bf16), ((0, extra), (0, 0)))
    if fits:
        mask = swap_images(mask)
        gathered = gather_packed(rest_low)
        gathered, pixels, cotangent, low_weight = lax.optimization_barrier(
            (gathered, pixels, cotangent, low_weight)
        )
        pixels, cotangent = swap_images(pixels), swap_images(cotangent)
    else:
        gathered = lax.all_gather(rest_low, ("group", "img"), axis=0, tiled=True)
    shards = gathered.size // ((own_rows + extra) * 128)
    gathered = gathered.reshape(shards, own_rows + extra, 128)
    total_blocks = owner_order.shape[0]
    slots = jnp.pad(
        owner_order.reshape(shards, own_blocks),
        ((0, 0), (0, slot_blocks - own_blocks)),
        constant_values=total_blocks,
    ).reshape(-1)
    unpacked = spread_packed(gathered, slots, total_blocks)
    block_mats, wave_mats = unpacked[:4], unpacked[4:10]
    block_vectors, wave_vectors = unpacked[10:]
    embedded = embed_waves(wavelength).reshape(groups * NB, E)
    shaped_low, own_shaped, kept, slope = wave_layer(embedded, wave_mats, wave_vectors)
    master = lax.all_gather(low_weight, "group", axis=0, tiled=True)
    kernel_low = make_kernels(shaped_low, master)
    if fits:
        kernel_all, mask = lax.optimization_barrier((share_kernels(kernel_low), mask))
    else:
        kernel_all = lax.all_gather(kernel_low, "img", axis=0, tiled=True)
    mask = jnp.repeat(mask, PATCH, axis=1)
    stream = embed_patches(pixels, mask, kernel_all)
    block_out, grad_low, block_vectors, *block_grads = block_pass(
        stream, cotangent, block_vectors, *block_mats
    )
    pixel_grad, kernel_grad = unembed_patches(pixels, mask, kernel_all, grad_low)
    if fits:
        all_groups = fold_kernels(kernel_grad)
        all_groups, block_out, pixel_grad = lax.optimization_barrier((all_groups, block_out, pixel_grad))
        block_out, pixel_grad = swap_images(block_out), swap_images(pixel_grad)
    else:
        kernel_grad_low = lax.psum_scatter(kernel_grad, "img", scatter_dimension=0, tiled=True)
        all_groups = lax.all_gather(kernel_grad_low[None], "group", axis=0, tiled=True)
    fc_new, fc_first, fc_second, shaped_part = master_update(
        all_groups,
        own_shaped,
        fc_weight,
        fc_moment1,
        fc_moment2,
        kernel_rate,
    )
    *wave_grads, wave_vectors = wave_back(shaped_part, embedded, kept, slope, wave_mats, wave_vectors)
    given = [*block_grads, *wave_grads, block_vectors, wave_vectors]
    joint_term = collect_packed(given, slots, total_blocks, shards, own_rows + extra)
    if fits:
        rest_grad = reduce_packed(joint_term.reshape(2, 2, 4, 2, own_rows + extra, 128))
    else:
        rest_grad = lax.psum_scatter(
            joint_term, ("group", "img"), scatter_dimension=0, tiled=False
        ).astype(f32)
    rest_grad = rest_grad[:own_rows]
    rest_new, rest_first, rest_second = adamw_step(
        rest_weight, rest_moment1, rest_moment2, rest_grad, rest_rate
    )
    return (block_out, pixel_grad, rest_new, rest_first, rest_second, fc_new, fc_first, fc_second)


def solution(mesh):
    placed = (
        P(("group", "img"), None, None),
        P(("group", "img"), None),
        P(),
        P(),
        P(("group", "img"), None),
        P(("group", "img"), None),
        P(("group", "img"), None),
        P("group", "img"),
        P("group", "img"),
        P("group", "img"),
        P(("group", "img"), None),
    )
    return jax.shard_map(
        on_device,
        mesh=mesh,
        in_specs=placed,
        out_specs=(
            P(("group", "img"), None),
            P(("group", "img"), None, None),
            P(("group", "img"), None),
            P(("group", "img"), None),
            P(("group", "img"), None),
            P("group", "img"),
            P("group", "img"),
            P("group", "img"),
        ),
        check_vma=False,
    )
```

profile of v0, /device:TPU:0, one launch (start us, length us, event | category | flops | bytes accessed | tf_op | source)
XLA Modules:
  0.0 553.9 jit_solution(10532813242600768827)
XLA Ops:
  7.2 1.2 convert_element_type.14
  8.5 3.2 convert_element_type.15
  11.6 0.8 pad.8.own_ref
  12.5 83.9 %gather_packed.1 = bf16[2,2,4,2,1920,128]{5,4,3,2,1,0:T(8,128)(2,1)} custom-call(bf16[1920,128]{1,0:T(8,128)(2,1)} %pad.8.own_ref), custom_call_target="tpu_custom_call" | custom-call | tf_op jit(solution)/shard_map/gather_packed/pallas_call | solution.py:791
  96.4 2.6 collective-permute-start
  99.6 3.9 collective-permute-start.2
  104.5 37.1 %spread_packed.1 = (bf16[768,2304]{1,0:T(8,128)(2,1)}, bf16[768,768]{1,0:T(8,128)(2,1)}, bf16[768,3072]{1,0:T(8,128)(2,1)}, bf16[3072,768]{1,0:T(8,128)(2,1)}, f...) custom-call(s32[7680]{0:T(1024)} %reshape.55.order_ref, ...), custom_call_target="tpu_custom_call" | custom-call | tf_op jit(solution)/shard_map/spread_packed/pallas_call | solution.py:118
  141.9 0.7 pad_maximum_fusion.embed_ref
  142.7 8.3 %wave_layer.1 = (bf16[128,128]{1,0:T(8,128)(2,1)}, bf16[128,32]{1,0:T(8,128)(2,1)}, f32[12,128,128]{2,1,0:T(8,128)}, f32[2,128,2048]{2,1,0:T(8,128)}) custom-call(f32[128,128]{1,0:T(8,128)} %pad_maximum_fusion.embed_ref, f32[128,128]{1,0:T(8,128)} %get-tuple-element.55.wq_ref, f32[128,128]{1,0:T(8,128)} %get-tuple-element.56.wk_ref, ...), custom_call_target="tpu_custom_call" | custom-call | tf_op jit(solution)/shard_map/wave_layer/pallas_call | solution.py:254
  151.0 6.4 %make_kernels.1.made_ref = bf16[96,8192]{1,0:T(8,128)(2,1)} custom-call(bf16[128,128]{1,0:T(8,128)(2,1)} %get-tuple-element.62.shaped_ref, bf16[128,24576]{1,0:T(8,128)(2,1)} %all-gather.2.cloned.1.call-done.master_ref), custom_call_target="tpu_custom_call" | custom-call | tf_op jit(solution)/shard_map/make_kernels/pallas_call | solution.py:549
  157.4 91.9 %share_kernels.1 = bf16[4,2,96,8192]{3,2,1,0:T(8,128)(2,1)} custom-call(bf16[96,8192]{1,0:T(8,128)(2,1)} %make_kernels.1.made_ref), custom_call_target="tpu_custom_call" | custom-call | tf_op jit(solution)/shard_map/share_kernels/pallas_call | solution.py:1050
  250.1 1.7 copy-done
  251.8 11.2 %embed_patches.1.stream_ref = f32[196,768]{1,0:T(8,128)} custom-call(bf16[1,196,8192]{2,1,0:T(8,128)(2,1)} %copy-done, f32[1,8192]{1,0:T(1,128)} %bitcast.16, bf16[768,8192]{1,0:T(8,128)(2,1)} %bitcast.10), custom_call_target="tpu_custom_call" | custom-call | tf_op jit(solution)/shard_map/embed_patches/pallas_call | solution.py:580
  263.0 31.1 %block_pass.1 = (bf16[196,768]{1,0:T(8,128)(2,1)}, bf16[208,768]{1,0:T(8,128)(2,1)}, f32[8,768]{1,0:T(8,128)}, bf16[768,2304]{1,0:T(8,128)(2,1)}, bf16[768,768]{...) custom-call(f32[196,768]{1,0:T(8,128)} %embed_patches.1.stream_ref, ...), custom_call_target="tpu_custom_call" | custom-call | flops 8400000000 | bytes 30000000 | tf_op jit(solution)/shard_map/block_pass/pallas_call | solution.py:481
  294.2 16.1 %unembed_patches.1 = (bf16[1,196,8192]{2,1,0:T(8,128)(2,1)}, bf16[768,8192]{1,0:T(8,128)(2,1)}) custom-call(bf16[1,196,8192]{2,1,0:T(8,128)(2,1)} %copy-done, f32[1,8192]{1,0:T(1,128)} %bitcast.17, bf16[768,8192]{1,0:T(8,128)(2,1)} %bitcast.11, bf16[208,768]{1,0:T(8,128)(2,1)} %get-tuple-element.72.low_ref), custom_call_target="tpu_custom_call" | custom-call | tf_op jit(solution)/shard_map/unembed_patches/pallas_call | solution.py:607
  310.3 85.4 %fold_kernels.1 = bf16[2,2,96,8192]{3,2,1,0:T(8,128)(2,1)} custom-call(bf16[4,2,96,8192]{3,2,1,0:T(8,128)(2,1)} %bitcast.15), custom_call_target="tpu_custom_call" | custom-call | tf_op jit(solution)/shard_map/fold_kernels/pallas_call | solution.py:1198
  395.7 2.6 collective-permute-start.4
  399.0 13.3 %master_update.1 = (f32[32,24576]{1,0:T(8,128)}, f32[32,24576]{1,0:T(8,128)}, f32[32,24576]{1,0:T(8,128)}, f32[128,32]{1,0:T(8,128)}) custom-call(bf16[4,96,8192]{2,1,0:T(8,128)(2,1)} %bitcast.14, bf16[128,32]{1,0:T(8,128)(2,1)} %get-tuple-element.83.shaped_ref, f32[32,24576]{1,0:T(8,128)} %weight_ref.1, f32[32,24576]{1,0:T(8,128)} %one_ref.1, ...), custom_call_target="tpu_custom_call" | custom-call | tf_op jit(solution)/shard_map/master_update/pallas_call | solution.py:666
  412.3 9.8 %wave_back.1 = (f32[128,128]{1,0:T(8,128)}, f32[128,128]{1,0:T(8,128)}, f32[128,128]{1,0:T(8,128)}, f32[128,128]{1,0:T(8,128)}, f32[128,2048]{1,0:T(8,128)}, /*index=5*/f32[2048,128]{1,0:T(8,128)}, f32[8,128]{1,0:T(8,128)}) custom-call(f32[128,32]{1,0:T(8,128)} %get-tuple-element.84.part_ref, f32[128,128]{1,0:T(8,128)} %pad_maximum_fusion.embed_ref, ...), custom_call_target="tpu_custom_call" | custom-call | tf_op jit(solution)/shard_map/wave_back/pallas_call | solution.py:308
  422.1 32.4 %collect_packed.1 = bf16[32,1920,128]{2,1,0:T(8,128)(2,1)} custom-call(s32[7680]{0:T(1024)} %reshape.55.order_ref, bf16[768,2304]{1,0:T(8,128)(2,1)} %get-tuple-element.78.refs_0_, bf16[768,768]{1,0:T(8,128)(2,1)} %get-tuple-element.79.refs_1_, bf16[768,3072]{1,0:T(8,128)(2,1)} %get-tuple-element.80.refs_2_, bf16[3072,768]{1,0:T(8,128)(2,1)} %get-tuple-element.81.refs_3_, ...), custom_call_target="tpu_custom_call" | custom-call | tf_op jit(solution)/shard_map/collect_packed/pallas_call | solution.py:168
  454.6 85.9 %reduce_packed.1 = f32[1920,128]{1,0:T(8,128)} custom-call(bf16[2,2,4,2,1920,128]{5,4,3,2,1,0:T(8,128)(2,1)} %bitcast.12), custom_call_target="tpu_custom_call" | custom-call | tf_op jit(solution)/shard_map/reduce_packed/pallas_call | solution.py:891
  540.5 3.7 multiply_subtract_fusion
  544.2 0.7 copy.22
  544.9 1.7 copy.23
  (35 shorter events, 3.4 us)
Async XLA Ops:
  7.2 143.8 %all-gather.2.cloned.1.call-start = ((), (), s32[]{:S(2)}) async-start(), calls=%async_computation | async-start | bytes 7864320 | tf_op jit(solution)/shard_map/all_gather | solution.py:1269
  12.5 86.5 %copy-start.7 = (s32[1,32]{1,0:T(1,128)S(1)}, s32[1,32]{1,0:T(1,128)}, u32[]{:S(2)}) copy-start(s32[1,32]{1,0:T(1,128)} %param.12) | copy-start | bytes 388
  12.5 91.1 %copy-start.5 = (s32[4,32]{1,0:T(4,128)S(1)}, s32[4,32]{1,0:T(4,128)}, u32[]{:S(2)}) copy-start(s32[4,32]{1,0:T(4,128)} %param.13) | copy-start | bytes 1540
  12.5 91.2 %copy-start.4 = (s32[7520]{0:T(1024)S(1)}, s32[7520]{0:T(1024)}, u32[]{:S(2)}) copy-start(s32[7520]{0:T(1024)} %param.14) | copy-start | bytes 90244
  96.4 153.7 %collective-permute-start = (bf16[1,196,8192]{2,1,0:T(8,128)(2,1)}, bf16[1,196,8192]{2,1,0:T(8,128)(2,1)S(1)}, u32[]{:S(2)}, u32[]{:S(2)}) collective-permute-start(bf16[1,196,8192]{2,1,0:T(8,128)(2,1)} %param.11), channel_id=1, source_target_pairs={{0,0},{1,1},{2,2},{3,3},{4,8},{5,9},{6,10},{7,11},{8,4},{9,5},{10,... | collective-permute-start | bytes 9633800 | tf_op jit(solution)/shard_map/ppermute | solution.py:935
  99.0 150.4 %collective-permute-start.1 = (f32[1,32]{1,0:T(1,128)S(1)}, f32[1,32]{1,0:T(1,128)S(1)}, u32[]{:S(2)}, u32[]{:S(2)}) collective-permute-start(f32[1,32]{1,0:T(1,128)S(1)} %convert_element_type.17), channel_id=1, source_target_pairs={{0,0},{1,1},{2,2},{3,3},{4,8},{5,9},{6,10},{7,11},{8,4},{9,5},{10,... | collective-permute-start | bytes 392 | tf_op jit(solution)/shard_map/ppermute | solution.py:935
  99.6 163.4 %collective-permute-start.2 = (bf16[196,768]{1,0:T(8,128)(2,1)}, bf16[196,768]{1,0:T(8,128)(2,1)}, u32[]{:S(2)}, u32[]{:S(2)}) collective-permute-start(bf16[196,768]{1,0:T(8,128)(2,1)} %param.21), channel_id=1, source_target_pairs={{0,0},{1,1},{2,2},{3,3},{4,8},{5,9},{6,10},{7,11},{8,4},{9,5},{10,... | collective-permute-start | bytes 903176 | tf_op jit(solution)/shard_map/ppermute | solution.py:935
  250.1 1.7 copy-start
  310.3 88.0 %copy-start.6 = (bf16[196,768]{1,0:T(8,128)(2,1)S(1)}, bf16[196,768]{1,0:T(8,128)(2,1)}, u32[]{:S(2)}) copy-start(bf16[196,768]{1,0:T(8,128)(2,1)} %get-tuple-element.76) | copy-start | bytes 903172
  395.7 148.5 %collective-permute-start.4 = (bf16[1,196,8192]{2,1,0:T(8,128)(2,1)}, bf16[1,196,8192]{2,1,0:T(8,128)(2,1)S(1)}, u32[]{:S(2)}, u32[]{:S(2)}) collective-permute-start(bf16[1,196,8192]{2,1,0:T(8,128)(2,1)} %get-tuple-element.77), channel_id=1, source_target_pairs={{0,0},{1,1},{2,2},{3,3},{4,8},{5,9},{6,10},{7,11},{8,4},{9,5},{10,... | collective-permute-start | bytes 9633800 | tf_op jit(solution)/shard_map/ppermute | solution.py:935
  398.3 145.9 %collective-permute-start.3 = (bf16[196,768]{1,0:T(8,128)(2,1)S(1)}, bf16[196,768]{1,0:T(8,128)(2,1)S(1)}, u32[]{:S(2)}, u32[]{:S(2)}) collective-permute-start(bf16[196,768]{1,0:T(8,128)(2,1)S(1)} %copy-done.6), channel_id=1, source_target_pairs={{0,0},{1,1},{2,2},{3,3},{4,8},{5,9},{6,10},{7,11},{8,4},{9,5},{10,... | collective-permute-start | bytes 903176 | tf_op jit(solution)/shard_map/ppermute | solution.py:935
  454.5 85.9 %copy-start.1 = (f32[1880,128]{1,0:T(8,128)S(1)}, f32[1880,128]{1,0:T(8,128)}, u32[]{:S(2)}) copy-start(f32[1880,128]{1,0:T(8,128)} %param.15) | copy-start | bytes 2887684
  454.6 85.9 %copy-start.2 = (f32[1880,128]{1,0:T(8,128)S(1)}, f32[1880,128]{1,0:T(8,128)}, u32[]{:S(2)}) copy-start(f32[1880,128]{1,0:T(8,128)} %param.16) | copy-start | bytes 2887684
  454.6 85.9 %copy-start.3 = (f32[1880,128]{1,0:T(8,128)S(1)}, f32[1880,128]{1,0:T(8,128)}, u32[]{:S(2)}) copy-start(f32[1880,128]{1,0:T(8,128)} %param.17) | copy-start | bytes 2887684
Sparse Core Ops, SparseCore 0:
  96.5 45.2 all-gather.1
where the time goes:
time: 563 us; the launch traced here: 554 us
  Pallas kernels  513 us (91%)
  between operations  14.6 us (3%)
  starting transfers between devices  10.4 us (2%)
  other arithmetic  9.16 us (2%)
  local copies, waits for them, and re-layouts  6.62 us (1%)
    pallas_call x1, Pallas kernels, share_kernels(): pl.pallas_call(share_kernel, out_shape=jax.ShapeDtypeStruct((4, 2, dims,...  91.9 us
    pallas_call x1, Pallas kernels, reduce_packed(): pl.pallas_call(reduce_kernel, out_shape=jax.ShapeDtypeStruct((rows, 128),...  85.9 us
    pallas_call x1, Pallas kernels, fold_kernels(): pl.pallas_call(fold_kernel, out_shape=jax.ShapeDtypeStruct((2, 2, dims, w...  85.4 us
    pallas_call x1, Pallas kernels, gather_packed(): pl.pallas_call(gather_kernel, out_shape=jax.ShapeDtypeStruct((2, 2, 4, 2,...  83.9 us
    pallas_call x1, Pallas kernels, spread_packed(): pl.pallas_call(spread_kernel, out_shape=shapes, grid_spec=pltpu.PrefetchS...  37.1 us
    pallas_call x1, Pallas kernels, collect_packed(): pl.pallas_call(collect_kernel, out_shape=jax.ShapeDtypeStruct((shards, ro...  32.4 us
    pallas_call x1, Pallas kernels, block_pass(): pl.pallas_call(block_kernel, out_shape=[jax.ShapeDtypeStruct((seq, D), bf...  31.1 us
    pallas_call x1, Pallas kernels, unembed_patches(): pl.pallas_call(unembed_kernel, out_shape=[jax.ShapeDtypeStruct(pixels.sha...  16.1 us
  transfers between devices with their start and end apart: 6, of which 0 were waited for; matrix products, arithmetic and copies ran while one was open for 1% of the time, Pallas kernels for 54%

commit v1 on v0

--- a/solution.py
+++ b/solution.py
@@ -53,6 +53,13 @@
     ]
 
 
+def embed_waves(wavelength):
+    half_width = E // 2
+    frequency = jnp.exp(-math.log(10000.0) * jnp.arange(half_width, dtype=jnp.float32) / half_width)
+    angles = wavelength.astype(jnp.float32)[..., None] * frequency
+    return jnp.concatenate([jnp.sin(angles), jnp.cos(angles)], axis=-1)
+
+
 def matrices():
     listed, at = [], 0
     for name, extent in layout():
@@ -75,26 +82,37 @@
     return listed
 
 
+def vector_shapes():
+    return [jax.ShapeDtypeStruct((8, D), jnp.float32), jax.ShapeDtypeStruct((8, E), jnp.float32)]
+
+
+def shards_a_step(shards, wanted):
+    return wanted if shards % wanted == 0 else 1
+
+
 def spread_kernel(order_ref, low_ref, *refs):
-    outs, linear = refs[:-1], refs[-1]
+    big, small = matrices()[:4], matrices()[4:]
+    far, outs, linear, kept, sem = refs[:4], refs[4:12], refs[12], refs[13:17], refs[17]
     step = pl.program_id(0)
-    rows = low_ref.shape[0]
-
-    def two(j, carry):
-        pair = low_ref[pl.ds(pl.multiple_of(j * 16, 16), 16), :].astype(jnp.float32)
-        for half in range(2):
-            block = order_ref[step * (rows // 8) + j * 2 + half]
-            linear[pl.ds(pl.multiple_of(block * 8, 8), 8), :] = pair[half * 8 : half * 8 + 8]
-        return carry
-
-    lax.fori_loop(0, rows // 16, two, 0, unroll=8)
+    shards, rows = low_ref.shape[0], low_ref.shape[1]
+
+    for shard in range(shards):
+
+        def two(j, carry, shard=shard):
+            pair = low_ref[shard, pl.ds(pl.multiple_of(j * 16, 16), 16), :].astype(jnp.float32)
+            for half in range(2):
+                block = order_ref[(step * shards + shard) * (rows // 8) + j * 2 + half]
+                linear[pl.ds(pl.multiple_of(block * 8, 8), 8), :] = pair[half * 8 : half * 8 + 8]
+            return carry
+
+        lax.fori_loop(0, rows // 16, two, 0, unroll=8)
 
     @pl.when(step == pl.num_programs(0) - 1)
     def _():
-        for (name, height, width, first), out in zip(matrices(), outs):
+        def relay(height, width, first, out):
             lanes = width // 128
 
-            def some(j, carry, out=out, lanes=lanes, first=first):
+            def some(j, carry):
                 top = pl.multiple_of(j * 128, 128)
                 for lane in range(lanes):
                     part = linear[pl.ds(first + top * lanes + lane, 128, stride=lanes), :]
@@ -102,28 +120,40 @@
                 return carry
 
             lax.fori_loop(0, height // 128, some, 0)
+
+        copies = []
+        for j, (name, height, width, first) in enumerate(big):
+            relay(height, width, first, kept[j])
+            copies.append(pltpu.make_async_copy(kept[j], far[j], sem.at[j]))
+            copies[-1].start()
+        for (name, height, width, first), out in zip(small, outs):
+            relay(height, width, first, out)
         for out in outs[-2:]:
             out[...] = jnp.zeros_like(out)
         for row, kind, top, lane in vector_places():
             outs[kind - 2][top : top + 1, lane : lane + 128] = linear[row : row + 1, :]
+        for copy in copies:
+            copy.wait()
 
 
 def spread_packed(gathered, slots, blocks):
     shards, rows = gathered.shape[0], gathered.shape[1]
-    shapes = [
-        jax.ShapeDtypeStruct((height, width), jnp.bfloat16 if name.startswith("w_") else jnp.float32)
-        for name, height, width, first in matrices()
-    ]
-    shapes += [jax.ShapeDtypeStruct((8, D), jnp.float32), jax.ShapeDtypeStruct((8, E), jnp.float32)]
+    some = shards_a_step(shards, 4)
+    big = [jax.ShapeDtypeStruct((height, width), jnp.bfloat16) for name, height, width, first in matrices()[:4]]
+    small = [jax.ShapeDtypeStruct((height, width), jnp.float32) for name, height, width, first in matrices()[4:]]
+    small += vector_shapes()
     return pl.pallas_call(
         spread_kernel,
-        out_shape=shapes,
+        out_shape=big + small,
         grid_spec=pltpu.PrefetchScalarGridSpec(
             num_scalar_prefetch=1,
-            grid=(shards,),
-            in_specs=[pl.BlockSpec((None, rows, 128), lambda s, order: (s, 0, 0))],
-            out_specs=[pl.BlockSpec(shape.shape, lambda s, order: (0, 0), pipeline_mode=pl.Buffered(1)) for shape in shapes],
-            scratch_shapes=[pltpu.VMEM(((blocks + 1) * 8, 128), jnp.float32)],
+            grid=(shards // some,),
+            in_specs=[pl.BlockSpec((some, rows, 128), lambda s, order: (s, 0, 0))],
+            out_specs=[pl.BlockSpec(memory_space=pl.ANY) for shape in big]
+            + [pl.BlockSpec(shape.shape, lambda s, order: (0, 0), pipeline_mode=pl.Buffered(1)) for shape in small],
+            scratch_shapes=[pltpu.VMEM(((blocks + 1) * 8, 128), jnp.float32)]
+            + [pltpu.VMEM(shape.shape, shape.dtype) for shape in big]
+            + [pltpu.SemaphoreType.DMA((4,))],
         ),
         compiler_params=pltpu.CompilerParams(vmem_limit_bytes=60 << 20),
         name="spread_packed",
@@ -131,16 +161,21 @@
 
 
 def collect_kernel(order_ref, *refs):
-    ins, low_ref, linear = refs[:-2], refs[-2], refs[-1]
+    big, small = matrices()[:4], matrices()[4:]
+    far, ins, low_ref, linear, kept, sem = refs[:4], refs[4:12], refs[12], refs[13], refs[14:18], refs[18]
     step = pl.program_id(0)
-    rows = low_ref.shape[0]
+    shards, rows = low_ref.shape[0], low_ref.shape[1]
 
     @pl.when(step == 0)
     def _():
-        for (name, height, width, first), given in zip(matrices(), ins):
+        copies = [pltpu.make_async_copy(far[j], kept[j], sem.at[j]) for j in range(4)]
+        for copy in copies:
+            copy.start()
+
+        def relay(height, width, first, given):
             lanes = width // 128
 
-            def some(j, carry, given=given, lanes=lanes, first=first):
+            def some(j, carry):
                 top = pl.multiple_of(j * 128, 128)
                 for lane in range(lanes):
                     part = given[pl.ds(top, 128), lane * 128 : lane * 128 + 128]
@@ -148,43 +183,48 @@
                 return carry
 
             lax.fori_loop(0, height // 128, some, 0)
+
+        for (name, height, width, first), given in zip(small, ins):
+            relay(height, width, first, given)
         first = vector_places()[0][0]
         linear[first:, :] = jnp.zeros((linear.shape[0] - first, 128), jnp.float32)
         for row, kind, top, lane in vector_places():
             linear[row : row + 1, :] = ins[kind - 2][top : top + 1, lane : lane + 128]
-
-    def two(j, carry):
-        parts = []
-        for half in range(2):
-            block = order_ref[step * (rows // 8) + j * 2 + half]
-            parts.append(linear[pl.ds(pl.multiple_of(block * 8, 8), 8), :])
-        low_ref[pl.ds(pl.multiple_of(j * 16, 16), 16), :] = jnp.concatenate(parts, axis=0).astype(low_ref.dtype)
-        return carry
-
-    lax.fori_loop(0, rows // 16, two, 0, unroll=8)
+        for j, (name, height, width, first) in enumerate(big):
+            copies[j].wait()
+            relay(height, width, first, kept[j])
+
+    for shard in range(shards):
+
+        def two(j, carry, shard=shard):
+            parts = []
+            for half in range(2):
+                block = order_ref[(step * shards + shard) * (rows // 8) + j * 2 + half]
+                parts.append(linear[pl.ds(pl.multiple_of(block * 8, 8), 8), :])
+            low_ref[shard, pl.ds(pl.multiple_of(j * 16, 16), 16), :] = jnp.concatenate(parts, axis=0).astype(low_ref.dtype)
+            return carry
+
+        lax.fori_loop(0, rows // 16, two, 0, unroll=20)
 
 
 def collect_packed(grads, slots, blocks, shards, rows):
+    some = shards_a_step(shards, 2)
+    whole = [pl.BlockSpec(grad.shape, lambda s, order: (0, 0), pipeline_mode=pl.Buffered(1)) for grad in grads[4:]]
     return pl.pallas_call(
         collect_kernel,
         out_shape=jax.ShapeDtypeStruct((shards, rows, 128), jnp.bfloat16),
         grid_spec=pltpu.PrefetchScalarGridSpec(
             num_scalar_prefetch=1,
-            grid=(shards,),
-            in_specs=[pl.BlockSpec(grad.shape, lambda s, order: (0, 0), pipeline_mode=pl.Buffered(1)) for grad in grads],
-            out_specs=pl.BlockSpec((None, rows, 128), lambda s, order: (s, 0, 0)),
-            scratch_shapes=[pltpu.VMEM(((blocks + 1) * 8, 128), jnp.float32)],
+            grid=(shards // some,),
+            in_specs=[pl.BlockSpec(memory_space=pl.ANY)] * 4 + whole,
+            out_specs=pl.BlockSpec((some, rows, 128), lambda s, order: (s, 0, 0)),
+            scratch_shapes=[pltpu.VMEM(((blocks + 1) * 8, 128), jnp.float32)]
+            + [pltpu.VMEM(grad.shape, grad.dtype) for grad in grads[:4]]
+            + [pltpu.SemaphoreType.DMA((4,))],
         ),
         compiler_params=pltpu.CompilerParams(vmem_limit_bytes=60 << 20),
         name="collect_packed",
     )(slots, *grads)
-
-
-def embed_waves(wavelength):
-    half_width = E // 2
-    frequency = jnp.exp(-math.log(10000.0) * jnp.arange(half_width, dtype=jnp.float32) / half_width)
-    angles = wavelength.astype(jnp.float32)[..., None] * frequency
-    return jnp.concatenate([jnp.sin(angles), jnp.cos(angles)], axis=-1)
 
 
 def exact(a, b, left, right):
@@ -523,6 +563,7 @@
 
 
 NC = 15
+HEAD = 96
 
 
 def dims_step(count):
@@ -592,27 +633,24 @@
     )(pixels, mask, kernels)
 
 
-def unembed_kernel(pixel_ref, mask_ref, kernel_ref, low_ref, back_ref, grad_ref, masked):
-    seq = pixel_ref.shape[0]
-    mask = mask_ref[...]
-    masked[...] = jnp.zeros_like(masked)
-    masked[0:seq, :] = pixel_ref[...].astype(jnp.float32) * mask
-    back_ref[...] = (dot_nn(low_ref[...], kernel_ref[...])[0:seq] * mask).astype(back_ref.dtype)
-    grad_ref[...] = dot_tn(low_ref[...], masked[...].astype(jnp.bfloat16)).astype(grad_ref.dtype)
-
-
-def unembed_patches(pixels, mask, kernels, low):
-    seq, width = pixels.shape[1], pixels.shape[2]
+def unembed_kernel(masked_ref, mask_ref, kernel_ref, low_ref, back_ref, grad_ref):
+    seq = back_ref.shape[0]
+    back_ref[...] = (dot_nn(low_ref[...], kernel_ref[...])[0:seq] * mask_ref[...]).astype(back_ref.dtype)
+    grad_ref[...] = dot_tn(low_ref[...], masked_ref[...]).astype(grad_ref.dtype)
+
+
+def unembed_patches(masked, mask, kernels, low, seq):
+    rows, width = masked.shape
     cut = 1024
     return pl.pallas_call(
         unembed_kernel,
         out_shape=[
-            jax.ShapeDtypeStruct(pixels.shape, jnp.bfloat16),
+            jax.ShapeDtypeStruct((1, seq, width), jnp.bfloat16),
             jax.ShapeDtypeStruct((D, width), jnp.bfloat16),
         ],
         grid=(width // cut,),
         in_specs=[
-            pl.BlockSpec((None, seq, cut), lambda j: (0, 0, j)),
+            pl.BlockSpec((rows, cut), lambda j: (0, j)),
             pl.BlockSpec((1, cut), lambda j: (0, j)),
             pl.BlockSpec((D, cut), lambda j: (0, j)),
             pl.BlockSpec(low.shape, lambda j: (0, 0)),
@@ -621,10 +659,9 @@
             pl.BlockSpec((None, seq, cut), lambda j: (0, 0, j)),
             pl.BlockSpec((D, cut), lambda j: (0, j)),
         ],
-        scratch_shapes=[pltpu.VMEM((low.shape[0], cut), jnp.float32)],
         compiler_params=pltpu.CompilerParams(vmem_limit_bytes=60 << 20),
         name="unembed_patches",
-    )(pixels, mask, kernels, low)
+    )(masked, mask, kernels, low)
 
 
 def master_kernel(rate, grad_ref, shaped_ref, weight_ref, one_ref, two_ref, new_ref, first_ref, second_ref, back_ref, turned):
@@ -706,18 +743,23 @@
     pl.semaphore_wait(barrier, len(peers))
 
 
-def gather_kernel(own_ref, all_ref, local_sem, line_send, line_recv, group_send, group_recv, twin_send, twin_recv):
+def remote(src, dst, send_sem, recv_sem, target):
+    return pltpu.make_async_remote_copy(
+        src_ref=src, dst_ref=dst, send_sem=send_sem, recv_sem=recv_sem, device_id=target, device_id_type=MESH
+    )
+
+
+def gather_kernel(own_ref, pixel_ref, all_ref, head_ref, head_sem, local_sem, line_send, line_recv, group_send, group_recv, twin_send, twin_recv):
     y, c, z, x = spot()
     (x2, y2), (x3, y3), around, second, third, twin = partners()
+    partner = place(y, 1 - c, (z + 2) % 4, x)
+    moved = (c + z // 2) % 2 == 1
     rows = own_ref.shape[0] // NC
 
     def cut(k):
         return pl.ds(k * rows, rows)
 
-    def remote(src, dst, send_sem, recv_sem, target):
-        return pltpu.make_async_remote_copy(
-            src_ref=src, dst_ref=dst, send_sem=send_sem, recv_sem=recv_sem, device_id=target, device_id_type=MESH
-        )
+    head = remote(pixel_ref.at[0, pl.ds(0, HEAD)], head_ref.at[0], head_sem.at[0], head_sem.at[1], partner)
 
     def along(d, k):
         return remote(own_ref.at[cut(k)], all_ref.at[y, c, z, x, cut(k)], line_send.at[d - 1, k], line_recv.at[d - 1, k], around[d - 1])
@@ -750,7 +792,7 @@
 
     keep = pltpu.make_async_copy(own_ref, all_ref.at[y, c, z, x], local_sem)
     keep.start()
-    greet(around + [second, third, twin])
+    greet(around + [second, third, twin, partner])
     for k in range(NC):
         for d in (1, 2, 3):
             along(d, k).start()
@@ -763,6 +805,12 @@
             hop(0, third, k, 0, 2).start()
             hop(0, second, k, 1, 1).start()
             share(0, k).start()
+        if step == NC - 3:
+
+            @pl.when(moved)
+            def _():
+                head.start()
+
         k = step - 1
         if 0 <= k < NC:
             hop_in(1, k).wait_recv()
@@ -784,19 +832,26 @@
             share(j, k).wait_send()
             share_in(j, k).wait_recv()
 
-
-def gather_packed(own):
+    @pl.when(moved)
+    def _():
+        head.wait()
+
+
+def gather_packed(own, pixels):
     rows = own.shape[0]
     dma = pltpu.SemaphoreType.DMA
     return pl.pallas_call(
         gather_kernel,
-        out_shape=jax.ShapeDtypeStruct((2, 2, 4, 2, rows, 128), own.dtype),
-        in_specs=[pl.BlockSpec(memory_space=pltpu.VMEM)],
-        out_specs=pl.BlockSpec(memory_space=pl.ANY),
-        scratch_shapes=[dma, dma((3, NC)), dma((3, NC)), dma((3, NC)), dma((4, NC)), dma((4, NC)), dma((4, NC))],
+        out_shape=[
+            jax.ShapeDtypeStruct((2, 2, 4, 2, rows, 128), own.dtype),
+            jax.ShapeDtypeStruct((1, HEAD, pixels.shape[2]), pixels.dtype),
+        ],
+        in_specs=[pl.BlockSpec(memory_space=pltpu.VMEM), pl.BlockSpec(memory_space=pl.ANY)],
+        out_specs=[pl.BlockSpec(memory_space=pl.ANY)] * 2,
+        scratch_shapes=[dma((2,)), dma, dma((3, NC)), dma((3, NC)), dma((3, NC)), dma((4, NC)), dma((4, NC)), dma((4, NC))],
         compiler_params=pltpu.CompilerParams(collective_id=0, has_side_effects=True, vmem_limit_bytes=60 << 20),
         name="gather_packed",
-    )(own)
+    )(own, pixels)
 
 
 def reduce_kernel(part_ref, sum_ref, own, twin_in, third_in, second_in, line_in, load_sem, twin_send, twin_recv, third_send, third_recv, second_send, second_recv, line_send, line_recv):
@@ -807,11 +862,6 @@
 
     def cut(k):
         return pl.ds(k * rows, rows)
-
-    def remote(src, dst, send_sem, recv_sem, target):
-        return pltpu.make_async_remote_copy(
-            src_ref=src, dst_ref=dst, send_sem=send_sem, recv_sem=recv_sem, device_id=target, device_id_type=MESH
-        )
 
     spots = ((1 - y, 1 - x), (y3, x3), (y2, x2), (y, x))
     turned = ((1 - y, 1 - x), (y2, x2), (y3, x3), (y, x))
@@ -935,21 +985,20 @@
     return lax.ppermute(value, ("group", "img"), pairs)
 
 
-def remote(src, dst, send_sem, recv_sem, target):
-    return pltpu.make_async_remote_copy(
-        src_ref=src, dst_ref=dst, send_sem=send_sem, recv_sem=recv_sem, device_id=target, device_id_type=MESH
-    )
-
-
-def share_kernel(made_ref, all_ref, keep_sem, swap_send, swap_recv, side_send, side_recv, along_send, along_recv, far_send, far_recv, twin_send, twin_recv):
+def share_kernel(made_ref, mask_ref, pixel_ref, head_ref, rest_ref, all_ref, masked_ref, stream_ref,
+                 held, top, bottom, tile, mixed, order, pixel_sem, store_sem, keep_sem, swap_send, swap_recv,
+                 side_send, side_recv, along_send, along_recv, far_send, far_recv, twin_send, twin_recv):
+    f32, bf16 = jnp.float32, jnp.bfloat16
     y, c, z, x, low, side, along, twin, partner, moved = quad_peers()
-    count = made_ref.shape[0] // CHUNK
+    dims, width = made_ref.shape
+    count = dims // CHUNK
+    group = 8 * CHUNK
 
     def cut(k):
         return pl.ds(k * CHUNK, CHUNK)
 
     def block(core, j, k):
-        return all_ref.at[2 * core + (low + j // 2) % 2, (x + j % 2) % 2, cut(k)]
+        return held.at[2 * core + (low + j // 2) % 2, (x + j % 2) % 2, cut(k)]
 
     def keep(k):
         return pltpu.make_async_copy(made_ref.at[cut(k)], block(c, 0, k), keep_sem.at[k])
@@ -985,19 +1034,53 @@
     def given(j, k):
         return remote(block(1 - c, j, k), block(1 - c, j, k), twin_send.at[j, k], twin_recv.at[j, k], twin)
 
+    def store(k):
+        return pltpu.make_async_copy(held.at[:, :, cut(k)], all_ref.at[:, :, cut(k)], store_sem.at[k])
+
+    swapped = pltpu.make_async_copy(head_ref.at[0], top, pixel_sem.at[0])
+    owned = pltpu.make_async_copy(pixel_ref.at[0, pl.ds(0, HEAD)], top, pixel_sem.at[0])
+    lower = pltpu.make_async_copy(rest_ref.at[0], bottom, pixel_sem.at[1])
+
     @pl.when(jnp.logical_not(moved))
     def _():
+        owned.start()
         for k in range(count):
             keep(k).start()
 
+    lower.start()
     greet([side, along, twin, partner])
 
     @pl.when(moved)
     def _():
+        swapped.start()
         for k in range(count):
             swap(k).start()
 
-    for step in range(count + 2):
+    def mask_pixels(part):
+        @pl.when(part == 0)
+        def _():
+            lower.wait()
+            owned.wait()
+
+        def some(j, carry):
+            lanes = pl.ds(pl.multiple_of(j * 1024, 1024), 1024)
+            mask = mask_ref[:, lanes]
+            masked_ref[0:HEAD, lanes] = (top[:, lanes].astype(f32) * mask).astype(bf16)
+            tile[...] = jnp.zeros_like(tile)
+            tile[0 : bottom.shape[0], :] = bottom[:, lanes].astype(f32) * mask
+            masked_ref[HEAD:, lanes] = tile[...].astype(bf16)
+            return carry
+
+        cuts = width // 1024
+        lax.fori_loop(part * (cuts // 2), (part + 1) * (cuts // 2), some, 0)
+
+    def make_order():
+        row = lax.broadcasted_iota(jnp.int32, order.shape, 0)
+        column = lax.broadcasted_iota(jnp.int32, order.shape, 1)
+        wanted = row % group // CHUNK * dims + row // group * CHUNK + row % CHUNK
+        order[...] = jnp.where(column == wanted, 1.0, 0.0)
+
+    for step in range(count + 3):
         k = step
         if k < count:
 
@@ -1012,6 +1095,10 @@
             to_side(k).start()
             to_along(k).start()
             give(0, k).start()
+        if step < 2:
+            mask_pixels(step)
+        elif step == 2:
+            make_order()
         k = step - 1
         if 0 <= k < count:
             if over_x(k):
@@ -1028,6 +1115,15 @@
         if 0 <= k < count:
             from_far(k).wait_recv()
             give(3, k).start()
+        k = step - 3
+        if 0 <= k < count:
+            for j in range(4):
+                given(j, k).wait_recv()
+            store(k).start()
+            part = held[:, :, cut(k), :].reshape(group, width)
+            mixed[:, k * group : (k + 1) * group] = dot_nt(masked_ref[...], part)
+
+    stream_ref[...] = exact(mixed[...], order[...], 1, 0)[0 : stream_ref.shape[0]]
 
     @pl.when(moved)
     def _():
@@ -1038,25 +1134,43 @@
         to_side(k).wait_send()
         to_along(k).wait_send()
         pass_on(k).wait_send()
+        store(k).wait()
         for j in range(4):
             give(j, k).wait_send()
-            given(j, k).wait_recv()
-
-
-def share_kernels(made):
+
+
+def share_kernels(made, mask, pixels, head, rest):
     dims, width = made.shape
     count = dims // CHUNK
+    seq = pixels.shape[1]
+    rows = tall(seq)
+    f32 = jnp.float32
     dma = pltpu.SemaphoreType.DMA
-    shared = pl.pallas_call(
+    vmem, far = pl.BlockSpec(memory_space=pltpu.VMEM), pl.BlockSpec(memory_space=pl.ANY)
+    shared, masked, stream = pl.pallas_call(
         share_kernel,
-        out_shape=jax.ShapeDtypeStruct((4, 2, dims, width), made.dtype),
-        in_specs=[pl.BlockSpec(memory_space=pltpu.VMEM)],
-        out_specs=pl.BlockSpec(memory_space=pl.ANY),
-        scratch_shapes=[dma((count,))] * 9 + [dma((4, count))] * 2,
+        out_shape=[
+            jax.ShapeDtypeStruct((4, 2, dims, width), made.dtype),
+            jax.ShapeDtypeStruct((rows, width), made.dtype),
+            jax.ShapeDtypeStruct((seq, 8 * dims), f32),
+        ],
+        in_specs=[vmem, vmem, far, far, far],
+        out_specs=[far, vmem, vmem],
+        scratch_shapes=[
+            pltpu.VMEM((4, 2, dims, width), made.dtype),
+            pltpu.VMEM((HEAD, width), made.dtype),
+            pltpu.VMEM((seq - HEAD, width), made.dtype),
+            pltpu.VMEM((rows - HEAD, 1024), f32),
+            pltpu.VMEM((rows, 8 * dims), f32),
+            pltpu.VMEM((8 * dims, 8 * dims), f32),
+            dma((2,)),
+        ]
+        + [dma((count,))] * 10
+        + [dma((4, count))] * 2,
         compiler_params=pltpu.CompilerParams(collective_id=2, has_side_effects=True, vmem_limit_bytes=60 << 20),
         name="share_kernels",
-    )(made)
-    return shared.reshape(8 * dims, width)
+    )(made, mask, pixels, head, rest)
+    return shared.reshape(8 * dims, width), masked, stream
 
 
 def fold_kernel(part_ref, all_ref, own, twin_in, relay_in, side_in, along_in, load_sem, keep_sem, twin_send, twin_recv, relay_send, relay_recv,
@@ -1246,11 +1360,11 @@
     rest_low = jnp.pad(rest_weight.astype(bf16), ((0, extra), (0, 0)))
     if fits:
         mask = swap_images(mask)
-        gathered = gather_packed(rest_low)
-        gathered, pixels, cotangent, low_weight = lax.optimization_barrier(
-            (gathered, pixels, cotangent, low_weight)
+        gathered, head = gather_packed(rest_low, pixels)
+        gathered, rest, cotangent, low_weight = lax.optimization_barrier(
+            (gathered, pixels[:, HEAD:], cotangent, low_weight)
         )
-        pixels, cotangent = swap_images(pixels), swap_images(cotangent)
+        rest, cotangent = swap_images(rest), swap_images(cotangent)
     else:
         gathered = lax.all_gather(rest_low, ("group", "img"), axis=0, tiled=True)
     shards = gathered.size // ((own_rows + extra) * 128)
@@ -1268,16 +1382,17 @@
     shaped_low, own_shaped, kept, slope = wave_layer(embedded, wave_mats, wave_vectors)
     master = lax.all_gather(low_weight, "group", axis=0, tiled=True)
     kernel_low = make_kernels(shaped_low, master)
+    mask = jnp.repeat(mask, PATCH, axis=1)
     if fits:
-        kernel_all, mask = lax.optimization_barrier((share_kernels(kernel_low), mask))
+        kernel_all, masked, stream = share_kernels(kernel_low, mask, pixels, head, rest)
     else:
         kernel_all = lax.all_gather(kernel_low, "img", axis=0, tiled=True)
-    mask = jnp.repeat(mask, PATCH, axis=1)
-    stream = embed_patches(pixels, mask, kernel_all)
+        stream = embed_patches(pixels, mask, kernel_all)
+        masked = jnp.pad((pixels[0] * mask).astype(bf16), ((0, tall(pixels.shape[1]) - pixels.shape[1]), (0, 0)))
     block_out, grad_low, block_vectors, *block_grads = block_pass(
         stream, cotangent, block_vectors, *block_mats
     )
-    pixel_grad, kernel_grad = unembed_patches(pixels, mask, kernel_all, grad_low)
+    pixel_grad, kernel_grad = unembed_patches(masked, mask, kernel_all, grad_low, pixels.shape[1])
     if fits:
         all_groups = fold_kernels(kernel_grad)
         all_groups, block_out, pixel_grad = lax.optimization_barrier((all_groups, block_out, pixel_grad))

time: 563 us -> 550 us (0.977)
  Pallas kernels: 513 us -> 486 us
  waiting for transfers between devices: 0.03 us -> 15.4 us
    pallas_call x5 -> x4, Pallas kernels: 240 us -> 210 us  [the longest x1 83.5 us: gather_packed(): pl.pallas_call(gather_kernel, out_shape=[jax.ShapeDtypeStruct((2, 2, 4, 2...]
    all_gather x1, waiting for transfers between devices: 0.01 us -> 15.4 us  [on_device(): master = lax.all_gather(low_weight, 'group', axis=0, tiled=True)]
    pallas_call x1, Pallas kernels: 85.9 us -> 95.7 us  [reduce_packed(): pl.pallas_call(reduce_kernel, out_shape=jax.ShapeDtypeStruct((rows, 128),...]
    pallas_call x1, Pallas kernels: 32.4 us -> 25.8 us  [collect_packed(): pl.pallas_call(collect_kernel, out_shape=jax.ShapeDtypeStruct((shards, ro...]
  transfers between devices with their start and end apart: 6 -> 6, of which waited for: 0 -> 1; matrix products, arithmetic and copies ran while one was open for 1% -> 1% of each run, Pallas kernels for 54% -> 50%
where the time goes in v1:
time: 550 us; the launch traced here: 542 us
  Pallas kernels  486 us (88%)
  waiting for transfers between devices  15.4 us (3%)
  between operations  14.5 us (3%)
  other arithmetic  10.1 us (2%)
  starting transfers between devices  8.55 us (2%)
  local copies, waits for them, and re-layouts  7.42 us (1%)
    pallas_call x1, Pallas kernels, reduce_packed(): pl.pallas_call(reduce_kernel, out_shape=jax.ShapeDtypeStruct((rows, 128),...  95.7 us
    pallas_call x1, Pallas kernels, fold_kernels(): pl.pallas_call(fold_kernel, out_shape=jax.ShapeDtypeStruct((2, 2, dims, w...  84.6 us
    pallas_call x1, Pallas kernels, gather_packed(): pl.pallas_call(gather_kernel, out_shape=[jax.ShapeDtypeStruct((2, 2, 4, 2...  83.5 us
    pallas_call x1, Pallas kernels, share_kernels(): pl.pallas_call(share_kernel, out_shape=[jax.ShapeDtypeStruct((4, 2, dims,...  83.3 us
    pallas_call x1, Pallas kernels, block_pass(): pl.pallas_call(block_kernel, out_shape=[jax.ShapeDtypeStruct((seq, D), bf...  31.5 us
    pallas_call x1, Pallas kernels, spread_packed(): pl.pallas_call(spread_kernel, out_shape=big + small, grid_spec=pltpu.Pref...  27.2 us
    pallas_call x1, Pallas kernels, collect_packed(): pl.pallas_call(collect_kernel, out_shape=jax.ShapeDtypeStruct((shards, ro...  25.8 us
    pallas_call x1, Pallas kernels, unembed_patches(): pl.pallas_call(unembed_kernel, out_shape=[jax.ShapeDtypeStruct((1, seq, w...  16.1 us
  transfers between devices with their start and end apart: 6, of which 1 were waited for; matrix products, arithmetic and copies ran while one was open for 1% of the time, Pallas kernels for 50%

profile of v1, /device:TPU:0, one launch (start us, length us, event | category | flops | bytes accessed | tf_op | source)
XLA Modules:
  0.0 541.5 jit_solution(4723403737545917637)
XLA Ops:
  7.2 2.2 convert_element_type.15
  9.4 3.2 convert_element_type.16
  12.6 1.3 slice.6
  13.9 0.8 pad.9.own_ref
  14.7 83.5 %gather_packed.1 = (bf16[2,2,4,2,1920,128]{5,4,3,2,1,0:T(8,128)(2,1)}, bf16[1,96,8192]{2,1,0:T(8,128)(2,1)}) custom-call(bf16[1920,128]{1,0:T(8,128)(2,1)} %pad.9.own_ref, bf16[1,196,8192]{2,1,0:T(8,128)(2,1)} %pixel_ref.3), custom_call_target="tpu_custom_call" | custom-call | tf_op jit(solution)/shard_map/gather_packed/pallas_call | solution.py:843
  98.3 0.8 collective-permute-start.1
  99.8 3.8 collective-permute-start.2
  104.5 27.2 %spread_packed.1 = (bf16[768,2304]{1,0:T(8,128)(2,1)}, bf16[768,768]{1,0:T(8,128)(2,1)}, bf16[768,3072]{1,0:T(8,128)(2,1)}, bf16[3072,768]{1,0:T(8,128)(2,1)}, f...) custom-call(s32[7680]{0:T(1024)} %reshape.55.order_ref, ...), custom_call_target="tpu_custom_call" | custom-call | tf_op jit(solution)/shard_map/spread_packed/pallas_call | solution.py:145
  132.1 0.7 pad_maximum_fusion.embed_ref
  132.8 8.3 %wave_layer.1 = (bf16[128,128]{1,0:T(8,128)(2,1)}, bf16[128,32]{1,0:T(8,128)(2,1)}, f32[12,128,128]{2,1,0:T(8,128)}, f32[2,128,2048]{2,1,0:T(8,128)}) custom-call(f32[128,128]{1,0:T(8,128)} %pad_maximum_fusion.embed_ref, f32[128,128]{1,0:T(8,128)} %get-tuple-element.58.wq_ref, f32[128,128]{1,0:T(8,128)} %get-tuple-element.59.wk_ref, ...), custom_call_target="tpu_custom_call" | custom-call | tf_op jit(solution)/shard_map/wave_layer/pallas_call | solution.py:294
  141.9 15.4 %all-gather.2.cloned.1.call-done.master_ref = bf16[128,24576]{1,0:T(8,128)(2,1)} async-done(((bf16[32,24576]{1,0:T(8,128)(2,1)}), bf16[128,24576]{1,0:T(8,128)(2,1)}) %all-gather.2.cloned.1.call-update) | async-done | bytes 6291472 | tf_op jit(solution)/shard_map/all_gather | solution.py:1383
  157.2 6.4 %make_kernels.1.made_ref = bf16[96,8192]{1,0:T(8,128)(2,1)} custom-call(bf16[128,128]{1,0:T(8,128)(2,1)} %get-tuple-element.65.shaped_ref, bf16[128,24576]{1,0:T(8,128)(2,1)} %all-gather.2.cloned.1.call-done.master_ref), custom_call_target="tpu_custom_call" | custom-call | tf_op jit(solution)/shard_map/make_kernels/pallas_call | solution.py:590
  163.7 1.2 copy-done.4
  164.8 83.3 %share_kernels.1 = (bf16[4,2,96,8192]{3,2,1,0:T(8,128)(2,1)}, bf16[208,8192]{1,0:T(8,128)(2,1)}, f32[196,768]{1,0:T(8,128)}) custom-call(bf16[96,8192]{1,0:T(8,128)(2,1)} %make_kernels.1.made_ref, f32[1,8192]{1,0:T(1,128)} %bitcast.15, bf16[1,196,8192]{2,1,0:T(8,128)(2,1)} %pixel_ref.3, bf16[1,96,8192]{2,1,0:T(8,128)(2,1)} %get-tuple-element.67.head_ref, ...), custom_call_target="tpu_custom_call" | custom-call | tf_op jit(solution)/shard_map/share_kernels/pallas_call | solution.py:1150
  248.2 31.5 %block_pass.1 = (bf16[196,768]{1,0:T(8,128)(2,1)}, bf16[208,768]{1,0:T(8,128)(2,1)}, f32[8,768]{1,0:T(8,128)}, bf16[768,2304]{1,0:T(8,128)(2,1)}, bf16[768,768]{...) custom-call(f32[196,768]{1,0:T(8,128)} %get-tuple-element.71.stream_ref, ...), custom_call_target="tpu_custom_call" | custom-call | flops 8400000000 | bytes 30000000 | tf_op jit(solution)/shard_map/block_pass/pallas_call | solution.py:521
  279.7 16.1 %unembed_patches.1 = (bf16[1,196,8192]{2,1,0:T(8,128)(2,1)}, bf16[768,8192]{1,0:T(8,128)(2,1)}) custom-call(bf16[208,8192]{1,0:T(8,128)(2,1)} %get-tuple-element.69.masked_ref, f32[1,8192]{1,0:T(1,128)} %bitcast.16, bf16[768,8192]{1,0:T(8,128)(2,1)} %bitcast.14, bf16[208,768]{1,0:T(8,128)(2,1)} %get-tuple-element.78.low_ref), custom_call_target="tpu_custom_call" | custom-call | tf_op jit(solution)/shard_map/unembed_patches/pallas_call | solution.py:645
  295.8 84.6 %fold_kernels.1 = bf16[2,2,96,8192]{3,2,1,0:T(8,128)(2,1)} custom-call(bf16[4,2,96,8192]{3,2,1,0:T(8,128)(2,1)} %bitcast.13), custom_call_target="tpu_custom_call" | custom-call | tf_op jit(solution)/shard_map/fold_kernels/pallas_call | solution.py:1312
  380.4 2.6 collective-permute-start.4
  383.7 13.3 %master_update.1 = (f32[32,24576]{1,0:T(8,128)}, f32[32,24576]{1,0:T(8,128)}, f32[32,24576]{1,0:T(8,128)}, f32[128,32]{1,0:T(8,128)}) custom-call(bf16[4,96,8192]{2,1,0:T(8,128)(2,1)} %bitcast.11, bf16[128,32]{1,0:T(8,128)(2,1)} %get-tuple-element.89.shaped_ref, f32[32,24576]{1,0:T(8,128)} %weight_ref.1, f32[32,24576]{1,0:T(8,128)} %one_ref.1, ...), custom_call_target="tpu_custom_call" | custom-call | tf_op jit(solution)/shard_map/master_update/pallas_call | solution.py:703
  397.0 9.8 %wave_back.1 = (f32[128,128]{1,0:T(8,128)}, f32[128,128]{1,0:T(8,128)}, f32[128,128]{1,0:T(8,128)}, f32[128,128]{1,0:T(8,128)}, f32[128,2048]{1,0:T(8,128)}, /*index=5*/f32[2048,128]{1,0:T(8,128)}, f32[8,128]{1,0:T(8,128)}) custom-call(f32[128,32]{1,0:T(8,128)} %get-tuple-element.90.part_ref, f32[128,128]{1,0:T(8,128)} %pad_maximum_fusion.embed_ref, ...), custom_call_target="tpu_custom_call" | custom-call | tf_op jit(solution)/shard_map/wave_back/pallas_call | solution.py:348
  406.8 25.8 %collect_packed.1 = bf16[32,1920,128]{2,1,0:T(8,128)(2,1)} custom-call(s32[7680]{0:T(1024)} %reshape.55.order_ref, bf16[768,2304]{1,0:T(8,128)(2,1)} %get-tuple-element.84.refs_0_, bf16[768,768]{1,0:T(8,128)(2,1)} %get-tuple-element.85.refs_1_, bf16[768,3072]{1,0:T(8,128)(2,1)} %get-tuple-element.86.refs_2_, bf16[3072,768]{1,0:T(8,128)(2,1)} %get-tuple-element.87.refs_3_, ...), custom_call_target="tpu_custom_call" | custom-call | tf_op jit(solution)/shard_map/collect_packed/pallas_call | solution.py:213
  432.7 95.7 %reduce_packed.1 = f32[1920,128]{1,0:T(8,128)} custom-call(bf16[2,2,4,2,1920,128]{5,4,3,2,1,0:T(8,128)(2,1)} %bitcast.10), custom_call_target="tpu_custom_call" | custom-call | tf_op jit(solution)/shard_map/reduce_packed/pallas_call | solution.py:941
  528.4 3.7 multiply_subtract_fusion
  532.7 1.7 copy.23
  (41 shorter events, 4.1 us)
Async XLA Ops:
  7.2 5.4 copy-start
  7.2 150.1 %all-gather.2.cloned.1.call-start = ((), (), s32[]{:S(2)}) async-start(), calls=%async_computation | async-start | bytes 7864320 | tf_op jit(solution)/shard_map/all_gather | solution.py:1383
  12.6 1.3 copy-start.2
  13.9 84.4 %copy-start.3 = (bf16[1,100,8192]{2,1,0:T(8,128)(2,1)S(1)}, bf16[1,100,8192]{2,1,0:T(8,128)(2,1)}, u32[]{:S(2)}) copy-start(bf16[1,100,8192]{2,1,0:T(8,128)(2,1)} %slice.6) | copy-start | bytes 4915204
  13.9 85.2 %copy-start.10 = (s32[1,32]{1,0:T(1,128)S(1)}, s32[1,32]{1,0:T(1,128)}, u32[]{:S(2)}) copy-start(s32[1,32]{1,0:T(1,128)} %param.12) | copy-start | bytes 388
  13.9 89.7 %copy-start.8 = (s32[4,32]{1,0:T(4,128)S(1)}, s32[4,32]{1,0:T(4,128)}, u32[]{:S(2)}) copy-start(s32[4,32]{1,0:T(4,128)} %param.13) | copy-start | bytes 1540
  13.9 89.8 %copy-start.7 = (s32[7520]{0:T(1024)S(1)}, s32[7520]{0:T(1024)}, u32[]{:S(2)}) copy-start(s32[7520]{0:T(1024)} %param.14) | copy-start | bytes 90244
  98.3 65.4 %collective-permute-start.1 = (bf16[1,100,8192]{2,1,0:T(8,128)(2,1)S(1)}, bf16[1,100,8192]{2,1,0:T(8,128)(2,1)S(1)}, u32[]{:S(2)}, u32[]{:S(2)}) collective-permute-start(bf16[1,100,8192]{2,1,0:T(8,128)(2,1)S(1)} %copy-done.3), channel_id=1, source_target_pairs={{0,0},{1,1},{2,2},{3,3},{4,8},{5,9},{6,10},{7,11},{8,4},{9,5},{10,... | collective-permute-start | bytes 4915208 | tf_op jit(solution)/shard_map/ppermute | solution.py:985
  99.1 42.1 %collective-permute-start = (f32[1,32]{1,0:T(1,128)S(1)}, f32[1,32]{1,0:T(1,128)S(1)}, u32[]{:S(2)}, u32[]{:S(2)}) collective-permute-start(f32[1,32]{1,0:T(1,128)S(1)} %convert_element_type.17), channel_id=1, source_target_pairs={{0,0},{1,1},{2,2},{3,3},{4,8},{5,9},{6,10},{7,11},{8,4},{9,5},{10,... | collective-permute-start | bytes 392 | tf_op jit(solution)/shard_map/ppermute | solution.py:985
  99.8 148.4 %collective-permute-start.2 = (bf16[196,768]{1,0:T(8,128)(2,1)}, bf16[196,768]{1,0:T(8,128)(2,1)}, u32[]{:S(2)}, u32[]{:S(2)}) collective-permute-start(bf16[196,768]{1,0:T(8,128)(2,1)} %param.21), channel_id=1, source_target_pairs={{0,0},{1,1},{2,2},{3,3},{4,8},{5,9},{6,10},{7,11},{8,4},{9,5},{10,... | collective-permute-start | bytes 903176 | tf_op jit(solution)/shard_map/ppermute | solution.py:985
  163.7 1.2 copy-start.4
  295.8 87.2 %copy-start.9 = (bf16[196,768]{1,0:T(8,128)(2,1)S(1)}, bf16[196,768]{1,0:T(8,128)(2,1)}, u32[]{:S(2)}) copy-start(bf16[196,768]{1,0:T(8,128)(2,1)} %get-tuple-element.82) | copy-start | bytes 903172
  380.4 151.6 %collective-permute-start.4 = (bf16[1,196,8192]{2,1,0:T(8,128)(2,1)}, bf16[1,196,8192]{2,1,0:T(8,128)(2,1)S(1)}, u32[]{:S(2)}, u32[]{:S(2)}) collective-permute-start(bf16[1,196,8192]{2,1,0:T(8,128)(2,1)} %get-tuple-element.83), channel_id=1, source_target_pairs={{0,0},{1,1},{2,2},{3,3},{4,8},{5,9},{6,10},{7,11},{8,4},{9,5},{10,... | collective-permute-start | bytes 9633800 | tf_op jit(solution)/shard_map/ppermute | solution.py:985
  383.0 149.0 %collective-permute-start.3 = (bf16[196,768]{1,0:T(8,128)(2,1)S(1)}, bf16[196,768]{1,0:T(8,128)(2,1)S(1)}, u32[]{:S(2)}, u32[]{:S(2)}) collective-permute-start(bf16[196,768]{1,0:T(8,128)(2,1)S(1)} %copy-done.9), channel_id=1, source_target_pairs={{0,0},{1,1},{2,2},{3,3},{4,8},{5,9},{6,10},{7,11},{8,4},{9,5},{10,... | collective-permute-start | bytes 903176 | tf_op jit(solution)/shard_map/ppermute | solution.py:985
  432.6 95.7 %copy-start.1 = (f32[1880,128]{1,0:T(8,128)S(1)}, f32[1880,128]{1,0:T(8,128)}, u32[]{:S(2)}) copy-start(f32[1880,128]{1,0:T(8,128)} %param.15) | copy-start | bytes 2887684
  432.6 95.7 %copy-start.5 = (f32[1880,128]{1,0:T(8,128)S(1)}, f32[1880,128]{1,0:T(8,128)}, u32[]{:S(2)}) copy-start(f32[1880,128]{1,0:T(8,128)} %param.16) | copy-start | bytes 2887684
  432.6 95.7 %copy-start.6 = (f32[1880,128]{1,0:T(8,128)S(1)}, f32[1880,128]{1,0:T(8,128)}, u32[]{:S(2)}) copy-start(f32[1880,128]{1,0:T(8,128)} %param.17) | copy-start | bytes 2887684
Sparse Core Ops, SparseCore 0:
  98.4 58.7 all-gather.1

commit v2 on v1

--- a/solution.py
+++ b/solution.py
@@ -570,11 +570,16 @@
     return 16 if count % 16 == 0 else count
 
 
-def make_kernel(shaped_ref, master_ref, kernel_ref, turned):
+def make_kernel(paired, shaped_ref, *refs):
+    slabs, kernel_ref, master, turned = refs[:-3], refs[-3], refs[-2], refs[-1]
     dims = kernel_ref.shape[0]
-    shaped = shaped_ref[pl.ds(pl.multiple_of(lax.axis_index("group") * NB, NB), NB), :]
+    group = lax.axis_index("group")
+    shaped = shaped_ref[pl.ds(pl.multiple_of(group * NB, NB), NB), :]
+    for j, slab in enumerate(slabs):
+        owner = (group + 2 * (j // 2)) % 4 + (j % 2) * (1 - 2 * (group % 2)) if paired else j
+        master[pl.ds(pl.multiple_of(owner * slab.shape[0], slab.shape[0]), slab.shape[0]), :] = slab[...]
     for dim in range(dims):
-        part = dot_nn(shaped, master_ref[:, dim * PATCH : (dim + 1) * PATCH])
+        part = dot_nn(shaped, master[:, dim * PATCH : (dim + 1) * PATCH])
         turned[pl.ds(dim, NB, stride=dims), :] = part[:, :128]
         turned[pl.ds(NB * dims + dim, NB, stride=dims), :] = part[:, 128:]
     for band in range(NB):
@@ -584,22 +589,23 @@
             kernel_ref[:, lane : lane + 128] = turned[row : row + dims, :].astype(kernel_ref.dtype)
 
 
-def make_kernels(shaped, master):
-    dims = master.shape[1] // PATCH
+def make_kernels(shaped, slabs, paired):
+    dims = slabs[0].shape[1] // PATCH
     step = dims_step(dims)
     return pl.pallas_call(
-        make_kernel,
+        functools.partial(make_kernel, paired),
         out_shape=jax.ShapeDtypeStruct((dims, NB * PATCH), jnp.bfloat16),
         grid=(dims // step,),
-        in_specs=[
-            pl.BlockSpec(shaped.shape, lambda j: (0, 0)),
-            pl.BlockSpec((E, step * PATCH), lambda j: (0, j)),
+        in_specs=[pl.BlockSpec(shaped.shape, lambda j: (0, 0))]
+        + [pl.BlockSpec((slab.shape[0], step * PATCH), lambda j: (0, j)) for slab in slabs],
+        out_specs=pl.BlockSpec((step, NB * PATCH), lambda j: (j, 0)),
+        scratch_shapes=[
+            pltpu.VMEM((E, step * PATCH), jnp.bfloat16),
+            pltpu.VMEM((2 * NB * step, 128), jnp.float32),
         ],
-        out_specs=pl.BlockSpec((step, NB * PATCH), lambda j: (j, 0)),
-        scratch_shapes=[pltpu.VMEM((2 * NB * step, 128), jnp.float32)],
         compiler_params=pltpu.CompilerParams(vmem_limit_bytes=60 << 20),
         name="make_kernels",
-    )(shaped, master)
+    )(shaped, *slabs)
 
 
 def embed_kernel(pixel_ref, mask_ref, kernel_ref, stream_ref):
@@ -974,6 +980,10 @@
     return y, c, z, x, low, side, along, twin, partner, moved
 
 
+def swap_group(value, flip):
+    return lax.ppermute(value, "group", [(j, j ^ flip) for j in range(4)])
+
+
 def swap_images(value):
     pairs = []
     for y in range(2):
@@ -1173,42 +1183,48 @@
     return shared.reshape(8 * dims, width), masked, stream
 
 
-def fold_kernel(part_ref, all_ref, own, twin_in, relay_in, side_in, along_in, load_sem, keep_sem, twin_send, twin_recv, relay_send, relay_recv,
-                side_send, side_recv, along_send, along_recv, swap_send, swap_recv, group_send, group_recv, give_send, give_recv):
+def fold_kernel(masked_ref, mask_ref, low_ref, kernel_ref, all_ref, back_ref,
+                gone, own, twin_in, relay_in, side_in, along_in, tiles, backs, tile_sem, back_sem, keep_sem, twin_send, twin_recv,
+                relay_send, relay_recv, side_send, side_recv, along_send, along_recv, swap_send, swap_recv,
+                group_send, group_recv, give_send, give_recv):
     f32, bf16 = jnp.float32, jnp.bfloat16
     y, c, z, x, low, side, along, twin, partner, moved = quad_peers()
     over = place(1 - y, c, z, x)
-    count = all_ref.shape[2] // CHUNK
+    dims, width = all_ref.shape[2], all_ref.shape[3]
+    count = dims // CHUNK
+    seq = back_ref.shape[1]
+    lane = tiles.shape[2]
 
     def cut(k):
         return pl.ds(k * CHUNK, CHUNK)
 
-    def part(core, j, k):
-        return part_ref.at[2 * core + (low + j // 2) % 2, (x + j % 2) % 2, cut(k)]
-
-    def load(j, k):
-        return pltpu.make_async_copy(part(c, j, k), own.at[j, cut(k)], load_sem.at[j, k])
-
-    def swap(j, k):
-        return remote(part(1 - c, j, k), twin_in.at[j, cut(k)], twin_send.at[j, k], twin_recv.at[j, k], twin)
+    def spot_of(j):
+        return (low + j // 2) % 2, (x + j % 2) % 2
+
+    def mine(j, k):
+        a, b = spot_of(j)
+        return own.at[a, b, cut(k)]
+
+    def swap(k):
+        return remote(gone.at[:, :, cut(k)], twin_in.at[:, :, cut(k)], twin_send.at[k], twin_recv.at[k], twin)
 
     def relay(k):
-        return remote(own.at[3, cut(k)], relay_in.at[cut(k)], relay_send.at[k], relay_recv.at[k], along if over_x(k) else side)
+        return remote(mine(3, k), relay_in.at[cut(k)], relay_send.at[k], relay_recv.at[k], along if over_x(k) else side)
 
     def to_side(k):
-        return remote(own.at[1, cut(k)], side_in.at[cut(k)], side_send.at[k], side_recv.at[k], side)
+        return remote(mine(1, k), side_in.at[cut(k)], side_send.at[k], side_recv.at[k], side)
 
     def to_along(k):
-        return remote(own.at[2, cut(k)], along_in.at[cut(k)], along_send.at[k], along_recv.at[k], along)
+        return remote(mine(2, k), along_in.at[cut(k)], along_send.at[k], along_recv.at[k], along)
 
     def keep(k):
-        return pltpu.make_async_copy(own.at[0, cut(k)], all_ref.at[y, c, cut(k)], keep_sem.at[k])
+        return pltpu.make_async_copy(mine(0, k), all_ref.at[y, c, cut(k)], keep_sem.at[k])
 
     def move(k):
-        return remote(own.at[0, cut(k)], all_ref.at[y, 1 - c, cut(k)], swap_send.at[k], swap_recv.at[k], partner)
+        return remote(mine(0, k), all_ref.at[y, 1 - c, cut(k)], swap_send.at[k], swap_recv.at[k], partner)
 
     def moved_in(k):
-        return remote(own.at[0, cut(k)], all_ref.at[y, c, cut(k)], swap_send.at[k], swap_recv.at[k], partner)
+        return remote(mine(0, k), all_ref.at[y, c, cut(k)], swap_send.at[k], swap_recv.at[k], partner)
 
     def cross(k):
         return remote(all_ref.at[y, c, cut(k)], all_ref.at[y, c, cut(k)], group_send.at[k], group_recv.at[k], over)
@@ -1224,41 +1240,69 @@
         here = all_ref.at[(y + j) % 2, 1 - c, cut(k)]
         return remote(here, here, give_send.at[j, k], give_recv.at[j, k], twin)
 
+    def fetch(j):
+        return pltpu.make_async_copy(kernel_ref.at[:, pl.ds(j * lane, lane)], tiles.at[j % 2], tile_sem.at[j % 2])
+
+    def drain(j):
+        return pltpu.make_async_copy(backs.at[j % 2], back_ref.at[0, :, pl.ds(j * lane, lane)], back_sem.at[j % 2])
+
+    def half(core, out):
+        chosen = low_ref[:, pl.ds(pl.multiple_of(core * 4 * dims, 128), 4 * dims)]
+
+        def some(j, carry):
+            lanes = pl.ds(pl.multiple_of(j * 1024, 1024), 1024)
+            part = dot_tn(chosen, masked_ref[:, lanes]).astype(bf16)
+            out[:, :, :, lanes] = part.reshape(2, 2, dims, 1024)
+            return carry
+
+        lax.fori_loop(0, width // 1024, some, 0)
+
+    def pixels_back(j):
+        fetch(j).wait()
+        if j >= 2:
+            drain(j - 2).wait()
+        part = dot_nn(low_ref[...], tiles[j % 2])[0:seq] * mask_ref[:, j * lane : (j + 1) * lane]
+        backs[j % 2] = part.astype(bf16)
+        drain(j).start()
+        if (j + 2) * lane < width:
+            fetch(j + 2).start()
+
     def pair(j, k):
-        load(j, k).wait()
-        swap(j, k).wait_recv()
-        return own[j, cut(k)].astype(f32) + twin_in[j, cut(k)].astype(f32)
-
+        a, b = spot_of(j)
+        return own[a, b, cut(k)].astype(f32) + twin_in[a, b, cut(k)].astype(f32)
+
+    def put(j, k, value):
+        a, b = spot_of(j)
+        own[a, b, cut(k)] = value.astype(bf16)
+
+    fetch(0).start()
+    fetch(1).start()
+    greet([side, along, twin, partner, over])
+    half(1 - c, gone)
     for k in range(count):
-        for j in (3, 1, 2, 0):
-            load(j, k).start()
-    greet([side, along, twin, partner, over])
-    for k in range(count):
-        for j in (3, 1, 2, 0):
-            swap(j, k).start()
+        swap(k).start()
+    half(c, own)
 
     for step in range(count + 4):
         k = step
         if k < count:
-            own[3, cut(k)] = pair(3, k).astype(bf16)
+            swap(k).wait_recv()
+            put(3, k, pair(3, k))
             relay(k).start()
         k = step - 1
         if 0 <= k < count:
             first, second = (to_along, to_side) if over_x(k) else (to_side, to_along)
             plain, summed = (2, 1) if over_x(k) else (1, 2)
-            own[plain, cut(k)] = pair(plain, k).astype(bf16)
+            put(plain, k, pair(plain, k))
             first(k).start()
-            held = pair(summed, k)
             relay(k).wait_recv()
-            own[summed, cut(k)] = (held + relay_in[cut(k)].astype(f32)).astype(bf16)
+            put(summed, k, pair(summed, k) + relay_in[cut(k)].astype(f32))
             second(k).start()
         k = step - 2
         if 0 <= k < count:
-            held = pair(0, k)
             to_side(k).wait_recv()
             to_along(k).wait_recv()
-            held += side_in[cut(k)].astype(f32) + along_in[cut(k)].astype(f32)
-            own[0, cut(k)] = held.astype(bf16)
+            put(0, k, pair(0, k) + side_in[cut(k)].astype(f32) + along_in[cut(k)].astype(f32))
 
             @pl.when(moved)
             def _(k=k):
@@ -1285,15 +1329,18 @@
         if 0 <= k < count:
             crossed(k).wait_recv()
             give(1, k).start()
+        if step * lane < width:
+            pixels_back(step)
 
     @pl.when(moved)
     def _():
         for k in range(count):
             move(k).wait_send()
 
+    for j in (width // lane - 2, width // lane - 1):
+        drain(j).wait()
     for k in range(count):
-        for j in range(4):
-            swap(j, k).wait_send()
+        swap(k).wait_send()
         relay(k).wait_send()
         to_side(k).wait_send()
         to_along(k).wait_send()
@@ -1303,34 +1350,40 @@
             given(j, k).wait_recv()
 
 
-def fold_kernels(part):
-    width = part.shape[1]
-    dims = part.shape[0] // 8
+def fold_kernels(masked, mask, low, kernels, seq):
+    width = masked.shape[1]
+    dims = kernels.shape[0] // 8
     count = dims // CHUNK
     bf16 = jnp.bfloat16
     dma = pltpu.SemaphoreType.DMA
-    folded = pl.pallas_call(
+    vmem, far = pl.BlockSpec(memory_space=pltpu.VMEM), pl.BlockSpec(memory_space=pl.ANY)
+    folded, back = pl.pallas_call(
         fold_kernel,
-        out_shape=jax.ShapeDtypeStruct((2, 2, dims, width), bf16),
-        in_specs=[pl.BlockSpec(memory_space=pl.ANY)],
-        out_specs=pl.BlockSpec(memory_space=pl.ANY),
+        out_shape=[
+            jax.ShapeDtypeStruct((2, 2, dims, width), bf16),
+            jax.ShapeDtypeStruct((1, seq, width), bf16),
+        ],
+        in_specs=[vmem, vmem, vmem, far],
+        out_specs=[far, far],
         scratch_shapes=[
-            pltpu.VMEM((4, dims, width), bf16),
-            pltpu.VMEM((4, dims, width), bf16),
+            pltpu.VMEM((2, 2, dims, width), bf16),
+            pltpu.VMEM((2, 2, dims, width), bf16),
+            pltpu.VMEM((2, 2, dims, width), bf16),
             pltpu.VMEM((dims, width), bf16),
             pltpu.VMEM((dims, width), bf16),
             pltpu.VMEM((dims, width), bf16),
-            dma((4, count)),
+            pltpu.VMEM((2, 8 * dims, 1024), bf16),
+            pltpu.VMEM((2, seq, 1024), bf16),
+            dma((2,)),
+            dma((2,)),
             dma((count,)),
-            dma((4, count)),
-            dma((4, count)),
         ]
-        + [dma((count,))] * 10
+        + [dma((count,))] * 12
         + [dma((2, count))] * 2,
         compiler_params=pltpu.CompilerParams(collective_id=3, has_side_effects=True, vmem_limit_bytes=60 << 20),
         name="fold_kernels",
-    )(part.reshape(4, 2, dims, width))
-    return folded.reshape(4, dims, width)
+    )(masked, mask, low, kernels)
+    return folded.reshape(4, dims, width), back
 
 
 def on_device(
@@ -1364,6 +1417,7 @@
         gathered, rest, cotangent, low_weight = lax.optimization_barrier(
             (gathered, pixels[:, HEAD:], cotangent, low_weight)
         )
+        across = swap_group(low_weight, 2)
         rest, cotangent = swap_images(rest), swap_images(cotangent)
     else:
         gathered = lax.all_gather(rest_low, ("group", "img"), axis=0, tiled=True)
@@ -1376,12 +1430,17 @@
         constant_values=total_blocks,
     ).reshape(-1)
     unpacked = spread_packed(gathered, slots, total_blocks)
+    if fits:
+        *unpacked, across = lax.optimization_barrier((*unpacked, across))
+        slabs = [low_weight, swap_group(low_weight, 1), across, swap_group(across, 1)]
+    else:
+        master = lax.all_gather(low_weight, "group", axis=0, tiled=False)
+        slabs = [master[j] for j in range(groups)]
     block_mats, wave_mats = unpacked[:4], unpacked[4:10]
     block_vectors, wave_vectors = unpacked[10:]
     embedded = embed_waves(wavelength).reshape(groups * NB, E)
     shaped_low, own_shaped, kept, slope = wave_layer(embedded, wave_mats, wave_vectors)
-    master = lax.all_gather(low_weight, "group", axis=0, tiled=True)
-    kernel_low = make_kernels(shaped_low, master)
+    kernel_low = make_kernels(shaped_low, slabs, fits)
     mask = jnp.repeat(mask, PATCH, axis=1)
     if fits:
         kernel_all, masked, stream = share_kernels(kernel_low, mask, pixels, head, rest)
@@ -1392,12 +1451,12 @@
     block_out, grad_low, block_vectors, *block_grads = block_pass(
         stream, cotangent, block_vectors, *block_mats
     )
-    pixel_grad, kernel_grad = unembed_patches(masked, mask, kernel_all, grad_low, pixels.shape[1])
     if fits:
-        all_groups = fold_kernels(kernel_grad)
+        all_groups, pixel_grad = fold_kernels(masked, mask, grad_low, kernel_all, pixels.shape[1])
         all_groups, block_out, pixel_grad = lax.optimization_barrier((all_groups, block_out, pixel_grad))
         block_out, pixel_grad = swap_images(block_out), swap_images(pixel_grad)
     else:
+        pixel_grad, kernel_grad = unembed_patches(masked, mask, kernel_all, grad_low, pixels.shape[1])
         kernel_grad_low = lax.psum_scatter(kernel_grad, "img", scatter_dimension=0, tiled=True)
         all_groups = lax.all_gather(kernel_grad_low[None], "group", axis=0, tiled=True)
     fc_new, fc_first, fc_second, shaped_part = master_update(

time: 550 us -> 529 us (0.962)
  starting transfers between devices: 8.55 us -> 25.9 us
  waiting for transfers between devices: 15.4 us -> 0.02 us
  between operations: 14.5 us -> 1.1 us
  Pallas kernels: 486 us -> 480 us
    ppermute x0 -> x3, starting transfers between devices: none -> 16.3 us  [swap_group(): return lax.ppermute(value, 'group', [(j, j ^ flip) for j in range(4)])]
    all_gather x1 -> x0, waiting for transfers between devices: 15.4 us -> none  [on_device(): master = lax.all_gather(low_weight, 'group', axis=0, tiled=True)]
    pallas_call x3 -> x2, Pallas kernels: 107 us -> 98.7 us  [the longest x1 92.1 us: fold_kernels(): pl.pallas_call(fold_kernel, out_shape=[jax.ShapeDtypeStruct((2, 2, dims,...]
  transfers between devices with their start and end apart: 6 -> 8, of which waited for: 1 -> 0; matrix products, arithmetic and copies ran while one was open for 1% -> 1% of each run, Pallas kernels for 50% -> 52%
where the time goes in v2:
time: 529 us; the launch traced here: 521 us
  Pallas kernels  480 us (91%)
  starting transfers between devices  25.9 us (5%)
  other arithmetic  9.29 us (2%)
    pallas_call x1, Pallas kernels, reduce_packed(): pl.pallas_call(reduce_kernel, out_shape=jax.ShapeDtypeStruct((rows, 128),...  94.1 us
    pallas_call x1, Pallas kernels, fold_kernels(): pl.pallas_call(fold_kernel, out_shape=[jax.ShapeDtypeStruct((2, 2, dims,...  92.1 us
    pallas_call x1, Pallas kernels, share_kernels(): pl.pallas_call(share_kernel, out_shape=[jax.ShapeDtypeStruct((4, 2, dims,...  87.2 us
    pallas_call x1, Pallas kernels, gather_packed(): pl.pallas_call(gather_kernel, out_shape=[jax.ShapeDtypeStruct((2, 2, 4, 2...  83.5 us
    pallas_call x1, Pallas kernels, block_pass(): pl.pallas_call(block_kernel, out_shape=[jax.ShapeDtypeStruct((seq, D), bf...  31.5 us
    pallas_call x1, Pallas kernels, spread_packed(): pl.pallas_call(spread_kernel, out_shape=big + small, grid_spec=pltpu.Pref...  27.3 us
    pallas_call x1, Pallas kernels, collect_packed(): pl.pallas_call(collect_kernel, out_shape=jax.ShapeDtypeStruct((shards, ro...  25.8 us
    ppermute x3, starting transfers between devices, swap_group(): return lax.ppermute(value, 'group', [(j, j ^ flip) for j in range(4)])  16.3 us
  transfers between devices with their start and end apart: 8, of which 0 were waited for; matrix products, arithmetic and copies ran while one was open for 1% of the time, Pallas kernels for 52%

profile of v2, /device:TPU:0, one launch (start us, length us, event | category | flops | bytes accessed | tf_op | source)
XLA Modules:
  0.0 521.0 jit_solution(9054056528545360244)
XLA Ops:
  0.6 1.4 convert_element_type.15
  2.0 3.2 convert_element_type.16.refs_0_
  5.4 0.8 pad.9.own_ref
  6.2 83.5 %gather_packed.1 = (bf16[2,2,4,2,1920,128]{5,4,3,2,1,0:T(8,128)(2,1)}, bf16[1,96,8192]{2,1,0:T(8,128)(2,1)}) custom-call(bf16[1920,128]{1,0:T(8,128)(2,1)} %pad.9.own_ref, bf16[1,196,8192]{2,1,0:T(8,128)(2,1)} %pixel_ref.3), custom_call_target="tpu_custom_call" | custom-call | tf_op jit(solution)/shard_map/gather_packed/pallas_call | solution.py:849
  89.8 1.0 collective-permute-start
  90.8 1.9 collective-permute-start.4
  92.6 15.2 %collective-permute-start.1 = (bf16[32,24576]{1,0:T(8,128)(2,1)S(1)}, bf16[32,24576]{1,0:T(8,128)(2,1)}, u32[]{:S(2)}, u32[]{:S(2)}) collective-permute-start(bf16[32,24576]{1,0:T(8,128)(2,1)S(1)} %copy-done.1), channel_id=1, source_target_pairs={{0,8},{8,0},{16,24},{24,16},{1,9},{9,1},{17,25},{25,17},{2,10},{10... | collective-permute-start | bytes 4718600 | tf_op jit(solution)/shard_map/ppermute | solution.py:984
  108.0 0.7 reshape.52.order_ref
  108.7 27.3 %spread_packed.1 = (bf16[768,2304]{1,0:T(8,128)(2,1)}, bf16[768,768]{1,0:T(8,128)(2,1)}, bf16[768,3072]{1,0:T(8,128)(2,1)}, bf16[3072,768]{1,0:T(8,128)(2,1)}, f...) custom-call(s32[7680]{0:T(1024)} %reshape.52.order_ref, ...), custom_call_target="tpu_custom_call" | custom-call | tf_op jit(solution)/shard_map/spread_packed/pallas_call | solution.py:145
  136.9 3.8 collective-permute-start.5
  141.1 0.7 pad_maximum_fusion.embed_ref
  142.5 8.3 %wave_layer.1 = (bf16[128,128]{1,0:T(8,128)(2,1)}, bf16[128,32]{1,0:T(8,128)(2,1)}, f32[12,128,128]{2,1,0:T(8,128)}, f32[2,128,2048]{2,1,0:T(8,128)}) custom-call(f32[128,128]{1,0:T(8,128)} %pad_maximum_fusion.embed_ref, f32[128,128]{1,0:T(8,128)} %get-tuple-element.84.wq_ref, f32[128,128]{1,0:T(8,128)} %get-tuple-element.85.wk_ref, ...), custom_call_target="tpu_custom_call" | custom-call | tf_op jit(solution)/shard_map/wave_layer/pallas_call | solution.py:294
  150.9 6.6 %make_kernels.1.made_ref = bf16[96,8192]{1,0:T(8,128)(2,1)} custom-call(bf16[128,128]{1,0:T(8,128)(2,1)} %get-tuple-element.91.shaped_ref, bf16[32,24576]{1,0:T(8,128)(2,1)} %convert_element_type.16.refs_0_, bf16[32,24576]{1,0:T(8,128)(2,1)} %collective-permute-done.1.refs_1_, bf16[32,24576]{1,0:T(8,128)(2,1)} %collective-permute-done.refs_2_, ...), custom_call_target="tpu_custom_call" | custom-call | tf_op jit(solution)/shard_map/make_kernels/pallas_call | solution.py:595
  157.5 87.2 %share_kernels.1 = (bf16[4,2,96,8192]{3,2,1,0:T(8,128)(2,1)}, bf16[208,8192]{1,0:T(8,128)(2,1)}, f32[196,768]{1,0:T(8,128)}) custom-call(bf16[96,8192]{1,0:T(8,128)(2,1)} %make_kernels.1.made_ref, f32[1,8192]{1,0:T(1,128)} %bitcast.13, bf16[1,196,8192]{2,1,0:T(8,128)(2,1)} %pixel_ref.3, bf16[1,96,8192]{2,1,0:T(8,128)(2,1)} %get-tuple-element.93.head_ref, ...), custom_call_target="tpu_custom_call" | custom-call | tf_op jit(solution)/shard_map/share_kernels/pallas_call | solution.py:1160
  244.7 31.5 %block_pass.1 = (bf16[196,768]{1,0:T(8,128)(2,1)}, bf16[208,768]{1,0:T(8,128)(2,1)}, f32[8,768]{1,0:T(8,128)}, bf16[768,2304]{1,0:T(8,128)(2,1)}, bf16[768,768]{...) custom-call(f32[196,768]{1,0:T(8,128)} %get-tuple-element.96.stream_ref, ...), custom_call_target="tpu_custom_call" | custom-call | flops 8400000000 | bytes 30000000 | tf_op jit(solution)/shard_map/block_pass/pallas_call | solution.py:521
  276.2 92.1 %fold_kernels.1 = (bf16[2,2,96,8192]{3,2,1,0:T(8,128)(2,1)}, bf16[1,196,8192]{2,1,0:T(8,128)(2,1)}) custom-call(bf16[208,8192]{1,0:T(8,128)(2,1)} %get-tuple-element.95.masked_ref, f32[1,8192]{1,0:T(1,128)} %bitcast.14, bf16[208,768]{1,0:T(8,128)(2,1)} %get-tuple-element.103.low_ref, bf16[768,8192]{1,0:T(8,128)(2,1)} %bitcast.11), custom_call_target="tpu_custom_call" | custom-call | tf_op jit(solution)/shard_map/fold_kernels/pallas_call | solution.py:1360
  368.3 2.6 collective-permute-start.7
  371.6 13.3 %master_update.1 = (f32[32,24576]{1,0:T(8,128)}, f32[32,24576]{1,0:T(8,128)}, f32[32,24576]{1,0:T(8,128)}, f32[128,32]{1,0:T(8,128)}) custom-call(bf16[4,96,8192]{2,1,0:T(8,128)(2,1)} %bitcast.12, bf16[128,32]{1,0:T(8,128)(2,1)} %get-tuple-element.115.shaped_ref, f32[32,24576]{1,0:T(8,128)} %weight_ref.1, f32[32,24576]{1,0:T(8,128)} %one_ref.1, ...), custom_call_target="tpu_custom_call" | custom-call | tf_op jit(solution)/shard_map/master_update/pallas_call | solution.py:709
  384.9 9.8 %wave_back.1 = (f32[128,128]{1,0:T(8,128)}, f32[128,128]{1,0:T(8,128)}, f32[128,128]{1,0:T(8,128)}, f32[128,128]{1,0:T(8,128)}, f32[128,2048]{1,0:T(8,128)}, /*index=5*/f32[2048,128]{1,0:T(8,128)}, f32[8,128]{1,0:T(8,128)}) custom-call(f32[128,32]{1,0:T(8,128)} %get-tuple-element.116.part_ref, f32[128,128]{1,0:T(8,128)} %pad_maximum_fusion.embed_ref, ...), custom_call_target="tpu_custom_call" | custom-call | tf_op jit(solution)/shard_map/wave_back/pallas_call | solution.py:348
  394.7 25.8 %collect_packed.1 = bf16[32,1920,128]{2,1,0:T(8,128)(2,1)} custom-call(s32[7680]{0:T(1024)} %reshape.52.order_ref, bf16[768,2304]{1,0:T(8,128)(2,1)} %get-tuple-element.110.refs_0_, bf16[768,768]{1,0:T(8,128)(2,1)} %get-tuple-element.111.refs_1_, bf16[768,3072]{1,0:T(8,128)(2,1)} %get-tuple-element.112.refs_2_, ...), custom_call_target="tpu_custom_call" | custom-call | tf_op jit(solution)/shard_map/collect_packed/pallas_call | solution.py:213
  420.6 94.1 %reduce_packed.1 = f32[1920,128]{1,0:T(8,128)} custom-call(bf16[2,2,4,2,1920,128]{5,4,3,2,1,0:T(8,128)(2,1)} %bitcast.9), custom_call_target="tpu_custom_call" | custom-call | tf_op jit(solution)/shard_map/reduce_packed/pallas_call | solution.py:947
  514.7 3.7 multiply_subtract_fusion
  518.4 0.7 copy.22
  519.1 1.7 copy.23
  (39 shorter events, 2.9 us)
Async XLA Ops:
  0.6 4.6 copy-start
  5.4 84.4 %copy-start.1 = (bf16[32,24576]{1,0:T(8,128)(2,1)S(1)}, bf16[32,24576]{1,0:T(8,128)(2,1)}, u32[]{:S(2)}) copy-start(bf16[32,24576]{1,0:T(8,128)(2,1)} %convert_element_type.16.refs_0_) | copy-start | bytes 4718596
  5.4 102.5 %copy-start.5 = (s32[7520]{0:T(1024)S(1)}, s32[7520]{0:T(1024)}, u32[]{:S(2)}) copy-start(s32[7520]{0:T(1024)} %param.14) | copy-start | bytes 90244
  89.8 46.3 %collective-permute-start = (bf16[32,24576]{1,0:T(8,128)(2,1)S(1)}, bf16[32,24576]{1,0:T(8,128)(2,1)}, u32[]{:S(2)}, u32[]{:S(2)}) collective-permute-start(bf16[32,24576]{1,0:T(8,128)(2,1)S(1)} %copy-done.1), channel_id=1, source_target_pairs={{0,16},{8,24},{16,0},{24,8},{1,17},{9,25},{17,1},{25,9},{2,18},{10... | collective-permute-start | bytes 4718600 | tf_op jit(solution)/shard_map/ppermute | solution.py:984
  90.8 66.7 %collective-permute-start.4 = (bf16[1,100,8192]{2,1,0:T(8,128)(2,1)S(1)}, bf16[1,100,8192]{2,1,0:T(8,128)(2,1)}, u32[]{:S(2)}, u32[]{:S(2)}) collective-permute-start(bf16[1,100,8192]{2,1,0:T(8,128)(2,1)S(1)} %slice.6), channel_id=1, source_target_pairs={{0,0},{1,1},{2,2},{3,3},{4,8},{5,9},{6,10},{7,11},{8,4},{9,5},{10,... | collective-permute-start | bytes 4915208 | tf_op jit(solution)/shard_map/ppermute | solution.py:995
  92.6 58.2 %collective-permute-start.1 = (bf16[32,24576]{1,0:T(8,128)(2,1)S(1)}, bf16[32,24576]{1,0:T(8,128)(2,1)}, u32[]{:S(2)}, u32[]{:S(2)}) collective-permute-start(bf16[32,24576]{1,0:T(8,128)(2,1)S(1)} %copy-done.1), channel_id=1, source_target_pairs={{0,8},{8,0},{16,24},{24,16},{1,9},{9,1},{17,25},{25,17},{2,10},{10... | collective-permute-start | bytes 4718600 | tf_op jit(solution)/shard_map/ppermute | solution.py:984
  108.7 27.4 %copy-start.8 = (s32[1,32]{1,0:T(1,128)S(1)}, s32[1,32]{1,0:T(1,128)}, u32[]{:S(2)}) copy-start(s32[1,32]{1,0:T(1,128)} %param.12) | copy-start | bytes 388
  108.7 31.9 %copy-start.6 = (s32[4,32]{1,0:T(4,128)S(1)}, s32[4,32]{1,0:T(4,128)}, u32[]{:S(2)}) copy-start(s32[4,32]{1,0:T(4,128)} %param.13) | copy-start | bytes 1540
  136.1 14.8 %collective-permute-start.2 = (bf16[32,24576]{1,0:T(8,128)(2,1)}, bf16[32,24576]{1,0:T(8,128)(2,1)}, u32[]{:S(2)}, u32[]{:S(2)}) collective-permute-start(bf16[32,24576]{1,0:T(8,128)(2,1)} %collective-permute-done.refs_2_), channel_id=1, source_target_pairs={{0,8},{8,0},{16,24},{24,16},{1,9},{9,1},{17,25},{25,17},{2,10},{10... | collective-permute-start | bytes 4718600 | tf_op jit(solution)/shard_map/ppermute | solution.py:984
  136.2 5.6 %collective-permute-start.3 = (f32[1,32]{1,0:T(1,128)S(1)}, f32[1,32]{1,0:T(1,128)S(1)}, u32[]{:S(2)}, u32[]{:S(2)}) collective-permute-start(f32[1,32]{1,0:T(1,128)S(1)} %convert_element_type.17), channel_id=1, source_target_pairs={{0,0},{1,1},{2,2},{3,3},{4,8},{5,9},{6,10},{7,11},{8,4},{9,5},{10,... | collective-permute-start | bytes 392 | tf_op jit(solution)/shard_map/ppermute | solution.py:995
  136.9 107.8 %collective-permute-start.5 = (bf16[196,768]{1,0:T(8,128)(2,1)}, bf16[196,768]{1,0:T(8,128)(2,1)}, u32[]{:S(2)}, u32[]{:S(2)}) collective-permute-start(bf16[196,768]{1,0:T(8,128)(2,1)} %param.21), channel_id=1, source_target_pairs={{0,0},{1,1},{2,2},{3,3},{4,8},{5,9},{6,10},{7,11},{8,4},{9,5},{10,... | collective-permute-start | bytes 903176 | tf_op jit(solution)/shard_map/ppermute | solution.py:995
  276.2 94.7 %copy-start.7 = (bf16[196,768]{1,0:T(8,128)(2,1)S(1)}, bf16[196,768]{1,0:T(8,128)(2,1)}, u32[]{:S(2)}) copy-start(bf16[196,768]{1,0:T(8,128)(2,1)} %get-tuple-element.108) | copy-start | bytes 903172
  368.3 150.0 %collective-permute-start.7 = (bf16[1,196,8192]{2,1,0:T(8,128)(2,1)}, bf16[1,196,8192]{2,1,0:T(8,128)(2,1)S(1)}, u32[]{:S(2)}, u32[]{:S(2)}) collective-permute-start(bf16[1,196,8192]{2,1,0:T(8,128)(2,1)} %get-tuple-element.109), channel_id=1, source_target_pairs={{0,0},{1,1},{2,2},{3,3},{4,8},{5,9},{6,10},{7,11},{8,4},{9,5},{10,... | collective-permute-start | bytes 9633800 | tf_op jit(solution)/shard_map/ppermute | solution.py:995
  370.9 147.5 %collective-permute-start.6 = (bf16[196,768]{1,0:T(8,128)(2,1)S(1)}, bf16[196,768]{1,0:T(8,128)(2,1)S(1)}, u32[]{:S(2)}, u32[]{:S(2)}) collective-permute-start(bf16[196,768]{1,0:T(8,128)(2,1)S(1)} %copy-done.7), channel_id=1, source_target_pairs={{0,0},{1,1},{2,2},{3,3},{4,8},{5,9},{6,10},{7,11},{8,4},{9,5},{10,... | collective-permute-start | bytes 903176 | tf_op jit(solution)/shard_map/ppermute | solution.py:995
  420.5 94.1 %copy-start.2 = (f32[1880,128]{1,0:T(8,128)S(1)}, f32[1880,128]{1,0:T(8,128)}, u32[]{:S(2)}) copy-start(f32[1880,128]{1,0:T(8,128)} %param.15) | copy-start | bytes 2887684
  420.6 94.1 %copy-start.3 = (f32[1880,128]{1,0:T(8,128)S(1)}, f32[1880,128]{1,0:T(8,128)}, u32[]{:S(2)}) copy-start(f32[1880,128]{1,0:T(8,128)} %param.16) | copy-start | bytes 2887684
  420.6 94.1 %copy-start.4 = (f32[1880,128]{1,0:T(8,128)S(1)}, f32[1880,128]{1,0:T(8,128)}, u32[]{:S(2)}) copy-start(f32[1880,128]{1,0:T(8,128)} %param.17) | copy-start | bytes 2887684

commit v3 on v2

--- a/solution.py
+++ b/solution.py
@@ -227,9 +227,9 @@
     )(slots, *grads)
 
 
-def exact(a, b, left, right):
+def finer(a, b, left, right):
     return lax.dot_general(
-        a, b, (((left,), (right,)), ((), ())), precision=lax.Precision.HIGHEST, preferred_element_type=jnp.float32
+        a, b, (((left,), (right,)), ((), ())), precision=lax.Precision.HIGH, preferred_element_type=jnp.float32
     )
 
 
@@ -250,28 +250,28 @@
     rows = embed_ref.shape[0]
     groups = rows // NB
     embedded = embed_ref[...]
-    queries = exact(embedded, wq_ref[...], 1, 0)
-    keys = exact(embedded, wk_ref[...], 1, 0)
-    values = exact(embedded, wv_ref[...], 1, 0)
+    queries = finer(embedded, wq_ref[...], 1, 0)
+    keys = finer(embedded, wk_ref[...], 1, 0)
+    values = finer(embedded, wv_ref[...], 1, 0)
     size = E // HH
     across = lax.broadcasted_iota(jnp.int32, (rows, rows), 0) // NB == lax.broadcasted_iota(jnp.int32, (rows, rows), 1) // NB
     mixed = []
     for head in range(HH):
         lanes = slice(head * size, head * size + size)
-        scores = exact(queries[:, lanes], keys[:, lanes], 1, 1) * size**-0.5
+        scores = finer(queries[:, lanes], keys[:, lanes], 1, 1) * size**-0.5
         scores = jnp.where(across, scores, -1e30)
         weight = jnp.exp(scores - jnp.max(scores, axis=-1, keepdims=True))
         weight = weight / jnp.sum(weight, axis=-1, keepdims=True)
         kept_ref[head] = weight
-        mixed.append(exact(weight, values[:, lanes], 1, 0))
+        mixed.append(finer(weight, values[:, lanes], 1, 0))
     mixed = jnp.concatenate(mixed, axis=1)
-    unit_one, scale_one = unit_scale(embedded + exact(mixed, wo_ref[...], 1, 0))
+    unit_one, scale_one = unit_scale(embedded + finer(mixed, wo_ref[...], 1, 0))
     first = unit_one * vec_ref[0:1, :] + vec_ref[1:2, :]
-    inner = exact(first, win_ref[...], 1, 0)
+    inner = finer(first, win_ref[...], 1, 0)
     half = 0.5 * (1.0 + lax.erf(inner * 0.5**0.5))
     slope_ref[0] = inner * half
     slope_ref[1] = half + inner * jnp.exp(-0.5 * inner * inner) * (2.0 * math.pi) ** -0.5
-    unit_two, scale_two = unit_scale(first + exact(inner * half, wout_ref[...], 1, 0))
+    unit_two, scale_two = unit_scale(first + finer(inner * half, wout_ref[...], 1, 0))
     shaped = (unit_two * vec_ref[2:3, :] + vec_ref[3:4, :] + embedded).astype(jnp.bfloat16)
     for j, part in enumerate((queries, keys, values, mixed, unit_one, unit_two)):
         kept_ref[HH + j] = part
@@ -320,27 +320,27 @@
     gvec_ref[2:3, :] = jnp.sum(grad * unit_two, axis=0, keepdims=True)
     gvec_ref[3:4, :] = jnp.sum(grad, axis=0, keepdims=True)
     grad = unit_back(grad, unit_two, scale_two, vec_ref[2:3, :])
-    gout_ref[...] = exact(slope_ref[0], grad, 0, 0)
-    inner = exact(grad, wout_ref[...], 1, 1) * slope_ref[1]
+    gout_ref[...] = finer(slope_ref[0], grad, 0, 0)
+    inner = finer(grad, wout_ref[...], 1, 1) * slope_ref[1]
     first = unit_one * vec_ref[0:1, :] + vec_ref[1:2, :]
-    gin_ref[...] = exact(first, inner, 0, 0)
-    grad = grad + exact(inner, win_ref[...], 1, 1)
+    gin_ref[...] = finer(first, inner, 0, 0)
+    grad = grad + finer(inner, win_ref[...], 1, 1)
     gvec_ref[0:1, :] = jnp.sum(grad * unit_one, axis=0, keepdims=True)
     gvec_ref[1:2, :] = jnp.sum(grad, axis=0, keepdims=True)
     grad = unit_back(grad, unit_one, scale_one, vec_ref[0:1, :])
-    go_ref[...] = exact(mixed, grad, 0, 0)
-    grad = exact(grad, wo_ref[...], 1, 1)
+    go_ref[...] = finer(mixed, grad, 0, 0)
+    grad = finer(grad, wo_ref[...], 1, 1)
     parts = [[], [], []]
     for head in range(HH):
         lanes = slice(head * size, head * size + size)
         weight = kept_ref[head]
-        grad_weight = exact(grad[:, lanes], values[:, lanes], 1, 1)
-        parts[2].append(exact(weight, grad[:, lanes], 0, 0))
+        grad_weight = finer(grad[:, lanes], values[:, lanes], 1, 1)
+        parts[2].append(finer(weight, grad[:, lanes], 0, 0))
         score = weight * (grad_weight - jnp.sum(weight * grad_weight, axis=-1, keepdims=True)) * size**-0.5
-        parts[0].append(exact(score, keys[:, lanes], 1, 0))
-        parts[1].append(exact(score, queries[:, lanes], 0, 0))
+        parts[0].append(finer(score, keys[:, lanes], 1, 0))
+        parts[1].append(finer(score, queries[:, lanes], 0, 0))
     for out, part in zip((gq_ref, gk_ref, gv_ref), parts):
-        out[...] = exact(embedded, jnp.concatenate(part, axis=1), 0, 0)
+        out[...] = finer(embedded, jnp.concatenate(part, axis=1), 0, 0)
 
 
 def wave_back(part, embedded, kept, slope, mats, vectors):
@@ -570,14 +570,8 @@
     return 16 if count % 16 == 0 else count
 
 
-def make_kernel(paired, shaped_ref, *refs):
-    slabs, kernel_ref, master, turned = refs[:-3], refs[-3], refs[-2], refs[-1]
-    dims = kernel_ref.shape[0]
-    group = lax.axis_index("group")
-    shaped = shaped_ref[pl.ds(pl.multiple_of(group * NB, NB), NB), :]
-    for j, slab in enumerate(slabs):
-        owner = (group + 2 * (j // 2)) % 4 + (j % 2) * (1 - 2 * (group % 2)) if paired else j
-        master[pl.ds(pl.multiple_of(owner * slab.shape[0], slab.shape[0]), slab.shape[0]), :] = slab[...]
+def spread_bands(shaped, master, turned, out):
+    dims = out.shape[0]
     for dim in range(dims):
         part = dot_nn(shaped, master[:, dim * PATCH : (dim + 1) * PATCH])
         turned[pl.ds(dim, NB, stride=dims), :] = part[:, :128]
@@ -586,26 +580,33 @@
         for half in range(2):
             row = half * NB * dims + band * dims
             lane = band * PATCH + half * 128
-            kernel_ref[:, lane : lane + 128] = turned[row : row + dims, :].astype(kernel_ref.dtype)
-
-
-def make_kernels(shaped, slabs, paired):
-    dims = slabs[0].shape[1] // PATCH
+            out[:, lane : lane + 128] = turned[row : row + dims, :].astype(out.dtype)
+
+
+def own_bands(shaped_ref):
+    return shaped_ref[pl.ds(pl.multiple_of(lax.axis_index("group") * NB, NB), NB), :]
+
+
+def make_kernel(shaped_ref, master_ref, kernel_ref, turned):
+    spread_bands(own_bands(shaped_ref), master_ref, turned, kernel_ref)
+
+
+def make_kernels(shaped, master):
+    dims = master.shape[1] // PATCH
     step = dims_step(dims)
     return pl.pallas_call(
-        functools.partial(make_kernel, paired),
+        make_kernel,
         out_shape=jax.ShapeDtypeStruct((dims, NB * PATCH), jnp.bfloat16),
         grid=(dims // step,),
-        in_specs=[pl.BlockSpec(shaped.shape, lambda j: (0, 0))]
-        + [pl.BlockSpec((slab.shape[0], step * PATCH), lambda j: (0, j)) for slab in slabs],
+        in_specs=[
+            pl.BlockSpec(shaped.shape, lambda j: (0, 0)),
+            pl.BlockSpec((E, step * PATCH), lambda j: (0, j)),
+        ],
         out_specs=pl.BlockSpec((step, NB * PATCH), lambda j: (j, 0)),
-        scratch_shapes=[
-            pltpu.VMEM((E, step * PATCH), jnp.bfloat16),
-            pltpu.VMEM((2 * NB * step, 128), jnp.float32),
-        ],
+        scratch_shapes=[pltpu.VMEM((2 * NB * step, 128), jnp.float32)],
         compiler_params=pltpu.CompilerParams(vmem_limit_bytes=60 << 20),
         name="make_kernels",
-    )(shaped, *slabs)
+    )(shaped, master)
 
 
 def embed_kernel(pixel_ref, mask_ref, kernel_ref, stream_ref):
@@ -755,7 +756,7 @@
     )
 
 
-def gather_kernel(own_ref, pixel_ref, all_ref, head_ref, head_sem, local_sem, line_send, line_recv, group_send, group_recv, twin_send, twin_recv):
+def gather_kernel(rest_ref, pixel_ref, weight_ref, all_ref, head_ref, low_ref, own_ref, wide, narrow, weight_sem, head_sem, local_sem, line_send, line_recv, group_send, group_recv, twin_send, twin_recv):
     y, c, z, x = spot()
     (x2, y2), (x3, y3), around, second, third, twin = partners()
     partner = place(y, 1 - c, (z + 2) % 4, x)
@@ -796,6 +797,16 @@
         part = all_ref.at[yy, 1 - c, :, xx, cut(k)]
         return remote(part, part, twin_send.at[0, k], twin_recv.at[landing, k], twin)
 
+    fetch = pltpu.make_async_copy(weight_ref, wide, weight_sem.at[0])
+    store = pltpu.make_async_copy(narrow, low_ref, weight_sem.at[1])
+    fetch.start()
+    even = rest_ref.shape[0] // 16 * 16
+    own_ref[0:even, :] = rest_ref[0:even, :].astype(jnp.bfloat16)
+    if even < own_ref.shape[0]:
+        left = rest_ref.shape[0] - even
+        parts = [rest_ref[even:, :]] if left else []
+        parts.append(jnp.zeros((own_ref.shape[0] - even - left, 128), jnp.float32))
+        own_ref[even:, :] = jnp.concatenate(parts, axis=0).astype(jnp.bfloat16)
     keep = pltpu.make_async_copy(own_ref, all_ref.at[y, c, z, x], local_sem)
     keep.start()
     greet(around + [second, third, twin, partner])
@@ -811,6 +822,10 @@
             hop(0, third, k, 0, 2).start()
             hop(0, second, k, 1, 1).start()
             share(0, k).start()
+        if step == 3:
+            fetch.wait()
+            narrow[...] = wide[...].astype(jnp.bfloat16)
+            store.start()
         if step == NC - 3:
 
             @pl.when(moved)
@@ -838,26 +853,35 @@
             share(j, k).wait_send()
             share_in(j, k).wait_recv()
 
+    store.wait()
+
     @pl.when(moved)
     def _():
         head.wait()
 
 
-def gather_packed(own, pixels):
-    rows = own.shape[0]
+def gather_packed(own, pixels, weight, rows):
+    bf16 = jnp.bfloat16
     dma = pltpu.SemaphoreType.DMA
     return pl.pallas_call(
         gather_kernel,
         out_shape=[
-            jax.ShapeDtypeStruct((2, 2, 4, 2, rows, 128), own.dtype),
+            jax.ShapeDtypeStruct((2, 2, 4, 2, rows, 128), bf16),
             jax.ShapeDtypeStruct((1, HEAD, pixels.shape[2]), pixels.dtype),
+            jax.ShapeDtypeStruct(weight.shape, bf16),
         ],
-        in_specs=[pl.BlockSpec(memory_space=pltpu.VMEM), pl.BlockSpec(memory_space=pl.ANY)],
-        out_specs=[pl.BlockSpec(memory_space=pl.ANY)] * 2,
-        scratch_shapes=[dma((2,)), dma, dma((3, NC)), dma((3, NC)), dma((3, NC)), dma((4, NC)), dma((4, NC)), dma((4, NC))],
+        in_specs=[pl.BlockSpec(memory_space=pltpu.VMEM)] + [pl.BlockSpec(memory_space=pl.ANY)] * 2,
+        out_specs=[pl.BlockSpec(memory_space=pl.ANY)] * 3,
+        scratch_shapes=[
+            pltpu.VMEM((rows, 128), bf16),
+            pltpu.VMEM(weight.shape, jnp.float32),
+            pltpu.VMEM(weight.shape, bf16),
+            dma((2,)),
+            dma((2,)),
+            dma, dma((3, NC)), dma((3, NC)), dma((3, NC)), dma((4, NC)), dma((4, NC)), dma((4, NC))],
         compiler_params=pltpu.CompilerParams(collective_id=0, has_side_effects=True, vmem_limit_bytes=60 << 20),
         name="gather_packed",
-    )(own, pixels)
+    )(own, pixels, weight)
 
 
 def reduce_kernel(part_ref, sum_ref, own, twin_in, third_in, second_in, line_in, load_sem, twin_send, twin_recv, third_send, third_recv, second_send, second_recv, line_send, line_recv):
@@ -995,8 +1019,8 @@
     return lax.ppermute(value, ("group", "img"), pairs)
 
 
-def share_kernel(made_ref, mask_ref, pixel_ref, head_ref, rest_ref, all_ref, masked_ref, stream_ref,
-                 held, top, bottom, tile, mixed, order, pixel_sem, store_sem, keep_sem, swap_send, swap_recv,
+def share_kernel(shaped_ref, mask_ref, own_slab, twin_slab, over_slab, far_slab, pixel_ref, head_ref, rest_ref,
+                 all_ref, masked_ref, stream_ref, made_ref, master, turned, held, top, bottom, tile, mixed, order, slab_sem, pixel_sem, store_sem, keep_sem, swap_send, swap_recv,
                  side_send, side_recv, along_send, along_recv, far_send, far_recv, twin_send, twin_recv):
     f32, bf16 = jnp.float32, jnp.bfloat16
     y, c, z, x, low, side, along, twin, partner, moved = quad_peers()
@@ -1044,6 +1068,31 @@
     def given(j, k):
         return remote(block(1 - c, j, k), block(1 - c, j, k), twin_send.at[j, k], twin_recv.at[j, k], twin)
 
+    def slabs(k):
+        lanes = pl.ds(k * CHUNK * PATCH, CHUNK * PATCH)
+        copies = []
+        for j, slab in enumerate((own_slab, twin_slab, over_slab, far_slab)):
+            owner = (y + j // 2) % 2 * 2 + (c + j % 2) % 2
+            place_rows = pl.ds(pl.multiple_of(owner * slab.shape[0], slab.shape[0]), slab.shape[0])
+            copies.append(pltpu.make_async_copy(slab.at[:, lanes], master.at[k % 2, place_rows], slab_sem.at[k % 2, j]))
+        return copies
+
+    def make(k):
+        for copy in slabs(k):
+            copy.wait()
+        spread_bands(own_bands(shaped_ref), master.at[k % 2], turned, made_ref.at[cut(k)])
+        if k + 2 < count:
+            for copy in slabs(k + 2):
+                copy.start()
+
+        @pl.when(moved)
+        def _():
+            swap(k).start()
+
+        @pl.when(jnp.logical_not(moved))
+        def _():
+            keep(k).start()
+
     def store(k):
         return pltpu.make_async_copy(held.at[:, :, cut(k)], all_ref.at[:, :, cut(k)], store_sem.at[k])
 
@@ -1051,20 +1100,21 @@
     owned = pltpu.make_async_copy(pixel_ref.at[0, pl.ds(0, HEAD)], top, pixel_sem.at[0])
     lower = pltpu.make_async_copy(rest_ref.at[0], bottom, pixel_sem.at[1])
 
+    for k in (0, 1):
+        for copy in slabs(k):
+            copy.start()
+
     @pl.when(jnp.logical_not(moved))
     def _():
         owned.start()
-        for k in range(count):
-            keep(k).start()
-
-    lower.start()
-    greet([side, along, twin, partner])
 
     @pl.when(moved)
     def _():
         swapped.start()
-        for k in range(count):
-            swap(k).start()
+
+    lower.start()
+    greet([side, along, twin, partner])
+    make(0)
 
     def mask_pixels(part):
         @pl.when(part == 0)
@@ -1105,9 +1155,11 @@
             to_side(k).start()
             to_along(k).start()
             give(0, k).start()
-        if step < 2:
-            mask_pixels(step)
-        elif step == 2:
+        if step + 1 < count:
+            make(step + 1)
+        if step in (1, 2):
+            mask_pixels(step - 1)
+        elif step == 3:
             make_order()
         k = step - 1
         if 0 <= k < count:
@@ -1133,7 +1185,7 @@
             part = held[:, :, cut(k), :].reshape(group, width)
             mixed[:, k * group : (k + 1) * group] = dot_nt(masked_ref[...], part)
 
-    stream_ref[...] = exact(mixed[...], order[...], 1, 0)[0 : stream_ref.shape[0]]
+    stream_ref[...] = finer(mixed[...], order[...], 1, 0)[0 : stream_ref.shape[0]]
 
     @pl.when(moved)
     def _():
@@ -1149,8 +1201,9 @@
             give(j, k).wait_send()
 
 
-def share_kernels(made, mask, pixels, head, rest):
-    dims, width = made.shape
+def share_kernels(shaped, mask, slabs, pixels, head, rest):
+    dims, width = slabs[0].shape[1] // PATCH, mask.shape[1]
+    bf16 = jnp.bfloat16
     count = dims // CHUNK
     seq = pixels.shape[1]
     rows = tall(seq)
@@ -1160,26 +1213,30 @@
     shared, masked, stream = pl.pallas_call(
         share_kernel,
         out_shape=[
-            jax.ShapeDtypeStruct((4, 2, dims, width), made.dtype),
-            jax.ShapeDtypeStruct((rows, width), made.dtype),
+            jax.ShapeDtypeStruct((4, 2, dims, width), bf16),
+            jax.ShapeDtypeStruct((rows, width), bf16),
             jax.ShapeDtypeStruct((seq, 8 * dims), f32),
         ],
-        in_specs=[vmem, vmem, far, far, far],
+        in_specs=[vmem, vmem] + [far] * 7,
         out_specs=[far, vmem, vmem],
         scratch_shapes=[
-            pltpu.VMEM((4, 2, dims, width), made.dtype),
-            pltpu.VMEM((HEAD, width), made.dtype),
-            pltpu.VMEM((seq - HEAD, width), made.dtype),
+            pltpu.VMEM((dims, width), bf16),
+            pltpu.VMEM((2, E, CHUNK * PATCH), bf16),
+            pltpu.VMEM((2 * NB * CHUNK, 128), f32),
+            pltpu.VMEM((4, 2, dims, width), bf16),
+            pltpu.VMEM((HEAD, width), bf16),
+            pltpu.VMEM((seq - HEAD, width), bf16),
             pltpu.VMEM((rows - HEAD, 1024), f32),
             pltpu.VMEM((rows, 8 * dims), f32),
             pltpu.VMEM((8 * dims, 8 * dims), f32),
+            dma((2, 4)),
             dma((2,)),
         ]
         + [dma((count,))] * 10
         + [dma((4, count))] * 2,
         compiler_params=pltpu.CompilerParams(collective_id=2, has_side_effects=True, vmem_limit_bytes=60 << 20),
         name="share_kernels",
-    )(made, mask, pixels, head, rest)
+    )(shaped, mask, *slabs, pixels, head, rest)
     return shared.reshape(8 * dims, width), masked, stream
 
 
@@ -1329,8 +1386,8 @@
         if 0 <= k < count:
             crossed(k).wait_recv()
             give(1, k).start()
-        if step * lane < width:
-            pixels_back(step)
+        if step >= 2 and (step - 2) * lane < width:
+            pixels_back(step - 2)
 
     @pl.when(moved)
     def _():
@@ -1409,17 +1466,17 @@
     extra = -own_rows % 128
     slot_blocks = (own_rows + extra) // 8
     mask = band_mask.astype(f32)
-    low_weight = fc_weight.astype(bf16)
-    rest_low = jnp.pad(rest_weight.astype(bf16), ((0, extra), (0, 0)))
     if fits:
         mask = swap_images(mask)
-        gathered, head = gather_packed(rest_low, pixels)
+        gathered, head, low_weight = gather_packed(rest_weight, pixels, fc_weight, own_rows + extra)
         gathered, rest, cotangent, low_weight = lax.optimization_barrier(
             (gathered, pixels[:, HEAD:], cotangent, low_weight)
         )
         across = swap_group(low_weight, 2)
         rest, cotangent = swap_images(rest), swap_images(cotangent)
     else:
+        low_weight = fc_weight.astype(bf16)
+        rest_low = jnp.pad(rest_weight.astype(bf16), ((0, extra), (0, 0)))
         gathered = lax.all_gather(rest_low, ("group", "img"), axis=0, tiled=True)
     shards = gathered.size // ((own_rows + extra) * 128)
     gathered = gathered.reshape(shards, own_rows + extra, 128)
@@ -1434,17 +1491,16 @@
         *unpacked, across = lax.optimization_barrier((*unpacked, across))
         slabs = [low_weight, swap_group(low_weight, 1), across, swap_group(across, 1)]
     else:
-        master = lax.all_gather(low_weight, "group", axis=0, tiled=False)
-        slabs = [master[j] for j in range(groups)]
+        master = lax.all_gather(low_weight, "group", axis=0, tiled=True)
     block_mats, wave_mats = unpacked[:4], unpacked[4:10]
     block_vectors, wave_vectors = unpacked[10:]
     embedded = embed_waves(wavelength).reshape(groups * NB, E)
     shaped_low, own_shaped, kept, slope = wave_layer(embedded, wave_mats, wave_vectors)
-    kernel_low = make_kernels(shaped_low, slabs, fits)
     mask = jnp.repeat(mask, PATCH, axis=1)
     if fits:
-        kernel_all, masked, stream = share_kernels(kernel_low, mask, pixels, head, rest)
+        kernel_all, masked, stream = share_kernels(shaped_low, mask, slabs, pixels, head, rest)
     else:
+        kernel_low = make_kernels(shaped_low, master)
         kernel_all = lax.all_gather(kernel_low, "img", axis=0, tiled=True)
         stream = embed_patches(pixels, mask, kernel_all)
         masked = jnp.pad((pixels[0] * mask).astype(bf16), ((0, tall(pixels.shape[1]) - pixels.shape[1]), (0, 0)))

time: 529 us -> 521 us (0.985)
  Pallas kernels: 480 us -> 474 us
    pallas_call x1 -> x0, Pallas kernels: 6.59 us -> none  [make_kernels(): pl.pallas_call(functools.partial(make_kernel, paired), out_shape=jax.Shap...]
where the time goes in v3:
time: 521 us; the launch traced here: 513 us
  Pallas kernels  474 us (91%)
  starting transfers between devices  25.9 us (5%)
  local copies, waits for them, and re-layouts  6.84 us (1%)
    pallas_call x1, Pallas kernels, reduce_packed(): pl.pallas_call(reduce_kernel, out_shape=jax.ShapeDtypeStruct((rows, 128),...  96.2 us
    pallas_call x1, Pallas kernels, fold_kernels(): pl.pallas_call(fold_kernel, out_shape=[jax.ShapeDtypeStruct((2, 2, dims,...  93 us
    pallas_call x1, Pallas kernels, share_kernels(): pl.pallas_call(share_kernel, out_shape=[jax.ShapeDtypeStruct((4, 2, dims,...  89.3 us
    pallas_call x1, Pallas kernels, gather_packed(): pl.pallas_call(gather_kernel, out_shape=[jax.ShapeDtypeStruct((2, 2, 4, 2...  83.8 us
    pallas_call x1, Pallas kernels, block_pass(): pl.pallas_call(block_kernel, out_shape=[jax.ShapeDtypeStruct((seq, D), bf...  31.1 us
    pallas_call x1, Pallas kernels, spread_packed(): pl.pallas_call(spread_kernel, out_shape=big + small, grid_spec=pltpu.Pref...  27.3 us
    pallas_call x1, Pallas kernels, collect_packed(): pl.pallas_call(collect_kernel, out_shape=jax.ShapeDtypeStruct((shards, ro...  25.8 us
    ppermute x3, starting transfers between devices, swap_group(): return lax.ppermute(value, 'group', [(j, j ^ flip) for j in range(4)])  17.4 us
  transfers between devices with their start and end apart: 8, of which 0 were waited for; matrix products, arithmetic and copies ran while one was open for 1% of the time, Pallas kernels for 52%

profile of v3, /device:TPU:0, one launch (start us, length us, event | category | flops | bytes accessed | tf_op | source)
XLA Modules:
  0.0 512.6 jit_solution(7806423029926064364)
XLA Ops:
  0.6 1.6 slice.6
  2.2 83.8 %gather_packed.1 = (bf16[2,2,4,2,1920,128]{5,4,3,2,1,0:T(8,128)(2,1)}, bf16[1,96,8192]{2,1,0:T(8,128)(2,1)}, bf16[32,24576]{1,0:T(8,128)(2,1)}) custom-call(f32[1880,128]{1,0:T(8,128)} %rest_ref.1, bf16[1,196,8192]{2,1,0:T(8,128)(2,1)} %pixel_ref.3, f32[32,24576]{1,0:T(8,128)} %weight_ref.3), custom_call_target="tpu_custom_call" | custom-call | tf_op jit(solution)/shard_map/gather_packed/pallas_call | solution.py:866
  86.1 1.0 collective-permute-start
  87.1 0.8 collective-permute-start.4
  87.8 16.3 %collective-permute-start.2 = (bf16[32,24576]{1,0:T(8,128)(2,1)}, bf16[32,24576]{1,0:T(8,128)(2,1)}, u32[]{:S(2)}, u32[]{:S(2)}) collective-permute-start(bf16[32,24576]{1,0:T(8,128)(2,1)} %get-tuple-element.85.own_slab), channel_id=1, source_target_pairs={{0,8},{8,0},{16,24},{24,16},{1,9},{9,1},{17,25},{25,17},{2,10},{10... | collective-permute-start | bytes 4718600 | tf_op jit(solution)/shard_map/ppermute | solution.py:1008
  104.3 0.7 reshape.52.order_ref
  105.0 27.3 %spread_packed.1 = (bf16[768,2304]{1,0:T(8,128)(2,1)}, bf16[768,768]{1,0:T(8,128)(2,1)}, bf16[768,3072]{1,0:T(8,128)(2,1)}, bf16[3072,768]{1,0:T(8,128)(2,1)}, f...) custom-call(s32[7680]{0:T(1024)} %reshape.52.order_ref, ...), custom_call_target="tpu_custom_call" | custom-call | tf_op jit(solution)/shard_map/spread_packed/pallas_call | solution.py:145
  132.4 0.7 collective-permute-start.1
  133.1 3.8 collective-permute-start.5
  137.3 0.7 pad_maximum_fusion.embed_ref
  138.8 6.7 %wave_layer.1 = (bf16[128,128]{1,0:T(8,128)(2,1)}, bf16[128,32]{1,0:T(8,128)(2,1)}, f32[12,128,128]{2,1,0:T(8,128)}, f32[2,128,2048]{2,1,0:T(8,128)}) custom-call(f32[128,128]{1,0:T(8,128)} %pad_maximum_fusion.embed_ref, f32[128,128]{1,0:T(8,128)} %get-tuple-element.86.wq_ref, f32[128,128]{1,0:T(8,128)} %get-tuple-element.87.wk_ref, ...), custom_call_target="tpu_custom_call" | custom-call | tf_op jit(solution)/shard_map/wave_layer/pallas_call | solution.py:294
  145.6 1.2 copy-done.1
  146.7 89.3 %share_kernels.1 = (bf16[4,2,96,8192]{3,2,1,0:T(8,128)(2,1)}, bf16[208,8192]{1,0:T(8,128)(2,1)}, f32[196,768]{1,0:T(8,128)}) custom-call(bf16[128,128]{1,0:T(8,128)(2,1)} %get-tuple-element.93.shaped_ref, f32[1,8192]{1,0:T(1,128)} %bitcast.13, bf16[32,24576]{1,0:T(8,128)(2,1)} %get-tuple-element.85.own_slab, ...), custom_call_target="tpu_custom_call" | custom-call | tf_op jit(solution)/shard_map/share_kernels/pallas_call | solution.py:1213
  236.1 31.1 %block_pass.1 = (bf16[196,768]{1,0:T(8,128)(2,1)}, bf16[208,768]{1,0:T(8,128)(2,1)}, f32[8,768]{1,0:T(8,128)}, bf16[768,2304]{1,0:T(8,128)(2,1)}, bf16[768,768]{...) custom-call(f32[196,768]{1,0:T(8,128)} %get-tuple-element.98.stream_ref, ...), custom_call_target="tpu_custom_call" | custom-call | flops 8400000000 | bytes 30000000 | tf_op jit(solution)/shard_map/block_pass/pallas_call | solution.py:521
  267.2 93.0 %fold_kernels.1 = (bf16[2,2,96,8192]{3,2,1,0:T(8,128)(2,1)}, bf16[1,196,8192]{2,1,0:T(8,128)(2,1)}) custom-call(bf16[208,8192]{1,0:T(8,128)(2,1)} %get-tuple-element.97.masked_ref, f32[1,8192]{1,0:T(1,128)} %bitcast.14, bf16[208,768]{1,0:T(8,128)(2,1)} %get-tuple-element.105.low_ref, bf16[768,8192]{1,0:T(8,128)(2,1)} %bitcast.11), custom_call_target="tpu_custom_call" | custom-call | tf_op jit(solution)/shard_map/fold_kernels/pallas_call | solution.py:1417
  360.2 2.6 collective-permute-start.7
  362.8 0.7 collective-permute-start.6
  363.5 13.1 %master_update.1 = (f32[32,24576]{1,0:T(8,128)}, f32[32,24576]{1,0:T(8,128)}, f32[32,24576]{1,0:T(8,128)}, f32[128,32]{1,0:T(8,128)}) custom-call(bf16[4,96,8192]{2,1,0:T(8,128)(2,1)} %bitcast.12, bf16[128,32]{1,0:T(8,128)(2,1)} %get-tuple-element.117.shaped_ref, f32[32,24576]{1,0:T(8,128)} %weight_ref.3, f32[32,24576]{1,0:T(8,128)} %one_ref.1, ...), custom_call_target="tpu_custom_call" | custom-call | tf_op jit(solution)/shard_map/master_update/pallas_call | solution.py:710
  376.6 7.3 %wave_back.1 = (f32[128,128]{1,0:T(8,128)}, f32[128,128]{1,0:T(8,128)}, f32[128,128]{1,0:T(8,128)}, f32[128,128]{1,0:T(8,128)}, f32[128,2048]{1,0:T(8,128)}, /*index=5*/f32[2048,128]{1,0:T(8,128)}, f32[8,128]{1,0:T(8,128)}) custom-call(f32[128,32]{1,0:T(8,128)} %get-tuple-element.118.part_ref, f32[128,128]{1,0:T(8,128)} %pad_maximum_fusion.embed_ref, ...), custom_call_target="tpu_custom_call" | custom-call | tf_op jit(solution)/shard_map/wave_back/pallas_call | solution.py:348
  383.9 25.8 %collect_packed.1 = bf16[32,1920,128]{2,1,0:T(8,128)(2,1)} custom-call(s32[7680]{0:T(1024)} %reshape.52.order_ref, bf16[768,2304]{1,0:T(8,128)(2,1)} %get-tuple-element.112.refs_0_, bf16[768,768]{1,0:T(8,128)(2,1)} %get-tuple-element.113.refs_1_, bf16[768,3072]{1,0:T(8,128)(2,1)} %get-tuple-element.114.refs_2_, ...), custom_call_target="tpu_custom_call" | custom-call | tf_op jit(solution)/shard_map/collect_packed/pallas_call | solution.py:213
  409.8 96.2 %reduce_packed.1 = f32[1920,128]{1,0:T(8,128)} custom-call(bf16[2,2,4,2,1920,128]{5,4,3,2,1,0:T(8,128)(2,1)} %bitcast.9), custom_call_target="tpu_custom_call" | custom-call | tf_op jit(solution)/shard_map/reduce_packed/pallas_call | solution.py:971
  506.0 3.7 multiply_subtract_fusion
  509.7 0.7 copy.22
  510.4 1.7 copy.23
  (33 shorter events, 1.4 us)
Async XLA Ops:
  2.2 101.9 %copy-start.4 = (s32[7520]{0:T(1024)S(1)}, s32[7520]{0:T(1024)}, u32[]{:S(2)}) copy-start(s32[7520]{0:T(1024)} %param.14) | copy-start | bytes 90244
  86.1 46.3 %collective-permute-start = (bf16[32,24576]{1,0:T(8,128)(2,1)}, bf16[32,24576]{1,0:T(8,128)(2,1)}, u32[]{:S(2)}, u32[]{:S(2)}) collective-permute-start(bf16[32,24576]{1,0:T(8,128)(2,1)} %get-tuple-element.85.own_slab), channel_id=1, source_target_pairs={{0,16},{8,24},{16,0},{24,8},{1,17},{9,25},{17,1},{25,9},{2,18},{10... | collective-permute-start | bytes 4718600 | tf_op jit(solution)/shard_map/ppermute | solution.py:1008
  87.1 58.5 %collective-permute-start.4 = (bf16[1,100,8192]{2,1,0:T(8,128)(2,1)S(1)}, bf16[1,100,8192]{2,1,0:T(8,128)(2,1)S(1)}, u32[]{:S(2)}, u32[]{:S(2)}) collective-permute-start(bf16[1,100,8192]{2,1,0:T(8,128)(2,1)S(1)} %slice.6), channel_id=1, source_target_pairs={{0,0},{1,1},{2,2},{3,3},{4,8},{5,9},{6,10},{7,11},{8,4},{9,5},{10,... | collective-permute-start | bytes 4915208 | tf_op jit(solution)/shard_map/ppermute | solution.py:1019
  87.8 57.7 %collective-permute-start.2 = (bf16[32,24576]{1,0:T(8,128)(2,1)}, bf16[32,24576]{1,0:T(8,128)(2,1)}, u32[]{:S(2)}, u32[]{:S(2)}) collective-permute-start(bf16[32,24576]{1,0:T(8,128)(2,1)} %get-tuple-element.85.own_slab), channel_id=1, source_target_pairs={{0,8},{8,0},{16,24},{24,16},{1,9},{9,1},{17,25},{25,17},{2,10},{10... | collective-permute-start | bytes 4718600 | tf_op jit(solution)/shard_map/ppermute | solution.py:1008
  105.0 27.4 %copy-start.7 = (s32[1,32]{1,0:T(1,128)S(1)}, s32[1,32]{1,0:T(1,128)}, u32[]{:S(2)}) copy-start(s32[1,32]{1,0:T(1,128)} %param.12) | copy-start | bytes 388
  105.0 31.9 %copy-start.5 = (s32[4,32]{1,0:T(4,128)S(1)}, s32[4,32]{1,0:T(4,128)}, u32[]{:S(2)}) copy-start(s32[4,32]{1,0:T(4,128)} %param.13) | copy-start | bytes 1540
  132.3 13.2 %collective-permute-start.3 = (bf16[32,24576]{1,0:T(8,128)(2,1)}, bf16[32,24576]{1,0:T(8,128)(2,1)}, u32[]{:S(2)}, u32[]{:S(2)}) collective-permute-start(bf16[32,24576]{1,0:T(8,128)(2,1)} %collective-permute-done.over_slab), channel_id=1, source_target_pairs={{0,8},{8,0},{16,24},{24,16},{1,9},{9,1},{17,25},{25,17},{2,10},{10... | collective-permute-start | bytes 4718600 | tf_op jit(solution)/shard_map/ppermute | solution.py:1008
  132.4 5.6 %collective-permute-start.1 = (f32[1,32]{1,0:T(1,128)S(1)}, f32[1,32]{1,0:T(1,128)S(1)}, u32[]{:S(2)}, u32[]{:S(2)}) collective-permute-start(f32[1,32]{1,0:T(1,128)S(1)} %convert_element_type.7), channel_id=1, source_target_pairs={{0,0},{1,1},{2,2},{3,3},{4,8},{5,9},{6,10},{7,11},{8,4},{9,5},{10,... | collective-permute-start | bytes 392 | tf_op jit(solution)/shard_map/ppermute | solution.py:1019
  133.1 103.0 %collective-permute-start.5 = (bf16[196,768]{1,0:T(8,128)(2,1)}, bf16[196,768]{1,0:T(8,128)(2,1)}, u32[]{:S(2)}, u32[]{:S(2)}) collective-permute-start(bf16[196,768]{1,0:T(8,128)(2,1)} %param.21), channel_id=1, source_target_pairs={{0,0},{1,1},{2,2},{3,3},{4,8},{5,9},{6,10},{7,11},{8,4},{9,5},{10,... | collective-permute-start | bytes 903176 | tf_op jit(solution)/shard_map/ppermute | solution.py:1019
  145.5 1.2 copy-start.1
  267.2 95.6 %copy-start.6 = (bf16[196,768]{1,0:T(8,128)(2,1)S(1)}, bf16[196,768]{1,0:T(8,128)(2,1)}, u32[]{:S(2)}) copy-start(bf16[196,768]{1,0:T(8,128)(2,1)} %get-tuple-element.110) | copy-start | bytes 903172
  360.2 149.5 %collective-permute-start.7 = (bf16[1,196,8192]{2,1,0:T(8,128)(2,1)}, bf16[1,196,8192]{2,1,0:T(8,128)(2,1)S(1)}, u32[]{:S(2)}, u32[]{:S(2)}) collective-permute-start(bf16[1,196,8192]{2,1,0:T(8,128)(2,1)} %get-tuple-element.111), channel_id=1, source_target_pairs={{0,0},{1,1},{2,2},{3,3},{4,8},{5,9},{6,10},{7,11},{8,4},{9,5},{10,... | collective-permute-start | bytes 9633800 | tf_op jit(solution)/shard_map/ppermute | solution.py:1019
  362.8 146.9 %collective-permute-start.6 = (bf16[196,768]{1,0:T(8,128)(2,1)S(1)}, bf16[196,768]{1,0:T(8,128)(2,1)S(1)}, u32[]{:S(2)}, u32[]{:S(2)}) collective-permute-start(bf16[196,768]{1,0:T(8,128)(2,1)S(1)} %copy-done.6), channel_id=1, source_target_pairs={{0,0},{1,1},{2,2},{3,3},{4,8},{5,9},{6,10},{7,11},{8,4},{9,5},{10,... | collective-permute-start | bytes 903176 | tf_op jit(solution)/shard_map/ppermute | solution.py:1019
  409.8 96.2 %copy-start = (f32[1880,128]{1,0:T(8,128)S(1)}, f32[1880,128]{1,0:T(8,128)}, u32[]{:S(2)}) copy-start(f32[1880,128]{1,0:T(8,128)} %rest_ref.1) | copy-start | bytes 2887684
  409.8 96.2 %copy-start.2 = (f32[1880,128]{1,0:T(8,128)S(1)}, f32[1880,128]{1,0:T(8,128)}, u32[]{:S(2)}) copy-start(f32[1880,128]{1,0:T(8,128)} %param.16) | copy-start | bytes 2887684
  409.8 96.2 %copy-start.3 = (f32[1880,128]{1,0:T(8,128)S(1)}, f32[1880,128]{1,0:T(8,128)}, u32[]{:S(2)}) copy-start(f32[1880,128]{1,0:T(8,128)} %param.17) | copy-start | bytes 2887684

commit v4 on v3

--- a/solution.py
+++ b/solution.py
@@ -756,7 +756,7 @@
     )
 
 
-def gather_kernel(rest_ref, pixel_ref, weight_ref, all_ref, head_ref, low_ref, own_ref, wide, narrow, weight_sem, head_sem, local_sem, line_send, line_recv, group_send, group_recv, twin_send, twin_recv):
+def gather_kernel(rest_ref, pixel_ref, weight_ref, up_ref, mask_ref, all_ref, head_ref, low_ref, up_in, mask_in, own_ref, wide, narrow, weight_sem, head_sem, local_sem, line_send, line_recv, group_send, group_recv, twin_send, twin_recv):
     y, c, z, x = spot()
     (x2, y2), (x3, y3), around, second, third, twin = partners()
     partner = place(y, 1 - c, (z + 2) % 4, x)
@@ -767,6 +767,10 @@
         return pl.ds(k * rows, rows)
 
     head = remote(pixel_ref.at[0, pl.ds(0, HEAD)], head_ref.at[0], head_sem.at[0], head_sem.at[1], partner)
+    small = [
+        remote(up_ref, up_in, head_sem.at[2], head_sem.at[3], partner),
+        remote(mask_ref, mask_in, head_sem.at[4], head_sem.at[5], partner),
+    ]
 
     def along(d, k):
         return remote(own_ref.at[cut(k)], all_ref.at[y, c, z, x, cut(k)], line_send.at[d - 1, k], line_recv.at[d - 1, k], around[d - 1])
@@ -826,11 +830,13 @@
             fetch.wait()
             narrow[...] = wide[...].astype(jnp.bfloat16)
             store.start()
-        if step == NC - 3:
+        if step == NC // 2 + 1:
 
             @pl.when(moved)
             def _():
                 head.start()
+                for copy in small:
+                    copy.start()
 
         k = step - 1
         if 0 <= k < NC:
@@ -858,9 +864,11 @@
     @pl.when(moved)
     def _():
         head.wait()
-
-
-def gather_packed(own, pixels, weight, rows):
+        for copy in small:
+            copy.wait()
+
+
+def gather_packed(own, pixels, weight, upstream, mask, rows):
     bf16 = jnp.bfloat16
     dma = pltpu.SemaphoreType.DMA
     return pl.pallas_call(
@@ -869,19 +877,21 @@
             jax.ShapeDtypeStruct((2, 2, 4, 2, rows, 128), bf16),
             jax.ShapeDtypeStruct((1, HEAD, pixels.shape[2]), pixels.dtype),
             jax.ShapeDtypeStruct(weight.shape, bf16),
+            jax.ShapeDtypeStruct(upstream.shape, upstream.dtype),
+            jax.ShapeDtypeStruct(mask.shape, mask.dtype),
         ],
-        in_specs=[pl.BlockSpec(memory_space=pltpu.VMEM)] + [pl.BlockSpec(memory_space=pl.ANY)] * 2,
-        out_specs=[pl.BlockSpec(memory_space=pl.ANY)] * 3,
+        in_specs=[pl.BlockSpec(memory_space=pltpu.VMEM)] + [pl.BlockSpec(memory_space=pl.ANY)] * 4,
+        out_specs=[pl.BlockSpec(memory_space=pl.ANY)] * 5,
         scratch_shapes=[
             pltpu.VMEM((rows, 128), bf16),
             pltpu.VMEM(weight.shape, jnp.float32),
             pltpu.VMEM(weight.shape, bf16),
             dma((2,)),
-            dma((2,)),
+            dma((6,)),
             dma, dma((3, NC)), dma((3, NC)), dma((3, NC)), dma((4, NC)), dma((4, NC)), dma((4, NC))],
         compiler_params=pltpu.CompilerParams(collective_id=0, has_side_effects=True, vmem_limit_bytes=60 << 20),
         name="gather_packed",
-    )(own, pixels, weight)
+    )(own, pixels, weight, upstream, mask)
 
 
 def reduce_kernel(part_ref, sum_ref, own, twin_in, third_in, second_in, line_in, load_sem, twin_send, twin_recv, third_send, third_recv, second_send, second_recv, line_send, line_recv):
@@ -1019,8 +1029,8 @@
     return lax.ppermute(value, ("group", "img"), pairs)
 
 
-def share_kernel(shaped_ref, mask_ref, own_slab, twin_slab, over_slab, far_slab, pixel_ref, head_ref, rest_ref,
-                 all_ref, masked_ref, stream_ref, made_ref, master, turned, held, top, bottom, tile, mixed, order, slab_sem, pixel_sem, store_sem, keep_sem, swap_send, swap_recv,
+def share_kernel(shaped_ref, mask_ref, own_slab, over_slab, pixel_ref, head_ref, rest_ref,
+                 all_ref, masked_ref, stream_ref, made_ref, master, turned, held, top, bottom, tile, mixed, order, slab_sem, slab_send, slab_recv, pixel_sem, store_sem, keep_sem, swap_send, swap_recv,
                  side_send, side_recv, along_send, along_recv, far_send, far_recv, twin_send, twin_recv):
     f32, bf16 = jnp.float32, jnp.bfloat16
     y, c, z, x, low, side, along, twin, partner, moved = quad_peers()
@@ -1068,22 +1078,29 @@
     def given(j, k):
         return remote(block(1 - c, j, k), block(1 - c, j, k), twin_send.at[j, k], twin_recv.at[j, k], twin)
 
-    def slabs(k):
+    def slab(core, j, k):
+        owner = (y + j) % 2 * 2 + core
+        size = own_slab.shape[0]
+        return master.at[k, pl.ds(pl.multiple_of(owner * size, size), size)]
+
+    def slab_here(j, k):
         lanes = pl.ds(k * CHUNK * PATCH, CHUNK * PATCH)
-        copies = []
-        for j, slab in enumerate((own_slab, twin_slab, over_slab, far_slab)):
-            owner = (y + j // 2) % 2 * 2 + (c + j % 2) % 2
-            place_rows = pl.ds(pl.multiple_of(owner * slab.shape[0], slab.shape[0]), slab.shape[0])
-            copies.append(pltpu.make_async_copy(slab.at[:, lanes], master.at[k % 2, place_rows], slab_sem.at[k % 2, j]))
-        return copies
+        return (own_slab, over_slab)[j].at[:, lanes]
+
+    def load_slab(j, k):
+        return pltpu.make_async_copy(slab_here(j, k), slab(c, j, k), slab_sem.at[j, k])
+
+    def send_slab(j, k):
+        return remote(slab_here(j, k), slab(c, j, k), slab_send.at[j, k], slab_recv.at[j, k], twin)
+
+    def slab_in(j, k):
+        return remote(slab_here(j, k), slab(1 - c, j, k), slab_send.at[j, k], slab_recv.at[j, k], twin)
 
     def make(k):
-        for copy in slabs(k):
-            copy.wait()
-        spread_bands(own_bands(shaped_ref), master.at[k % 2], turned, made_ref.at[cut(k)])
-        if k + 2 < count:
-            for copy in slabs(k + 2):
-                copy.start()
+        for j in range(2):
+            load_slab(j, k).wait()
+            slab_in(j, k).wait_recv()
+        spread_bands(own_bands(shaped_ref), master.at[k], turned, made_ref.at[cut(k)])
 
         @pl.when(moved)
         def _():
@@ -1100,9 +1117,9 @@
     owned = pltpu.make_async_copy(pixel_ref.at[0, pl.ds(0, HEAD)], top, pixel_sem.at[0])
     lower = pltpu.make_async_copy(rest_ref.at[0], bottom, pixel_sem.at[1])
 
-    for k in (0, 1):
-        for copy in slabs(k):
-            copy.start()
+    for k in range(count):
+        for j in range(2):
+            load_slab(j, k).start()
 
     @pl.when(jnp.logical_not(moved))
     def _():
@@ -1114,6 +1131,9 @@
 
     lower.start()
     greet([side, along, twin, partner])
+    for k in range(count):
+        for j in range(2):
+            send_slab(j, k).start()
     make(0)
 
     def mask_pixels(part):
@@ -1197,6 +1217,8 @@
         to_along(k).wait_send()
         pass_on(k).wait_send()
         store(k).wait()
+        for j in range(2):
+            send_slab(j, k).wait_send()
         for j in range(4):
             give(j, k).wait_send()
 
@@ -1217,11 +1239,11 @@
             jax.ShapeDtypeStruct((rows, width), bf16),
             jax.ShapeDtypeStruct((seq, 8 * dims), f32),
         ],
-        in_specs=[vmem, vmem] + [far] * 7,
+        in_specs=[vmem, vmem] + [far] * 5,
         out_specs=[far, vmem, vmem],
         scratch_shapes=[
             pltpu.VMEM((dims, width), bf16),
-            pltpu.VMEM((2, E, CHUNK * PATCH), bf16),
+            pltpu.VMEM((count, E, CHUNK * PATCH), bf16),
             pltpu.VMEM((2 * NB * CHUNK, 128), f32),
             pltpu.VMEM((4, 2, dims, width), bf16),
             pltpu.VMEM((HEAD, width), bf16),
@@ -1229,7 +1251,9 @@
             pltpu.VMEM((rows - HEAD, 1024), f32),
             pltpu.VMEM((rows, 8 * dims), f32),
             pltpu.VMEM((8 * dims, 8 * dims), f32),
-            dma((2, 4)),
+            dma((2, count)),
+            dma((2, count)),
+            dma((2, count)),
             dma((2,)),
         ]
         + [dma((count,))] * 10
@@ -1240,8 +1264,8 @@
     return shared.reshape(8 * dims, width), masked, stream
 
 
-def fold_kernel(masked_ref, mask_ref, low_ref, kernel_ref, all_ref, back_ref,
-                gone, own, twin_in, relay_in, side_in, along_in, tiles, backs, tile_sem, back_sem, keep_sem, twin_send, twin_recv,
+def fold_kernel(masked_ref, mask_ref, low_ref, kernel_ref, out_ref, all_ref, back_ref, out_in,
+                gone, own, twin_in, relay_in, side_in, along_in, tiles, backs, out_sem, tile_sem, back_sem, keep_sem, twin_send, twin_recv,
                 relay_send, relay_recv, side_send, side_recv, along_send, along_recv, swap_send, swap_recv,
                 group_send, group_recv, give_send, give_recv):
     f32, bf16 = jnp.float32, jnp.bfloat16
@@ -1332,9 +1356,15 @@
         a, b = spot_of(j)
         own[a, b, cut(k)] = value.astype(bf16)
 
+    output = remote(out_ref, out_in, out_sem.at[0], out_sem.at[1], partner)
     fetch(0).start()
     fetch(1).start()
     greet([side, along, twin, partner, over])
+
+    @pl.when(moved)
+    def _():
+        output.start()
+
     half(1 - c, gone)
     for k in range(count):
         swap(k).start()
@@ -1391,6 +1421,7 @@
 
     @pl.when(moved)
     def _():
+        output.wait()
         for k in range(count):
             move(k).wait_send()
 
@@ -1407,21 +1438,23 @@
             given(j, k).wait_recv()
 
 
-def fold_kernels(masked, mask, low, kernels, seq):
+def fold_kernels(masked, mask, low, kernels, out):
+    seq = out.shape[0]
     width = masked.shape[1]
     dims = kernels.shape[0] // 8
     count = dims // CHUNK
     bf16 = jnp.bfloat16
     dma = pltpu.SemaphoreType.DMA
     vmem, far = pl.BlockSpec(memory_space=pltpu.VMEM), pl.BlockSpec(memory_space=pl.ANY)
-    folded, back = pl.pallas_call(
+    folded, back, out_in = pl.pallas_call(
         fold_kernel,
         out_shape=[
             jax.ShapeDtypeStruct((2, 2, dims, width), bf16),
             jax.ShapeDtypeStruct((1, seq, width), bf16),
+            jax.ShapeDtypeStruct(out.shape, out.dtype),
         ],
-        in_specs=[vmem, vmem, vmem, far],
-        out_specs=[far, far],
+        in_specs=[vmem, vmem, vmem, far, far],
+        out_specs=[far, far, far],
         scratch_shapes=[
             pltpu.VMEM((2, 2, dims, width), bf16),
             pltpu.VMEM((2, 2, dims, width), bf16),
@@ -1433,14 +1466,15 @@
             pltpu.VMEM((2, seq, 1024), bf16),
             dma((2,)),
             dma((2,)),
+            dma((2,)),
             dma((count,)),
         ]
         + [dma((count,))] * 12
         + [dma((2, count))] * 2,
         compiler_params=pltpu.CompilerParams(collective_id=3, has_side_effects=True, vmem_limit_bytes=60 << 20),
         name="fold_kernels",
-    )(masked, mask, low, kernels)
-    return folded.reshape(4, dims, width), back
+    )(masked, mask, low, kernels, out)
+    return folded.reshape(4, dims, width), back, out_in
 
 
 def on_device(
@@ -1467,13 +1501,17 @@
     slot_blocks = (own_rows + extra) // 8
     mask = band_mask.astype(f32)
     if fits:
-        mask = swap_images(mask)
-        gathered, head, low_weight = gather_packed(rest_weight, pixels, fc_weight, own_rows + extra)
-        gathered, rest, cotangent, low_weight = lax.optimization_barrier(
-            (gathered, pixels[:, HEAD:], cotangent, low_weight)
+        group, image = lax.axis_index("group"), lax.axis_index("img")
+        moved = (group % 2 + image // 4) % 2 == 1
+        wide_mask = jnp.pad(mask, ((0, 7), (0, 128 - NB)))
+        gathered, head, low_weight, up_in, mask_in = gather_packed(
+            rest_weight, pixels, fc_weight, cotangent, wide_mask, own_rows + extra
         )
+        gathered, rest, low_weight = lax.optimization_barrier((gathered, pixels[:, HEAD:], low_weight))
         across = swap_group(low_weight, 2)
-        rest, cotangent = swap_images(rest), swap_images(cotangent)
+        rest = swap_images(rest)
+        cotangent = jnp.where(moved, up_in, cotangent)
+        mask = jnp.where(moved, mask_in[:1, :NB], mask)
     else:
         low_weight = fc_weight.astype(bf16)
         rest_low = jnp.pad(rest_weight.astype(bf16), ((0, extra), (0, 0)))
@@ -1487,10 +1525,7 @@
         constant_values=total_blocks,
     ).reshape(-1)
     unpacked = spread_packed(gathered, slots, total_blocks)
-    if fits:
-        *unpacked, across = lax.optimization_barrier((*unpacked, across))
-        slabs = [low_weight, swap_group(low_weight, 1), across, swap_group(across, 1)]
-    else:
+    if not fits:
         master = lax.all_gather(low_weight, "group", axis=0, tiled=True)
     block_mats, wave_mats = unpacked[:4], unpacked[4:10]
     block_vectors, wave_vectors = unpacked[10:]
@@ -1498,7 +1533,7 @@
     shaped_low, own_shaped, kept, slope = wave_layer(embedded, wave_mats, wave_vectors)
     mask = jnp.repeat(mask, PATCH, axis=1)
     if fits:
-        kernel_all, masked, stream = share_kernels(shaped_low, mask, slabs, pixels, head, rest)
+        kernel_all, masked, stream = share_kernels(shaped_low, mask, (low_weight, across), pixels, head, rest)
     else:
         kernel_low = make_kernels(shaped_low, master)
         kernel_all = lax.all_gather(kernel_low, "img", axis=0, tiled=True)
@@ -1508,9 +1543,10 @@
         stream, cotangent, block_vectors, *block_mats
     )
     if fits:
-        all_groups, pixel_grad = fold_kernels(masked, mask, grad_low, kernel_all, pixels.shape[1])
-        all_groups, block_out, pixel_grad = lax.optimization_barrier((all_groups, block_out, pixel_grad))
-        block_out, pixel_grad = swap_images(block_out), swap_images(pixel_grad)
+        all_groups, pixel_grad, out_in = fold_kernels(masked, mask, grad_low, kernel_all, block_out)
+        all_groups, pixel_grad = lax.optimization_barrier((all_groups, pixel_grad))
+        pixel_grad = swap_images(pixel_grad)
+        block_out = jnp.where(moved, out_in, block_out)
     else:
         pixel_grad, kernel_grad = unembed_patches(masked, mask, kernel_all, grad_low, pixels.shape[1])
         kernel_grad_low = lax.psum_scatter(kernel_grad, "img", scatter_dimension=0, tiled=True)

time: 521 us -> 509 us (0.977)
  starting transfers between devices: 25.9 us -> 4.36 us
  Pallas kernels: 474 us -> 480 us
    ppermute x3 -> x1, starting transfers between devices: 17.4 us -> 1.01 us  [swap_group(): return lax.ppermute(value, 'group', [(j, j ^ flip) for j in range(4)])]
    pallas_call x1, Pallas kernels: 89.3 us -> 101 us  [share_kernels(): pl.pallas_call(share_kernel, out_shape=[jax.ShapeDtypeStruct((4, 2, dims,...]
    pallas_call x1, Pallas kernels: 96.2 us -> 85 us  [reduce_packed(): pl.pallas_call(reduce_kernel, out_shape=jax.ShapeDtypeStruct((rows, 128),...]
    pallas_call x1, Pallas kernels: 93 us -> 99 us  [fold_kernels(): pl.pallas_call(fold_kernel, out_shape=[jax.ShapeDtypeStruct((2, 2, dims,...]
  transfers between devices with their start and end apart: 8 -> 3, of which waited for: 0 -> 0; matrix products, arithmetic and copies ran while one was open for 1% -> 2% of each run, Pallas kernels for 52% -> 33%
where the time goes in v4:
time: 509 us; the launch traced here: 500 us
  Pallas kernels  480 us (94%)
  other arithmetic  7.58 us (1%)
  local copies, waits for them, and re-layouts  6.74 us (1%)
    pallas_call x1, Pallas kernels, share_kernels(): pl.pallas_call(share_kernel, out_shape=[jax.ShapeDtypeStruct((4, 2, dims,...  101 us
    pallas_call x1, Pallas kernels, fold_kernels(): pl.pallas_call(fold_kernel, out_shape=[jax.ShapeDtypeStruct((2, 2, dims,...  99 us
    pallas_call x1, Pallas kernels, reduce_packed(): pl.pallas_call(reduce_kernel, out_shape=jax.ShapeDtypeStruct((rows, 128),...  85 us
    pallas_call x1, Pallas kernels, gather_packed(): pl.pallas_call(gather_kernel, out_shape=[jax.ShapeDtypeStruct((2, 2, 4, 2...  83.9 us
    pallas_call x1, Pallas kernels, block_pass(): pl.pallas_call(block_kernel, out_shape=[jax.ShapeDtypeStruct((seq, D), bf...  31.2 us
    pallas_call x1, Pallas kernels, spread_packed(): pl.pallas_call(spread_kernel, out_shape=big + small, grid_spec=pltpu.Pref...  27.3 us
    pallas_call x1, Pallas kernels, collect_packed(): pl.pallas_call(collect_kernel, out_shape=jax.ShapeDtypeStruct((shards, ro...  25.8 us
    pallas_call x1, Pallas kernels, master_update(): pl.pallas_call(functools.partial(master_kernel, rate), out_shape=[like, l...  13.1 us
  transfers between devices with their start and end apart: 3, of which 0 were waited for; matrix products, arithmetic and copies ran while one was open for 2% of the time, Pallas kernels for 33%

profile of v4, /device:TPU:0, one launch (start us, length us, event | category | flops | bytes accessed | tf_op | source)
XLA Modules:
  0.0 500.2 jit_solution(3741309739708483585)
XLA Ops:
  0.6 0.7 convert_element_type.9
  1.3 1.6 slice.9
  3.5 83.9 %gather_packed.1 = (bf16[2,2,4,2,1920,128]{5,4,3,2,1,0:T(8,128)(2,1)}, bf16[1,96,8192]{2,1,0:T(8,128)(2,1)}, bf16[32,24576]{1,0:T(8,128)(2,1)}, bf16[196,768]{1,0:T(8,128)(2,1)}, f32[8,128]{1,0:T(8,128)}) custom-call(f32[1880,128]{1,0:T(8,128)} %rest_ref.1, bf16[1,196,8192]{2,1,0:T(8,128)(2,1)} %pixel_ref.3, f32[32,24576]{1,0:T(8,128)} %weight_ref.3, ...), custom_call_target="tpu_custom_call" | custom-call | tf_op jit(solution)/shard_map/gather_packed/pallas_call | solution.py:874
  87.3 0.8 collective-permute-start.1
  88.1 1.0 collective-permute-start
  89.4 0.7 reshape.52.order_ref
  90.1 0.7 fusion.1
  90.8 0.7 copy.19
  91.5 27.3 %spread_packed.1 = (bf16[768,2304]{1,0:T(8,128)(2,1)}, bf16[768,768]{1,0:T(8,128)(2,1)}, bf16[768,3072]{1,0:T(8,128)(2,1)}, bf16[3072,768]{1,0:T(8,128)(2,1)}, f...) custom-call(s32[7680]{0:T(1024)} %reshape.52.order_ref, ...), custom_call_target="tpu_custom_call" | custom-call | tf_op jit(solution)/shard_map/spread_packed/pallas_call | solution.py:145
  119.2 0.7 pad_maximum_fusion.embed_ref
  119.9 6.7 %wave_layer.1 = (bf16[128,128]{1,0:T(8,128)(2,1)}, bf16[128,32]{1,0:T(8,128)(2,1)}, f32[12,128,128]{2,1,0:T(8,128)}, f32[2,128,2048]{2,1,0:T(8,128)}) custom-call(f32[128,128]{1,0:T(8,128)} %pad_maximum_fusion.embed_ref, f32[128,128]{1,0:T(8,128)} %get-tuple-element.61.wq_ref, f32[128,128]{1,0:T(8,128)} %get-tuple-element.62.wk_ref, ...), custom_call_target="tpu_custom_call" | custom-call | tf_op jit(solution)/shard_map/wave_layer/pallas_call | solution.py:294
  126.6 0.8 broadcast_select_fusion.1.up_ref
  127.4 1.2 copy-done.1
  128.6 101.0 %share_kernels.1 = (bf16[4,2,96,8192]{3,2,1,0:T(8,128)(2,1)}, bf16[208,8192]{1,0:T(8,128)(2,1)}, f32[196,768]{1,0:T(8,128)}) custom-call(bf16[128,128]{1,0:T(8,128)(2,1)} %get-tuple-element.68.shaped_ref, f32[1,8192]{1,0:T(1,128)} %bitcast.14, bf16[32,24576]{1,0:T(8,128)(2,1)} %get-tuple-element.70.own_slab, ...), custom_call_target="tpu_custom_call" | custom-call | tf_op jit(solution)/shard_map/share_kernels/pallas_call | solution.py:1235
  229.6 31.2 %block_pass.1 = (bf16[196,768]{1,0:T(8,128)(2,1)}, bf16[208,768]{1,0:T(8,128)(2,1)}, f32[8,768]{1,0:T(8,128)}, bf16[768,2304]{1,0:T(8,128)(2,1)}, bf16[768,768]{...) custom-call(f32[196,768]{1,0:T(8,128)} %get-tuple-element.74.stream_ref, ...), custom_call_target="tpu_custom_call" | custom-call | flops 8400000000 | bytes 30000000 | tf_op jit(solution)/shard_map/block_pass/pallas_call | solution.py:521
  260.7 99.0 %fold_kernels.1 = (bf16[2,2,96,8192]{3,2,1,0:T(8,128)(2,1)}, bf16[1,196,8192]{2,1,0:T(8,128)(2,1)}, bf16[196,768]{1,0:T(8,128)(2,1)}) custom-call(bf16[208,8192]{1,0:T(8,128)(2,1)} %get-tuple-element.73.masked_ref, f32[1,8192]{1,0:T(1,128)} %bitcast.15, bf16[208,768]{1,0:T(8,128)(2,1)} %get-tuple-element.81.low_ref, bf16[768,8192]{1,0:T(8,128)(2,1)} %bitcast.12, ...), custom_call_target="tpu_custom_call" | custom-call | tf_op jit(solution)/shard_map/fold_kernels/pallas_call | solution.py:1449
  359.7 2.6 collective-permute-start.2
  362.3 13.1 %master_update.1 = (f32[32,24576]{1,0:T(8,128)}, f32[32,24576]{1,0:T(8,128)}, f32[32,24576]{1,0:T(8,128)}, f32[128,32]{1,0:T(8,128)}) custom-call(bf16[4,96,8192]{2,1,0:T(8,128)(2,1)} %bitcast.13, bf16[128,32]{1,0:T(8,128)(2,1)} %get-tuple-element.93.shaped_ref, f32[32,24576]{1,0:T(8,128)} %weight_ref.3, f32[32,24576]{1,0:T(8,128)} %one_ref.1, ...), custom_call_target="tpu_custom_call" | custom-call | tf_op jit(solution)/shard_map/master_update/pallas_call | solution.py:710
  375.4 7.3 %wave_back.1 = (f32[128,128]{1,0:T(8,128)}, f32[128,128]{1,0:T(8,128)}, f32[128,128]{1,0:T(8,128)}, f32[128,128]{1,0:T(8,128)}, f32[128,2048]{1,0:T(8,128)}, /*index=5*/f32[2048,128]{1,0:T(8,128)}, f32[8,128]{1,0:T(8,128)}) custom-call(f32[128,32]{1,0:T(8,128)} %get-tuple-element.94.part_ref, f32[128,128]{1,0:T(8,128)} %pad_maximum_fusion.embed_ref, ...), custom_call_target="tpu_custom_call" | custom-call | tf_op jit(solution)/shard_map/wave_back/pallas_call | solution.py:348
  382.7 25.8 %collect_packed.1 = bf16[32,1920,128]{2,1,0:T(8,128)(2,1)} custom-call(s32[7680]{0:T(1024)} %reshape.52.order_ref, bf16[768,2304]{1,0:T(8,128)(2,1)} %get-tuple-element.88.refs_0_, bf16[768,768]{1,0:T(8,128)(2,1)} %get-tuple-element.89.refs_1_, bf16[768,3072]{1,0:T(8,128)(2,1)} %get-tuple-element.90.refs_2_, bf16[3072,768]{1,0:T(8,128)(2,1)} %get-tuple-element.91.refs_3_, ...), custom_call_target="tpu_custom_call" | custom-call | tf_op jit(solution)/shard_map/collect_packed/pallas_call | solution.py:213
  408.6 85.0 %reduce_packed.1 = f32[1920,128]{1,0:T(8,128)} custom-call(bf16[2,2,4,2,1920,128]{5,4,3,2,1,0:T(8,128)(2,1)} %bitcast.10), custom_call_target="tpu_custom_call" | custom-call | tf_op jit(solution)/shard_map/reduce_packed/pallas_call | solution.py:981
  493.6 0.8 broadcast_select_fusion
  494.4 3.7 multiply_subtract_fusion
  498.1 1.7 copy.21
  (32 shorter events, 1.3 us)
Async XLA Ops:
  3.5 85.7 %copy-start.9 = (s32[4,32]{1,0:T(4,128)S(1)}, s32[4,32]{1,0:T(4,128)}, u32[]{:S(2)}) copy-start(s32[4,32]{1,0:T(4,128)} %param.13) | copy-start | bytes 1540
  3.5 85.8 %copy-start.8 = (s32[7520]{0:T(1024)S(1)}, s32[7520]{0:T(1024)}, u32[]{:S(2)}) copy-start(s32[7520]{0:T(1024)} %param.14) | copy-start | bytes 90244
  3.5 86.6 %copy-start.10 = (s32[1,32]{1,0:T(1,128)S(1)}, s32[1,32]{1,0:T(1,128)}, u32[]{:S(2)}) copy-start(s32[1,32]{1,0:T(1,128)} %param.12) | copy-start | bytes 388
  87.3 40.0 %collective-permute-start.1 = (bf16[1,100,8192]{2,1,0:T(8,128)(2,1)S(1)}, bf16[1,100,8192]{2,1,0:T(8,128)(2,1)S(1)}, u32[]{:S(2)}, u32[]{:S(2)}) collective-permute-start(bf16[1,100,8192]{2,1,0:T(8,128)(2,1)S(1)} %slice.9), channel_id=1, source_target_pairs={{0,0},{1,1},{2,2},{3,3},{4,8},{5,9},{6,10},{7,11},{8,4},{9,5},{10,... | collective-permute-start | bytes 4915208 | tf_op jit(solution)/shard_map/ppermute | solution.py:1029
  88.1 39.3 %collective-permute-start = (bf16[32,24576]{1,0:T(8,128)(2,1)}, bf16[32,24576]{1,0:T(8,128)(2,1)}, u32[]{:S(2)}, u32[]{:S(2)}) collective-permute-start(bf16[32,24576]{1,0:T(8,128)(2,1)} %get-tuple-element.70.own_slab), channel_id=1, source_target_pairs={{0,16},{8,24},{16,0},{24,8},{1,17},{9,25},{17,1},{25,9},{2,18},{10... | collective-permute-start | bytes 4718600 | tf_op jit(solution)/shard_map/ppermute | solution.py:1018
  91.5 35.1 %copy-start.3 = (bf16[196,768]{1,0:T(8,128)(2,1)S(1)}, bf16[196,768]{1,0:T(8,128)(2,1)}, u32[]{:S(2)}) copy-start(bf16[196,768]{1,0:T(8,128)(2,1)} %up_ref.1) | copy-start | bytes 903172
  91.5 35.1 %copy-start.6 = (bf16[196,768]{1,0:T(8,128)(2,1)S(1)}, bf16[196,768]{1,0:T(8,128)(2,1)}, u32[]{:S(2)}) copy-start(bf16[196,768]{1,0:T(8,128)(2,1)} %get-tuple-element.75) | copy-start | bytes 903172
  127.4 1.2 copy-start.1
  359.7 138.3 %collective-permute-start.2 = (bf16[1,196,8192]{2,1,0:T(8,128)(2,1)}, bf16[1,196,8192]{2,1,0:T(8,128)(2,1)S(1)}, u32[]{:S(2)}, u32[]{:S(2)}) collective-permute-start(bf16[1,196,8192]{2,1,0:T(8,128)(2,1)} %get-tuple-element.87), channel_id=1, source_target_pairs={{0,0},{1,1},{2,2},{3,3},{4,8},{5,9},{6,10},{7,11},{8,4},{9,5},{10,... | collective-permute-start | bytes 9633800 | tf_op jit(solution)/shard_map/ppermute | solution.py:1029
  408.5 85.1 %copy-start.2 = (bf16[196,768]{1,0:T(8,128)(2,1)S(1)}, bf16[196,768]{1,0:T(8,128)(2,1)}, u32[]{:S(2)}) copy-start(bf16[196,768]{1,0:T(8,128)(2,1)} %get-tuple-element.83.out_ref) | copy-start | bytes 903172
  408.5 85.1 %copy-start.7 = (bf16[196,768]{1,0:T(8,128)(2,1)S(1)}, bf16[196,768]{1,0:T(8,128)(2,1)}, u32[]{:S(2)}) copy-start(bf16[196,768]{1,0:T(8,128)(2,1)} %get-tuple-element.84) | copy-start | bytes 903172
  408.6 85.8 %copy-start = (f32[1880,128]{1,0:T(8,128)S(1)}, f32[1880,128]{1,0:T(8,128)}, u32[]{:S(2)}) copy-start(f32[1880,128]{1,0:T(8,128)} %rest_ref.1) | copy-start | bytes 2887684
  408.6 85.8 %copy-start.4 = (f32[1880,128]{1,0:T(8,128)S(1)}, f32[1880,128]{1,0:T(8,128)}, u32[]{:S(2)}) copy-start(f32[1880,128]{1,0:T(8,128)} %param.16) | copy-start | bytes 2887684
  408.6 85.8 %copy-start.5 = (f32[1880,128]{1,0:T(8,128)S(1)}, f32[1880,128]{1,0:T(8,128)}, u32[]{:S(2)}) copy-start(f32[1880,128]{1,0:T(8,128)} %param.17) | copy-start | bytes 2887684

commit v5 on v4

--- a/solution.py
+++ b/solution.py
@@ -997,10 +997,15 @@
 
 
 CHUNK = 16
+CUTS = 2
 
 
 def over_x(k):
-    return k % 2 == 0
+    return k % 3 != 2
+
+
+def over_z(k):
+    return k % 3 == 0
 
 
 def quad_peers():
@@ -1035,23 +1040,27 @@
     f32, bf16 = jnp.float32, jnp.bfloat16
     y, c, z, x, low, side, along, twin, partner, moved = quad_peers()
     dims, width = made_ref.shape
-    count = dims // CHUNK
+    chunks = dims // CHUNK
+    count = chunks * CUTS
     group = 8 * CHUNK
 
     def cut(k):
-        return pl.ds(k * CHUNK, CHUNK)
+        return pl.ds(k // CUTS * CHUNK, CHUNK), pl.ds(k % CUTS * (width // CUTS), width // CUTS)
+
+    def rows_of(r):
+        return pl.ds(r * CHUNK, CHUNK)
 
     def block(core, j, k):
-        return held.at[2 * core + (low + j // 2) % 2, (x + j % 2) % 2, cut(k)]
+        return held.at[2 * core + (low + j // 2) % 2, (x + j % 2) % 2, *cut(k)]
 
     def keep(k):
-        return pltpu.make_async_copy(made_ref.at[cut(k)], block(c, 0, k), keep_sem.at[k])
+        return pltpu.make_async_copy(made_ref.at[*cut(k)], block(c, 0, k), keep_sem.at[k])
 
     def swap(k):
-        return remote(made_ref.at[cut(k)], block(1 - c, 0, k), swap_send.at[k], swap_recv.at[k], partner)
+        return remote(made_ref.at[*cut(k)], block(1 - c, 0, k), swap_send.at[k], swap_recv.at[k], partner)
 
     def swap_in(k):
-        return remote(made_ref.at[cut(k)], block(c, 0, k), swap_send.at[k], swap_recv.at[k], partner)
+        return remote(made_ref.at[*cut(k)], block(c, 0, k), swap_send.at[k], swap_recv.at[k], partner)
 
     def to_side(k):
         return remote(block(c, 0, k), block(c, 0, k), side_send.at[k], side_recv.at[k], side)
@@ -1100,24 +1109,26 @@
         for j in range(2):
             load_slab(j, k).wait()
             slab_in(j, k).wait_recv()
-        spread_bands(own_bands(shaped_ref), master.at[k], turned, made_ref.at[cut(k)])
+        spread_bands(own_bands(shaped_ref), master.at[k], turned, made_ref.at[rows_of(k)])
 
         @pl.when(moved)
         def _():
-            swap(k).start()
+            for cut_at in range(CUTS):
+                swap(k * CUTS + cut_at).start()
 
         @pl.when(jnp.logical_not(moved))
         def _():
-            keep(k).start()
-
-    def store(k):
-        return pltpu.make_async_copy(held.at[:, :, cut(k)], all_ref.at[:, :, cut(k)], store_sem.at[k])
+            for cut_at in range(CUTS):
+                keep(k * CUTS + cut_at).start()
+
+    def store(r):
+        return pltpu.make_async_copy(held.at[:, :, rows_of(r)], all_ref.at[:, :, rows_of(r)], store_sem.at[r])
 
     swapped = pltpu.make_async_copy(head_ref.at[0], top, pixel_sem.at[0])
     owned = pltpu.make_async_copy(pixel_ref.at[0, pl.ds(0, HEAD)], top, pixel_sem.at[0])
     lower = pltpu.make_async_copy(rest_ref.at[0], bottom, pixel_sem.at[1])
 
-    for k in range(count):
+    for k in range(chunks):
         for j in range(2):
             load_slab(j, k).start()
 
@@ -1131,7 +1142,7 @@
 
     lower.start()
     greet([side, along, twin, partner])
-    for k in range(count):
+    for k in range(chunks):
         for j in range(2):
             send_slab(j, k).start()
     make(0)
@@ -1175,11 +1186,11 @@
             to_side(k).start()
             to_along(k).start()
             give(0, k).start()
-        if step + 1 < count:
-            make(step + 1)
-        if step in (1, 2):
-            mask_pixels(step - 1)
-        elif step == 3:
+        if step % CUTS == 0 and step // CUTS + 1 < chunks:
+            make(step // CUTS + 1)
+        if step in (1, 3):
+            mask_pixels(step // 2)
+        elif step == 5:
             make_order()
         k = step - 1
         if 0 <= k < count:
@@ -1201,9 +1212,11 @@
         if 0 <= k < count:
             for j in range(4):
                 given(j, k).wait_recv()
-            store(k).start()
-            part = held[:, :, cut(k), :].reshape(group, width)
-            mixed[:, k * group : (k + 1) * group] = dot_nt(masked_ref[...], part)
+            if k % CUTS == CUTS - 1:
+                r = k // CUTS
+                store(r).start()
+                part = held[:, :, rows_of(r), :].reshape(group, width)
+                mixed[:, r * group : (r + 1) * group] = dot_nt(masked_ref[...], part)
 
     stream_ref[...] = finer(mixed[...], order[...], 1, 0)[0 : stream_ref.shape[0]]
 
@@ -1216,17 +1229,19 @@
         to_side(k).wait_send()
         to_along(k).wait_send()
         pass_on(k).wait_send()
+        for j in range(4):
+            give(j, k).wait_send()
+    for k in range(chunks):
         store(k).wait()
         for j in range(2):
             send_slab(j, k).wait_send()
-        for j in range(4):
-            give(j, k).wait_send()
 
 
 def share_kernels(shaped, mask, slabs, pixels, head, rest):
     dims, width = slabs[0].shape[1] // PATCH, mask.shape[1]
     bf16 = jnp.bfloat16
-    count = dims // CHUNK
+    chunks = dims // CHUNK
+    count = chunks * CUTS
     seq = pixels.shape[1]
     rows = tall(seq)
     f32 = jnp.float32
@@ -1243,7 +1258,7 @@
         out_specs=[far, vmem, vmem],
         scratch_shapes=[
             pltpu.VMEM((dims, width), bf16),
-            pltpu.VMEM((count, E, CHUNK * PATCH), bf16),
+            pltpu.VMEM((chunks, E, CHUNK * PATCH), bf16),
             pltpu.VMEM((2 * NB * CHUNK, 128), f32),
             pltpu.VMEM((4, 2, dims, width), bf16),
             pltpu.VMEM((HEAD, width), bf16),
@@ -1251,9 +1266,9 @@
             pltpu.VMEM((rows - HEAD, 1024), f32),
             pltpu.VMEM((rows, 8 * dims), f32),
             pltpu.VMEM((8 * dims, 8 * dims), f32),
-            dma((2, count)),
-            dma((2, count)),
-            dma((2, count)),
+            dma((2, chunks)),
+            dma((2, chunks)),
+            dma((2, chunks)),
             dma((2,)),
         ]
         + [dma((count,))] * 10
@@ -1272,53 +1287,53 @@
     y, c, z, x, low, side, along, twin, partner, moved = quad_peers()
     over = place(1 - y, c, z, x)
     dims, width = all_ref.shape[2], all_ref.shape[3]
-    count = dims // CHUNK
+    count = dims // CHUNK * CUTS
     seq = back_ref.shape[1]
     lane = tiles.shape[2]
 
     def cut(k):
-        return pl.ds(k * CHUNK, CHUNK)
+        return pl.ds(k // CUTS * CHUNK, CHUNK), pl.ds(k % CUTS * (width // CUTS), width // CUTS)
 
     def spot_of(j):
         return (low + j // 2) % 2, (x + j % 2) % 2
 
     def mine(j, k):
         a, b = spot_of(j)
-        return own.at[a, b, cut(k)]
+        return own.at[a, b, *cut(k)]
 
     def swap(k):
-        return remote(gone.at[:, :, cut(k)], twin_in.at[:, :, cut(k)], twin_send.at[k], twin_recv.at[k], twin)
+        return remote(gone.at[:, :, *cut(k)], twin_in.at[:, :, *cut(k)], twin_send.at[k], twin_recv.at[k], twin)
 
     def relay(k):
-        return remote(mine(3, k), relay_in.at[cut(k)], relay_send.at[k], relay_recv.at[k], along if over_x(k) else side)
+        return remote(mine(3, k), relay_in.at[*cut(k)], relay_send.at[k], relay_recv.at[k], along if over_z(k) else side)
 
     def to_side(k):
-        return remote(mine(1, k), side_in.at[cut(k)], side_send.at[k], side_recv.at[k], side)
+        return remote(mine(1, k), side_in.at[*cut(k)], side_send.at[k], side_recv.at[k], side)
 
     def to_along(k):
-        return remote(mine(2, k), along_in.at[cut(k)], along_send.at[k], along_recv.at[k], along)
+        return remote(mine(2, k), along_in.at[*cut(k)], along_send.at[k], along_recv.at[k], along)
 
     def keep(k):
-        return pltpu.make_async_copy(mine(0, k), all_ref.at[y, c, cut(k)], keep_sem.at[k])
+        return pltpu.make_async_copy(mine(0, k), all_ref.at[y, c, *cut(k)], keep_sem.at[k])
 
     def move(k):
-        return remote(mine(0, k), all_ref.at[y, 1 - c, cut(k)], swap_send.at[k], swap_recv.at[k], partner)
+        return remote(mine(0, k), all_ref.at[y, 1 - c, *cut(k)], swap_send.at[k], swap_recv.at[k], partner)
 
     def moved_in(k):
-        return remote(mine(0, k), all_ref.at[y, c, cut(k)], swap_send.at[k], swap_recv.at[k], partner)
+        return remote(mine(0, k), all_ref.at[y, c, *cut(k)], swap_send.at[k], swap_recv.at[k], partner)
 
     def cross(k):
-        return remote(all_ref.at[y, c, cut(k)], all_ref.at[y, c, cut(k)], group_send.at[k], group_recv.at[k], over)
+        return remote(all_ref.at[y, c, *cut(k)], all_ref.at[y, c, *cut(k)], group_send.at[k], group_recv.at[k], over)
 
     def crossed(k):
-        return remote(all_ref.at[1 - y, c, cut(k)], all_ref.at[1 - y, c, cut(k)], group_send.at[k], group_recv.at[k], over)
+        return remote(all_ref.at[1 - y, c, *cut(k)], all_ref.at[1 - y, c, *cut(k)], group_send.at[k], group_recv.at[k], over)
 
     def give(j, k):
-        here = all_ref.at[(y + j) % 2, c, cut(k)]
+        here = all_ref.at[(y + j) % 2, c, *cut(k)]
         return remote(here, here, give_send.at[j, k], give_recv.at[j, k], twin)
 
     def given(j, k):
-        here = all_ref.at[(y + j) % 2, 1 - c, cut(k)]
+        here = all_ref.at[(y + j) % 2, 1 - c, *cut(k)]
         return remote(here, here, give_send.at[j, k], give_recv.at[j, k], twin)
 
     def fetch(j):
@@ -1350,11 +1365,11 @@
 
     def pair(j, k):
         a, b = spot_of(j)
-        return own[a, b, cut(k)].astype(f32) + twin_in[a, b, cut(k)].astype(f32)
+        return own[a, b, *cut(k)].astype(f32) + twin_in[a, b, *cut(k)].astype(f32)
 
     def put(j, k, value):
         a, b = spot_of(j)
-        own[a, b, cut(k)] = value.astype(bf16)
+        own[a, b, *cut(k)] = value.astype(bf16)
 
     output = remote(out_ref, out_in, out_sem.at[0], out_sem.at[1], partner)
     fetch(0).start()
@@ -1378,18 +1393,18 @@
             relay(k).start()
         k = step - 1
         if 0 <= k < count:
-            first, second = (to_along, to_side) if over_x(k) else (to_side, to_along)
-            plain, summed = (2, 1) if over_x(k) else (1, 2)
+            first, second = (to_along, to_side) if over_z(k) else (to_side, to_along)
+            plain, summed = (2, 1) if over_z(k) else (1, 2)
             put(plain, k, pair(plain, k))
             first(k).start()
             relay(k).wait_recv()
-            put(summed, k, pair(summed, k) + relay_in[cut(k)].astype(f32))
+            put(summed, k, pair(summed, k) + relay_in[*cut(k)].astype(f32))
             second(k).start()
         k = step - 2
         if 0 <= k < count:
             to_side(k).wait_recv()
             to_along(k).wait_recv()
-            put(0, k, pair(0, k) + side_in[cut(k)].astype(f32) + along_in[cut(k)].astype(f32))
+            put(0, k, pair(0, k) + side_in[*cut(k)].astype(f32) + along_in[*cut(k)].astype(f32))
 
             @pl.when(moved)
             def _(k=k):
@@ -1442,7 +1457,7 @@
     seq = out.shape[0]
     width = masked.shape[1]
     dims = kernels.shape[0] // 8
-    count = dims // CHUNK
+    count = dims // CHUNK * CUTS
     bf16 = jnp.bfloat16
     dma = pltpu.SemaphoreType.DMA
     vmem, far = pl.BlockSpec(memory_space=pltpu.VMEM), pl.BlockSpec(memory_space=pl.ANY)

time: 509 us -> 500 us (0.982)
  Pallas kernels: 480 us -> 472 us
    pallas_call x1, Pallas kernels: 99 us -> 87.5 us  [fold_kernels(): pl.pallas_call(fold_kernel, out_shape=[jax.ShapeDtypeStruct((2, 2, dims,...]
  transfers between devices with their start and end apart: 3 -> 3, of which waited for: 0 -> 0; matrix products, arithmetic and copies ran while one was open for 2% -> 2% of each run, Pallas kernels for 33% -> 35%
where the time goes in v5:
time: 500 us; the launch traced here: 492 us
  Pallas kernels  472 us (94%)
  other arithmetic  7.58 us (2%)
  local copies, waits for them, and re-layouts  6.74 us (1%)
    pallas_call x1, Pallas kernels, share_kernels(): pl.pallas_call(share_kernel, out_shape=[jax.ShapeDtypeStruct((4, 2, dims,...  99.1 us
    pallas_call x1, Pallas kernels, reduce_packed(): pl.pallas_call(reduce_kernel, out_shape=jax.ShapeDtypeStruct((rows, 128),...  89.9 us
    pallas_call x1, Pallas kernels, fold_kernels(): pl.pallas_call(fold_kernel, out_shape=[jax.ShapeDtypeStruct((2, 2, dims,...  87.5 us
    pallas_call x1, Pallas kernels, gather_packed(): pl.pallas_call(gather_kernel, out_shape=[jax.ShapeDtypeStruct((2, 2, 4, 2...  83.9 us
    pallas_call x1, Pallas kernels, block_pass(): pl.pallas_call(block_kernel, out_shape=[jax.ShapeDtypeStruct((seq, D), bf...  31.4 us
    pallas_call x1, Pallas kernels, spread_packed(): pl.pallas_call(spread_kernel, out_shape=big + small, grid_spec=pltpu.Pref...  27.3 us
    pallas_call x1, Pallas kernels, collect_packed(): pl.pallas_call(collect_kernel, out_shape=jax.ShapeDtypeStruct((shards, ro...  25.8 us
    pallas_call x1, Pallas kernels, master_update(): pl.pallas_call(functools.partial(master_kernel, rate), out_shape=[like, l...  13.3 us
  transfers between devices with their start and end apart: 3, of which 0 were waited for; matrix products, arithmetic and copies ran while one was open for 2% of the time, Pallas kernels for 35%

profile of v5, /device:TPU:0, one launch (start us, length us, event | category | flops | bytes accessed | tf_op | source)
XLA Modules:
  0.0 491.8 jit_solution(15782656676968838867)
XLA Ops:
  0.6 0.7 convert_element_type.9
  1.3 1.6 slice.9
  3.5 83.9 %gather_packed.1 = (bf16[2,2,4,2,1920,128]{5,4,3,2,1,0:T(8,128)(2,1)}, bf16[1,96,8192]{2,1,0:T(8,128)(2,1)}, bf16[32,24576]{1,0:T(8,128)(2,1)}, bf16[196,768]{1,0:T(8,128)(2,1)}, f32[8,128]{1,0:T(8,128)}) custom-call(f32[1880,128]{1,0:T(8,128)} %rest_ref.1, bf16[1,196,8192]{2,1,0:T(8,128)(2,1)} %pixel_ref.3, f32[32,24576]{1,0:T(8,128)} %weight_ref.3, ...), custom_call_target="tpu_custom_call" | custom-call | tf_op jit(solution)/shard_map/gather_packed/pallas_call | solution.py:874
  87.3 0.8 collective-permute-start.1
  88.1 1.0 collective-permute-start
  89.4 0.7 reshape.52.order_ref
  90.1 0.7 fusion.1
  90.8 0.7 copy.19
  91.5 27.3 %spread_packed.1 = (bf16[768,2304]{1,0:T(8,128)(2,1)}, bf16[768,768]{1,0:T(8,128)(2,1)}, bf16[768,3072]{1,0:T(8,128)(2,1)}, bf16[3072,768]{1,0:T(8,128)(2,1)}, f...) custom-call(s32[7680]{0:T(1024)} %reshape.52.order_ref, ...), custom_call_target="tpu_custom_call" | custom-call | tf_op jit(solution)/shard_map/spread_packed/pallas_call | solution.py:145
  119.2 0.7 pad_maximum_fusion.embed_ref
  119.9 6.7 %wave_layer.1 = (bf16[128,128]{1,0:T(8,128)(2,1)}, bf16[128,32]{1,0:T(8,128)(2,1)}, f32[12,128,128]{2,1,0:T(8,128)}, f32[2,128,2048]{2,1,0:T(8,128)}) custom-call(f32[128,128]{1,0:T(8,128)} %pad_maximum_fusion.embed_ref, f32[128,128]{1,0:T(8,128)} %get-tuple-element.61.wq_ref, f32[128,128]{1,0:T(8,128)} %get-tuple-element.62.wk_ref, ...), custom_call_target="tpu_custom_call" | custom-call | tf_op jit(solution)/shard_map/wave_layer/pallas_call | solution.py:294
  126.6 0.8 broadcast_select_fusion.1.up_ref
  127.4 1.2 copy-done.1
  128.6 99.1 %share_kernels.1 = (bf16[4,2,96,8192]{3,2,1,0:T(8,128)(2,1)}, bf16[208,8192]{1,0:T(8,128)(2,1)}, f32[196,768]{1,0:T(8,128)}) custom-call(bf16[128,128]{1,0:T(8,128)(2,1)} %get-tuple-element.68.shaped_ref, f32[1,8192]{1,0:T(1,128)} %bitcast.14, bf16[32,24576]{1,0:T(8,128)(2,1)} %get-tuple-element.70.own_slab, ...), custom_call_target="tpu_custom_call" | custom-call | tf_op jit(solution)/shard_map/share_kernels/pallas_call | solution.py:1250
  227.7 31.4 %block_pass.1 = (bf16[196,768]{1,0:T(8,128)(2,1)}, bf16[208,768]{1,0:T(8,128)(2,1)}, f32[8,768]{1,0:T(8,128)}, bf16[768,2304]{1,0:T(8,128)(2,1)}, bf16[768,768]{...) custom-call(f32[196,768]{1,0:T(8,128)} %get-tuple-element.74.stream_ref, ...), custom_call_target="tpu_custom_call" | custom-call | flops 8400000000 | bytes 30000000 | tf_op jit(solution)/shard_map/block_pass/pallas_call | solution.py:521
  259.1 87.5 %fold_kernels.1 = (bf16[2,2,96,8192]{3,2,1,0:T(8,128)(2,1)}, bf16[1,196,8192]{2,1,0:T(8,128)(2,1)}, bf16[196,768]{1,0:T(8,128)(2,1)}) custom-call(bf16[208,8192]{1,0:T(8,128)(2,1)} %get-tuple-element.73.masked_ref, f32[1,8192]{1,0:T(1,128)} %bitcast.15, bf16[208,768]{1,0:T(8,128)(2,1)} %get-tuple-element.81.low_ref, bf16[768,8192]{1,0:T(8,128)(2,1)} %bitcast.12, ...), custom_call_target="tpu_custom_call" | custom-call | tf_op jit(solution)/shard_map/fold_kernels/pallas_call | solution.py:1464
  346.5 2.6 collective-permute-start.2
  349.1 13.3 %master_update.1 = (f32[32,24576]{1,0:T(8,128)}, f32[32,24576]{1,0:T(8,128)}, f32[32,24576]{1,0:T(8,128)}, f32[128,32]{1,0:T(8,128)}) custom-call(bf16[4,96,8192]{2,1,0:T(8,128)(2,1)} %bitcast.13, bf16[128,32]{1,0:T(8,128)(2,1)} %get-tuple-element.93.shaped_ref, f32[32,24576]{1,0:T(8,128)} %weight_ref.3, f32[32,24576]{1,0:T(8,128)} %one_ref.1, ...), custom_call_target="tpu_custom_call" | custom-call | tf_op jit(solution)/shard_map/master_update/pallas_call | solution.py:710
  362.4 7.3 %wave_back.1 = (f32[128,128]{1,0:T(8,128)}, f32[128,128]{1,0:T(8,128)}, f32[128,128]{1,0:T(8,128)}, f32[128,128]{1,0:T(8,128)}, f32[128,2048]{1,0:T(8,128)}, /*index=5*/f32[2048,128]{1,0:T(8,128)}, f32[8,128]{1,0:T(8,128)}) custom-call(f32[128,32]{1,0:T(8,128)} %get-tuple-element.94.part_ref, f32[128,128]{1,0:T(8,128)} %pad_maximum_fusion.embed_ref, ...), custom_call_target="tpu_custom_call" | custom-call | tf_op jit(solution)/shard_map/wave_back/pallas_call | solution.py:348
  369.7 25.8 %collect_packed.1 = bf16[32,1920,128]{2,1,0:T(8,128)(2,1)} custom-call(s32[7680]{0:T(1024)} %reshape.52.order_ref, bf16[768,2304]{1,0:T(8,128)(2,1)} %get-tuple-element.88.refs_0_, bf16[768,768]{1,0:T(8,128)(2,1)} %get-tuple-element.89.refs_1_, bf16[768,3072]{1,0:T(8,128)(2,1)} %get-tuple-element.90.refs_2_, bf16[3072,768]{1,0:T(8,128)(2,1)} %get-tuple-element.91.refs_3_, ...), custom_call_target="tpu_custom_call" | custom-call | tf_op jit(solution)/shard_map/collect_packed/pallas_call | solution.py:213
  395.5 89.9 %reduce_packed.1 = f32[1920,128]{1,0:T(8,128)} custom-call(bf16[2,2,4,2,1920,128]{5,4,3,2,1,0:T(8,128)(2,1)} %bitcast.10), custom_call_target="tpu_custom_call" | custom-call | tf_op jit(solution)/shard_map/reduce_packed/pallas_call | solution.py:981
  485.4 0.8 broadcast_select_fusion
  486.2 3.7 multiply_subtract_fusion
  489.9 1.7 copy.21
  (32 shorter events, 1.3 us)
Async XLA Ops:
  3.5 85.7 %copy-start.9 = (s32[4,32]{1,0:T(4,128)S(1)}, s32[4,32]{1,0:T(4,128)}, u32[]{:S(2)}) copy-start(s32[4,32]{1,0:T(4,128)} %param.13) | copy-start | bytes 1540
  3.5 85.8 %copy-start.8 = (s32[7520]{0:T(1024)S(1)}, s32[7520]{0:T(1024)}, u32[]{:S(2)}) copy-start(s32[7520]{0:T(1024)} %param.14) | copy-start | bytes 90244
  3.5 86.6 %copy-start.10 = (s32[1,32]{1,0:T(1,128)S(1)}, s32[1,32]{1,0:T(1,128)}, u32[]{:S(2)}) copy-start(s32[1,32]{1,0:T(1,128)} %param.12) | copy-start | bytes 388
  87.3 40.1 %collective-permute-start.1 = (bf16[1,100,8192]{2,1,0:T(8,128)(2,1)S(1)}, bf16[1,100,8192]{2,1,0:T(8,128)(2,1)S(1)}, u32[]{:S(2)}, u32[]{:S(2)}) collective-permute-start(bf16[1,100,8192]{2,1,0:T(8,128)(2,1)S(1)} %slice.9), channel_id=1, source_target_pairs={{0,0},{1,1},{2,2},{3,3},{4,8},{5,9},{6,10},{7,11},{8,4},{9,5},{10,... | collective-permute-start | bytes 4915208 | tf_op jit(solution)/shard_map/ppermute | solution.py:1034
  88.1 39.3 %collective-permute-start = (bf16[32,24576]{1,0:T(8,128)(2,1)}, bf16[32,24576]{1,0:T(8,128)(2,1)}, u32[]{:S(2)}, u32[]{:S(2)}) collective-permute-start(bf16[32,24576]{1,0:T(8,128)(2,1)} %get-tuple-element.70.own_slab), channel_id=1, source_target_pairs={{0,16},{8,24},{16,0},{24,8},{1,17},{9,25},{17,1},{25,9},{2,18},{10... | collective-permute-start | bytes 4718600 | tf_op jit(solution)/shard_map/ppermute | solution.py:1023
  91.5 35.1 %copy-start.3 = (bf16[196,768]{1,0:T(8,128)(2,1)S(1)}, bf16[196,768]{1,0:T(8,128)(2,1)}, u32[]{:S(2)}) copy-start(bf16[196,768]{1,0:T(8,128)(2,1)} %up_ref.1) | copy-start | bytes 903172
  91.5 35.1 %copy-start.6 = (bf16[196,768]{1,0:T(8,128)(2,1)S(1)}, bf16[196,768]{1,0:T(8,128)(2,1)}, u32[]{:S(2)}) copy-start(bf16[196,768]{1,0:T(8,128)(2,1)} %get-tuple-element.75) | copy-start | bytes 903172
  127.4 1.2 copy-start.1
  346.5 143.3 %collective-permute-start.2 = (bf16[1,196,8192]{2,1,0:T(8,128)(2,1)}, bf16[1,196,8192]{2,1,0:T(8,128)(2,1)S(1)}, u32[]{:S(2)}, u32[]{:S(2)}) collective-permute-start(bf16[1,196,8192]{2,1,0:T(8,128)(2,1)} %get-tuple-element.87), channel_id=1, source_target_pairs={{0,0},{1,1},{2,2},{3,3},{4,8},{5,9},{6,10},{7,11},{8,4},{9,5},{10,... | collective-permute-start | bytes 9633800 | tf_op jit(solution)/shard_map/ppermute | solution.py:1034
  395.5 89.9 %copy-start.2 = (bf16[196,768]{1,0:T(8,128)(2,1)S(1)}, bf16[196,768]{1,0:T(8,128)(2,1)}, u32[]{:S(2)}) copy-start(bf16[196,768]{1,0:T(8,128)(2,1)} %get-tuple-element.83.out_ref) | copy-start | bytes 903172
  395.5 89.9 %copy-start.7 = (bf16[196,768]{1,0:T(8,128)(2,1)S(1)}, bf16[196,768]{1,0:T(8,128)(2,1)}, u32[]{:S(2)}) copy-start(bf16[196,768]{1,0:T(8,128)(2,1)} %get-tuple-element.84) | copy-start | bytes 903172
  395.5 90.7 %copy-start = (f32[1880,128]{1,0:T(8,128)S(1)}, f32[1880,128]{1,0:T(8,128)}, u32[]{:S(2)}) copy-start(f32[1880,128]{1,0:T(8,128)} %rest_ref.1) | copy-start | bytes 2887684
  395.5 90.7 %copy-start.4 = (f32[1880,128]{1,0:T(8,128)S(1)}, f32[1880,128]{1,0:T(8,128)}, u32[]{:S(2)}) copy-start(f32[1880,128]{1,0:T(8,128)} %param.16) | copy-start | bytes 2887684
  395.5 90.7 %copy-start.5 = (f32[1880,128]{1,0:T(8,128)S(1)}, f32[1880,128]{1,0:T(8,128)}, u32[]{:S(2)}) copy-start(f32[1880,128]{1,0:T(8,128)} %param.17) | copy-start | bytes 2887684

commit v6 on v5

--- a/solution.py
+++ b/solution.py
@@ -86,6 +86,10 @@
     return [jax.ShapeDtypeStruct((8, D), jnp.float32), jax.ShapeDtypeStruct((8, E), jnp.float32)]
 
 
+def steps_together(count):
+    return max(j for j in range(1, min(count, 60) + 1) if count % j == 0)
+
+
 def shards_a_step(shards, wanted):
     return wanted if shards % wanted == 0 else 1
 
@@ -105,7 +109,7 @@
                 linear[pl.ds(pl.multiple_of(block * 8, 8), 8), :] = pair[half * 8 : half * 8 + 8]
             return carry
 
-        lax.fori_loop(0, rows // 16, two, 0, unroll=8)
+        lax.fori_loop(0, rows // 16, two, 0, unroll=steps_together(rows // 16))
 
     @pl.when(step == pl.num_programs(0) - 1)
     def _():
@@ -204,7 +208,7 @@
             low_ref[shard, pl.ds(pl.multiple_of(j * 16, 16), 16), :] = jnp.concatenate(parts, axis=0).astype(low_ref.dtype)
             return carry
 
-        lax.fori_loop(0, rows // 16, two, 0, unroll=20)
+        lax.fori_loop(0, rows // 16, two, 0, unroll=steps_together(rows // 16))
 
 
 def collect_packed(grads, slots, blocks, shards, rows):
@@ -563,6 +567,7 @@
 
 
 NC = 15
+SPAN = 128
 HEAD = 96
 
 
@@ -761,10 +766,10 @@
     (x2, y2), (x3, y3), around, second, third, twin = partners()
     partner = place(y, 1 - c, (z + 2) % 4, x)
     moved = (c + z // 2) % 2 == 1
-    rows = own_ref.shape[0] // NC
+    rows = own_ref.shape[0]
 
     def cut(k):
-        return pl.ds(k * rows, rows)
+        return pl.ds(k * SPAN, min(SPAN, rows - k * SPAN))
 
     head = remote(pixel_ref.at[0, pl.ds(0, HEAD)], head_ref.at[0], head_sem.at[0], head_sem.at[1], partner)
     small = [
@@ -898,10 +903,10 @@
     f32, bf16 = jnp.float32, jnp.bfloat16
     y, c, z, x = spot()
     (x2, y2), (x3, y3), around, second, third, twin = partners()
-    rows = sum_ref.shape[0] // NC
+    rows = sum_ref.shape[0]
 
     def cut(k):
-        return pl.ds(k * rows, rows)
+        return pl.ds(k * SPAN, min(SPAN, rows - k * SPAN))
 
     spots = ((1 - y, 1 - x), (y3, x3), (y2, x2), (y, x))
     turned = ((1 - y, 1 - x), (y2, x2), (y3, x3), (y, x))
@@ -1512,7 +1517,7 @@
     own_rows = rest_weight.shape[0]
     own_blocks = own_rows // 8
     fits = lax.axis_size("group") == 4 and lax.axis_size("img") == 8
-    extra = -own_rows % 128
+    extra = -own_rows % 16
     slot_blocks = (own_rows + extra) // 8
     mask = band_mask.astype(f32)
     if fits:

time: 500 us -> 496 us (level)
  Pallas kernels: 472 us -> 466 us
  transfers between devices with their start and end apart: 3 -> 3, of which waited for: 0 -> 0; matrix products, arithmetic and copies ran while one was open for 2% -> 2% of each run, Pallas kernels for 35% -> 34%
where the time goes in v6:
time: 496 us; the launch traced here: 487 us
  Pallas kernels  466 us (94%)
  other arithmetic  7.58 us (2%)
  local copies, waits for them, and re-layouts  6.78 us (1%)
    pallas_call x1, Pallas kernels, share_kernels(): pl.pallas_call(share_kernel, out_shape=[jax.ShapeDtypeStruct((4, 2, dims,...  97.6 us
    pallas_call x1, Pallas kernels, reduce_packed(): pl.pallas_call(reduce_kernel, out_shape=jax.ShapeDtypeStruct((rows, 128),...  90.7 us
    pallas_call x1, Pallas kernels, fold_kernels(): pl.pallas_call(fold_kernel, out_shape=[jax.ShapeDtypeStruct((2, 2, dims,...  87.9 us
    pallas_call x1, Pallas kernels, gather_packed(): pl.pallas_call(gather_kernel, out_shape=[jax.ShapeDtypeStruct((2, 2, 4, 2...  82.4 us
    pallas_call x1, Pallas kernels, block_pass(): pl.pallas_call(block_kernel, out_shape=[jax.ShapeDtypeStruct((seq, D), bf...  31.4 us
    pallas_call x1, Pallas kernels, collect_packed(): pl.pallas_call(collect_kernel, out_shape=jax.ShapeDtypeStruct((shards, ro...  25 us
    pallas_call x1, Pallas kernels, spread_packed(): pl.pallas_call(spread_kernel, out_shape=big + small, grid_spec=pltpu.Pref...  24.1 us
    pallas_call x1, Pallas kernels, master_update(): pl.pallas_call(functools.partial(master_kernel, rate), out_shape=[like, l...  13.3 us
  transfers between devices with their start and end apart: 3, of which 0 were waited for; matrix products, arithmetic and copies ran while one was open for 2% of the time, Pallas kernels for 34%

profile of v6, /device:TPU:0, one launch (start us, length us, event | category | flops | bytes accessed | tf_op | source)
XLA Modules:
  0.0 486.5 jit_solution(15964467152954542480)
XLA Ops:
  0.6 0.7 convert_element_type.9
  1.3 1.6 slice.9
  3.5 82.4 %gather_packed.1 = (bf16[2,2,4,2,1888,128]{5,4,3,2,1,0:T(8,128)(2,1)}, bf16[1,96,8192]{2,1,0:T(8,128)(2,1)}, bf16[32,24576]{1,0:T(8,128)(2,1)}, bf16[196,768]{1,0:T(8,128)(2,1)}, f32[8,128]{1,0:T(8,128)}) custom-call(f32[1880,128]{1,0:T(8,128)} %rest_ref.1, bf16[1,196,8192]{2,1,0:T(8,128)(2,1)} %pixel_ref.3, f32[32,24576]{1,0:T(8,128)} %weight_ref.3, ...), custom_call_target="tpu_custom_call" | custom-call | tf_op jit(solution)/shard_map/gather_packed/pallas_call | solution.py:879
  85.9 0.8 collective-permute-start.1
  86.7 1.3 collective-permute-start
  88.2 0.7 reshape.52.order_ref
  89.0 0.7 fusion.1
  89.7 0.7 copy.19
  90.4 24.1 %spread_packed.1 = (bf16[768,2304]{1,0:T(8,128)(2,1)}, bf16[768,768]{1,0:T(8,128)(2,1)}, bf16[768,3072]{1,0:T(8,128)(2,1)}, bf16[3072,768]{1,0:T(8,128)(2,1)}, f...) custom-call(s32[7552]{0:T(1024)} %reshape.52.order_ref, ...), custom_call_target="tpu_custom_call" | custom-call | tf_op jit(solution)/shard_map/spread_packed/pallas_call | solution.py:149
  114.8 0.7 pad_maximum_fusion.embed_ref
  115.5 6.7 %wave_layer.1 = (bf16[128,128]{1,0:T(8,128)(2,1)}, bf16[128,32]{1,0:T(8,128)(2,1)}, f32[12,128,128]{2,1,0:T(8,128)}, f32[2,128,2048]{2,1,0:T(8,128)}) custom-call(f32[128,128]{1,0:T(8,128)} %pad_maximum_fusion.embed_ref, f32[128,128]{1,0:T(8,128)} %get-tuple-element.61.wq_ref, f32[128,128]{1,0:T(8,128)} %get-tuple-element.62.wk_ref, ...), custom_call_target="tpu_custom_call" | custom-call | tf_op jit(solution)/shard_map/wave_layer/pallas_call | solution.py:298
  122.3 0.8 broadcast_select_fusion.1.up_ref
  123.1 1.2 copy-done.1
  124.2 97.6 %share_kernels.1 = (bf16[4,2,96,8192]{3,2,1,0:T(8,128)(2,1)}, bf16[208,8192]{1,0:T(8,128)(2,1)}, f32[196,768]{1,0:T(8,128)}) custom-call(bf16[128,128]{1,0:T(8,128)(2,1)} %get-tuple-element.68.shaped_ref, f32[1,8192]{1,0:T(1,128)} %bitcast.14, bf16[32,24576]{1,0:T(8,128)(2,1)} %get-tuple-element.70.own_slab, ...), custom_call_target="tpu_custom_call" | custom-call | tf_op jit(solution)/shard_map/share_kernels/pallas_call | solution.py:1255
  221.9 31.4 %block_pass.1 = (bf16[196,768]{1,0:T(8,128)(2,1)}, bf16[208,768]{1,0:T(8,128)(2,1)}, f32[8,768]{1,0:T(8,128)}, bf16[768,2304]{1,0:T(8,128)(2,1)}, bf16[768,768]{...) custom-call(f32[196,768]{1,0:T(8,128)} %get-tuple-element.74.stream_ref, ...), custom_call_target="tpu_custom_call" | custom-call | flops 8400000000 | bytes 30000000 | tf_op jit(solution)/shard_map/block_pass/pallas_call | solution.py:525
  253.3 87.9 %fold_kernels.1 = (bf16[2,2,96,8192]{3,2,1,0:T(8,128)(2,1)}, bf16[1,196,8192]{2,1,0:T(8,128)(2,1)}, bf16[196,768]{1,0:T(8,128)(2,1)}) custom-call(bf16[208,8192]{1,0:T(8,128)(2,1)} %get-tuple-element.73.masked_ref, f32[1,8192]{1,0:T(1,128)} %bitcast.15, bf16[208,768]{1,0:T(8,128)(2,1)} %get-tuple-element.81.low_ref, bf16[768,8192]{1,0:T(8,128)(2,1)} %bitcast.12, ...), custom_call_target="tpu_custom_call" | custom-call | tf_op jit(solution)/shard_map/fold_kernels/pallas_call | solution.py:1469
  341.2 2.6 collective-permute-start.2
  343.8 13.3 %master_update.1 = (f32[32,24576]{1,0:T(8,128)}, f32[32,24576]{1,0:T(8,128)}, f32[32,24576]{1,0:T(8,128)}, f32[128,32]{1,0:T(8,128)}) custom-call(bf16[4,96,8192]{2,1,0:T(8,128)(2,1)} %bitcast.13, bf16[128,32]{1,0:T(8,128)(2,1)} %get-tuple-element.93.shaped_ref, f32[32,24576]{1,0:T(8,128)} %weight_ref.3, f32[32,24576]{1,0:T(8,128)} %one_ref.1, ...), custom_call_target="tpu_custom_call" | custom-call | tf_op jit(solution)/shard_map/master_update/pallas_call | solution.py:715
  357.1 7.3 %wave_back.1 = (f32[128,128]{1,0:T(8,128)}, f32[128,128]{1,0:T(8,128)}, f32[128,128]{1,0:T(8,128)}, f32[128,128]{1,0:T(8,128)}, f32[128,2048]{1,0:T(8,128)}, /*index=5*/f32[2048,128]{1,0:T(8,128)}, f32[8,128]{1,0:T(8,128)}) custom-call(f32[128,32]{1,0:T(8,128)} %get-tuple-element.94.part_ref, f32[128,128]{1,0:T(8,128)} %pad_maximum_fusion.embed_ref, ...), custom_call_target="tpu_custom_call" | custom-call | tf_op jit(solution)/shard_map/wave_back/pallas_call | solution.py:352
  364.3 25.0 %collect_packed.1 = bf16[32,1888,128]{2,1,0:T(8,128)(2,1)} custom-call(s32[7552]{0:T(1024)} %reshape.52.order_ref, bf16[768,2304]{1,0:T(8,128)(2,1)} %get-tuple-element.88.refs_0_, bf16[768,768]{1,0:T(8,128)(2,1)} %get-tuple-element.89.refs_1_, bf16[768,3072]{1,0:T(8,128)(2,1)} %get-tuple-element.90.refs_2_, bf16[3072,768]{1,0:T(8,128)(2,1)} %get-tuple-element.91.refs_3_, ...), custom_call_target="tpu_custom_call" | custom-call | tf_op jit(solution)/shard_map/collect_packed/pallas_call | solution.py:217
  389.5 90.7 %reduce_packed.1 = f32[1888,128]{1,0:T(8,128)} custom-call(bf16[2,2,4,2,1888,128]{5,4,3,2,1,0:T(8,128)(2,1)} %bitcast.10), custom_call_target="tpu_custom_call" | custom-call | tf_op jit(solution)/shard_map/reduce_packed/pallas_call | solution.py:986
  480.1 0.8 broadcast_select_fusion
  480.9 3.7 multiply_subtract_fusion
  484.6 1.7 copy.21
  (32 shorter events, 1.3 us)
Async XLA Ops:
  3.5 84.5 %copy-start.9 = (s32[4,32]{1,0:T(4,128)S(1)}, s32[4,32]{1,0:T(4,128)}, u32[]{:S(2)}) copy-start(s32[4,32]{1,0:T(4,128)} %param.13) | copy-start | bytes 1540
  3.5 84.6 %copy-start.8 = (s32[7520]{0:T(1024)S(1)}, s32[7520]{0:T(1024)}, u32[]{:S(2)}) copy-start(s32[7520]{0:T(1024)} %param.14) | copy-start | bytes 90244
  3.5 85.5 %copy-start.10 = (s32[1,32]{1,0:T(1,128)S(1)}, s32[1,32]{1,0:T(1,128)}, u32[]{:S(2)}) copy-start(s32[1,32]{1,0:T(1,128)} %param.12) | copy-start | bytes 388
  85.9 37.2 %collective-permute-start.1 = (bf16[1,100,8192]{2,1,0:T(8,128)(2,1)S(1)}, bf16[1,100,8192]{2,1,0:T(8,128)(2,1)S(1)}, u32[]{:S(2)}, u32[]{:S(2)}) collective-permute-start(bf16[1,100,8192]{2,1,0:T(8,128)(2,1)S(1)} %slice.9), channel_id=1, source_target_pairs={{0,0},{1,1},{2,2},{3,3},{4,8},{5,9},{6,10},{7,11},{8,4},{9,5},{10,... | collective-permute-start | bytes 4915208 | tf_op jit(solution)/shard_map/ppermute | solution.py:1039
  86.7 36.4 %collective-permute-start = (bf16[32,24576]{1,0:T(8,128)(2,1)}, bf16[32,24576]{1,0:T(8,128)(2,1)}, u32[]{:S(2)}, u32[]{:S(2)}) collective-permute-start(bf16[32,24576]{1,0:T(8,128)(2,1)} %get-tuple-element.70.own_slab), channel_id=1, source_target_pairs={{0,16},{8,24},{16,0},{24,8},{1,17},{9,25},{17,1},{25,9},{2,18},{10... | collective-permute-start | bytes 4718600 | tf_op jit(solution)/shard_map/ppermute | solution.py:1028
  90.4 31.9 %copy-start.3 = (bf16[196,768]{1,0:T(8,128)(2,1)S(1)}, bf16[196,768]{1,0:T(8,128)(2,1)}, u32[]{:S(2)}) copy-start(bf16[196,768]{1,0:T(8,128)(2,1)} %up_ref.1) | copy-start | bytes 903172
  90.4 31.9 %copy-start.6 = (bf16[196,768]{1,0:T(8,128)(2,1)S(1)}, bf16[196,768]{1,0:T(8,128)(2,1)}, u32[]{:S(2)}) copy-start(bf16[196,768]{1,0:T(8,128)(2,1)} %get-tuple-element.75) | copy-start | bytes 903172
  123.1 1.2 copy-start.1
  341.2 143.4 %collective-permute-start.2 = (bf16[1,196,8192]{2,1,0:T(8,128)(2,1)}, bf16[1,196,8192]{2,1,0:T(8,128)(2,1)S(1)}, u32[]{:S(2)}, u32[]{:S(2)}) collective-permute-start(bf16[1,196,8192]{2,1,0:T(8,128)(2,1)} %get-tuple-element.87), channel_id=1, source_target_pairs={{0,0},{1,1},{2,2},{3,3},{4,8},{5,9},{6,10},{7,11},{8,4},{9,5},{10,... | collective-permute-start | bytes 9633800 | tf_op jit(solution)/shard_map/ppermute | solution.py:1039
  389.4 90.7 %copy-start.2 = (bf16[196,768]{1,0:T(8,128)(2,1)S(1)}, bf16[196,768]{1,0:T(8,128)(2,1)}, u32[]{:S(2)}) copy-start(bf16[196,768]{1,0:T(8,128)(2,1)} %get-tuple-element.83.out_ref) | copy-start | bytes 903172
  389.4 90.7 %copy-start.7 = (bf16[196,768]{1,0:T(8,128)(2,1)S(1)}, bf16[196,768]{1,0:T(8,128)(2,1)}, u32[]{:S(2)}) copy-start(bf16[196,768]{1,0:T(8,128)(2,1)} %get-tuple-element.84) | copy-start | bytes 903172
  389.4 91.5 %copy-start = (f32[1880,128]{1,0:T(8,128)S(1)}, f32[1880,128]{1,0:T(8,128)}, u32[]{:S(2)}) copy-start(f32[1880,128]{1,0:T(8,128)} %rest_ref.1) | copy-start | bytes 2887684
  389.4 91.5 %copy-start.4 = (f32[1880,128]{1,0:T(8,128)S(1)}, f32[1880,128]{1,0:T(8,128)}, u32[]{:S(2)}) copy-start(f32[1880,128]{1,0:T(8,128)} %param.16) | copy-start | bytes 2887684
  389.4 91.5 %copy-start.5 = (f32[1880,128]{1,0:T(8,128)S(1)}, f32[1880,128]{1,0:T(8,128)}, u32[]{:S(2)}) copy-start(f32[1880,128]{1,0:T(8,128)} %param.17) | copy-start | bytes 2887684
